TPU v7x, 32 devices: a whole 2x2x4 slice. The times are simulated.
32 devices in a mesh: seq: 32 (over z, y, x, core).
Axes of the slice: x: 2, y: 2, z: 4, core: 2. Of those that a mesh axis runs over, the one named last changes fastest.
Arguments:
- tokens: bfloat16 [2, 16384, 1024], P(None, 'seq'), may hold values from -6 to 6
- seq_starts: int32 [2, 16384], P(None, 'seq'), may hold values from 0 to 15360, as said below
- seq_lengths: int32 [2, 16384], P(None, 'seq'), may hold values from 1 to 16384, as said below
- gain_in: float32 [1024], replicated, may hold values from 0.25 to 1.75
- gain_mlp: float32 [1024], replicated, may hold values from 0.25 to 1.75
- w_in: bfloat16 [1024, 3584], replicated, may hold values from -0.1875 to 0.1875
- w_out: bfloat16 [1024, 1024], replicated, may hold values from -0.1875 to 0.1875
- w_gate_up: bfloat16 [1024, 5632], replicated, may hold values from -0.1875 to 0.1875
- w_down: bfloat16 [2816, 1024], replicated, may hold values from -0.109375 to 0.109375
- cotangent: bfloat16 [2, 16384, 1024], P(None, 'seq'), may hold values from -6 to 6
Outputs:
- mixed_out: bfloat16 [2, 16384, 1024], P(None, 'seq')
- grad_tokens: float32 [2, 16384, 1024], P(None, 'seq')
- grad_gain_in: float32 [1024], P('seq')
- grad_gain_mlp: float32 [1024], P('seq')
- grad_w_in: float32 [1024, 3584], P('seq')
- grad_w_out: float32 [1024, 1024], P('seq')
- grad_w_gate_up: float32 [1024, 5632], P('seq')
- grad_w_down: float32 [2816, 1024], P('seq')
Inputs may be any that keep to these rules, and one draw needn't show every extreme that they name: `seq_starts`: tokens of one sequence occupy a run of positions beginning at this value, which never falls along a row and is a multiple of 64. Row 0 holds a single sequence filling the whole row. Every other row holds sequences of 1024 to 8192 tokens, each followed by padding up to a multiple of 64 positions, and ends with a sequence of exactly 1024 tokens that starts at 15360; the sequence before that one may be cut short. `seq_lengths`: the same for all tokens of a sequence; positions from start + length up to the next sequence's start are padding, fewer than 64 of them.
All inputs are finite; a program needn't handle non-finite values.
Results may differ from a plain program's by a relative error of at most 0.017.
Values may be sent and summed in bfloat16 or wider, within the bound.
A program may use at most 896 MiB of HBM per device.

v0:
```python
import functools
import jax
import jax.numpy as jnp
from jax import lax
from jax.experimental import pallas as pl
from jax.experimental.pallas import tpu as pltpu
from jax.sharding import PartitionSpec as P
F32=jnp.float32; BF=jnp.bfloat16
EPSILON=1e-6
MIB=1<<20

def nn(a,b): return lax.dot_general(a,b,(((1,),(0,)),((),())),preferred_element_type=F32)
def nt(a,b): return lax.dot_general(a,b,(((1,),(1,)),((),())),preferred_element_type=F32)
def tn(a,b): return lax.dot_general(a,b,(((0,),(0,)),((),())),preferred_element_type=F32)

def parted(x, first, each):
    x = x.reshape(x.shape[0] // (2 * each), 2, each, x.shape[1])
    a, b = x[:, 0].reshape(-1, x.shape[3]), x[:, 1].reshape(-1, x.shape[3])
    return jnp.where(first, a, b).astype(BF), jnp.where(first, b, a).astype(BF)

def mlp_kernel(core_ref, mixed, tokens, cot, w_out, gain, wg, wu, wd,
               result, grad_resid, grad_mixed, keep_g, send_g, keep_u, send_u, keep_d, send_d, keep_o, send_o,
               resid, acc, dh, hn, hn_t, hid, dgu, wgu, *, steps, chunk, each):
    step = pl.program_id(0)
    toks = mixed.shape[0]
    width = mixed.shape[1]
    count = toks // chunk
    first = core_ref[0] == 0

    def rows(n):
        return pl.ds(pl.multiple_of(n * chunk, chunk), chunk)

    @pl.when(step == 0)
    def _():
        def one(n, carry):
            r = rows(n)
            res = tokens[r, :].astype(F32) + nn(mixed[r, :], w_out[...])
            scale = lax.rsqrt(jnp.mean(res * res, axis=-1, keepdims=True) + EPSILON)
            h = (res * scale * gain[...]).astype(BF)
            resid[r, :] = res
            acc[r, :] = res
            dh[r, :] = jnp.zeros((chunk, width), F32)
            hn[r, :] = h
            return carry
        lax.fori_loop(0, count, one, 0)
        for n in range(count):
            hn_t[:, n * chunk:(n + 1) * chunk] = hn[n * chunk:(n + 1) * chunk, :].T

    tile = wg.shape[1]
    wgu[:, :tile] = wg[...]
    wgu[:, tile:] = wu[...]

    def forward(n, carry):
        r = rows(n)
        h = hn[r, :]
        both = nn(h, wgu[...])
        gate, up = both[:, :tile], both[:, tile:]
        dhid = nt(cot[r, :], wd[...])
        sig = 1.0 / (1.0 + jnp.exp(-gate))
        silu = gate * sig
        hidden = (silu * up).astype(BF)
        d_gate = (dhid * up * (sig + silu * (1.0 - sig))).astype(BF)
        d_up = (dhid * silu).astype(BF)
        hid[r, :] = hidden
        dgu[r, :tile] = d_gate
        dgu[r, tile:] = d_up
        acc[r, :] += nn(hidden, wd[...])
        dh[r, :] += nt(dgu[r, :], wgu[...])
        return carry
    lax.fori_loop(0, count, forward, 0, unroll=2)

    half = width // 2
    grad_d = tn(hid[...], cot[...])
    left, right = grad_d[:, :half].astype(BF), grad_d[:, half:].astype(BF)
    keep_d[...] = jnp.where(first, left, right)
    send_d[...] = jnp.where(first, right, left)

    def weights(n, carry):
        r = rows(n)
        o = pl.ds(pl.multiple_of(n * (chunk // 2), chunk // 2), chunk // 2)
        grad = nn(hn_t[r, :], dgu[...])
        keep_g[o, :], send_g[o, :] = parted(grad[:, :tile], first, each)
        keep_u[o, :], send_u[o, :] = parted(grad[:, tile:], first, each)
        return carry
    lax.fori_loop(0, width // chunk, weights, 0, unroll=2)

    @pl.when(step == steps - 1)
    def _():
        def one(n, carry):
            r = rows(n)
            res = resid[r, :]
            scale = lax.rsqrt(jnp.mean(res * res, axis=-1, keepdims=True) + EPSILON)
            grad = dh[r, :]
            c = grad * gain[...]
            back = cot[r, :].astype(F32) + scale * c - res * (scale * scale * scale * jnp.mean(c * res, axis=-1, keepdims=True))
            result[r, :] = acc[r, :].astype(BF)
            grad_resid[r, :] = back
            b = back.astype(BF)
            hn[r, :] = b
            grad_mixed[r, :] = nt(b, w_out[...]).astype(BF)
            return carry
        lax.fori_loop(0, count, one, 0)
        for n in range(count):
            hn_t[:, n * chunk:(n + 1) * chunk] = mixed[n * chunk:(n + 1) * chunk, :].T
        def outer(n, carry):
            r = rows(n)
            o = pl.ds(pl.multiple_of(n * (chunk // 2), chunk // 2), chunk // 2)
            keep_o[o, :], send_o[o, :] = parted(nn(hn_t[r, :], hn[...]), first, each)
            return carry
        lax.fori_loop(0, width // chunk, outer, 0)


HEADS=16; FEAT=16; WINDOW=64; ROWS_PHI=160; FLAG_ROW=153
VMEM = 64 * MIB
GROUPS = HEADS // 4
EACH = 2
STEPS = GROUPS // EACH

def groups():
    return [(pl.program_id(1) * EACH + s, slice(s * 256, (s + 1) * 256)) for s in range(EACH)]

COST = dict(project_keys=6.8, state=7.4, project_rest=10, begun=2, joined=2.5, ended=3, intra=7.2, window=8.5, mix=10, mlp=88, numer_back=12,
    window_back=13, intra_back=14, sum_first=10.6, sum_second=6.4, state_back=0.1, weight_grad_early=0.1, weight_grad_late=0.1, input_grad_first=0.1, input_grad=0.1, in_first=3, in_second=3, quarters=3.5, tail=1.8, gathered=2.3, plain=2.0, sum_more=3)

class Order:
    last = None

def call(kernel, name, grid, ins, outs, scratch=(), flops=0, moved=10 * MIB, deps=(), into=None, alias=None, scalars=(), through=()):
    arrays, specs = [a for a, _ in ins], [s for _, s in ins]
    count, ahead = len(arrays), len(scalars)
    into = list(into or ())
    deps = list(deps)
    if Order.last is not None and not any(Order.last is a for a in into + deps + arrays):
        deps.append(Order.last)
    extra = deps + into + list(through)
    aliases = {ahead + count + len(deps) + n: n for n in range(len(into))}
    aliases.update({ahead + i: o for i, o in (alias or {}).items()})
    aliases.update({ahead + count + len(deps) + len(into) + n: len(outs) + n for n in range(len(through))})
    results = len(outs)
    outs = list(outs) + [(a.shape, a.dtype, pl.BlockSpec(memory_space=pl.ANY)) for a in through]
    def body(*refs):
        begin = ahead + count + len(extra)
        kernel(*refs[:ahead + count], *refs[begin:begin + results], *refs[begin + len(outs):])
    out = pl.pallas_call(
        body, grid_spec=pltpu.PrefetchScalarGridSpec(num_scalar_prefetch=ahead, grid=grid,
            in_specs=specs + [pl.BlockSpec(memory_space=pl.ANY)] * len(extra), out_specs=[s for _, _, s in outs], scratch_shapes=list(scratch)),
        out_shape=[jax.ShapeDtypeStruct(shape, dtype) for shape, dtype, _ in outs],
        input_output_aliases=aliases, name=name,
        compiler_params=pltpu.CompilerParams(vmem_limit_bytes=VMEM, dimension_semantics=("arbitrary",) * len(grid)),
        cost_estimate=pl.CostEstimate(flops=int(COST.get(name, 2.0) * 1e9), bytes_accessed=1000, transcendentals=0),
    )(*scalars, *arrays, *extra)
    Order.last = out[0]
    return out

def lane_mask(width, size, which, dtype=BF):
    lanes = lax.broadcasted_iota(jnp.int32, (1, width), 1)
    return ((lanes >> (size.bit_length() - 1)) == which).astype(dtype)

def spread(values, length):
    block = lax.broadcasted_iota(jnp.int32, (1, length), 1) >> 6
    out = jnp.zeros((1, length), jnp.int32)
    for n, value in enumerate(values):
        out = jnp.where(block == n, value, out)
    return out

def scalars(ref, row, length):
    per_row = length // WINDOW
    return [ref[row * per_row + n] for n in range(per_row)]

def early_line(low, row, length):
    return (spread(scalars(low, row, length), length) < 0).astype(F32)

def owned_line(low, high, row, length):
    lows = scalars(low, row, length)
    place = lax.broadcasted_iota(jnp.int32, (1, length), 1)
    same = spread(lows, length) == lows[-1]
    return (same & (place < spread(scalars(high, row, length), length))).astype(F32)

TURNS = FEAT // 2

def turn(d):
    row = lax.broadcasted_iota(jnp.int32, (HEADS * FEAT, HEADS * FEAT), 0)
    entry = lax.broadcasted_iota(jnp.int32, (HEADS * FEAT, HEADS * FEAT), 1)
    return (((row & -FEAT) | ((row + d) & (FEAT - 1))) == entry).astype(BF)

def turned_scratch(length):
    return pltpu.VMEM((TURNS, HEADS * FEAT, length), BF)

def turn_all(x, x_t, turned, line):
    flipped = x.astype(F32).T
    flat = (flipped if line is None else flipped * line).astype(BF)
    x_t[...] = flat
    for d in range(1, TURNS + 1):
        turned[d - 1] = nn(turn(d), flat).astype(BF)

def features_t(x_t, turned, at, line):
    half = FEAT // 2
    x = x_t[at, :]
    parts = [x * x * jnp.bfloat16((2.0 * FEAT) ** -0.5)]
    xs = x * jnp.bfloat16(FEAT ** -0.5)
    for d in range(1, half):
        parts.append(xs * turned[d - 1, at, :])
    parts.append(x * jnp.bfloat16(FEAT ** -0.25))
    row = lax.broadcasted_iota(jnp.int32, x.shape, 0)
    parts.append(jnp.where(row < half, xs * turned[half - 1, at, :], jnp.where(row == half, line, 0.0).astype(BF)))
    return jnp.concatenate(parts, axis=0)

def features_back_t(x_t, turned, at, g, pulled):
    half = FEAT // 2
    x = x_t[at, :]
    total = g[:FEAT] * x.astype(F32) * (2.0 * (2.0 * FEAT) ** -0.5) + g[half * FEAT:(half + 1) * FEAT] * FEAT ** -0.25
    mixed = jnp.zeros(x.shape, F32)
    xs = x * jnp.bfloat16(FEAT ** -0.5)
    row = lax.broadcasted_iota(jnp.int32, x.shape, 0)
    gb = g.astype(BF)
    for d in range(1, half + 1):
        if d < half:
            gd = gb[d * FEAT:(d + 1) * FEAT]
        else:
            gd = jnp.where(row < half, gb[(half + 1) * FEAT:(half + 2) * FEAT], jnp.bfloat16(0))
        mixed = mixed + (gd * turned[d - 1, at, :]).astype(F32)
        pulled[d - 1, at, :] = gd * xs
    return total + mixed * FEAT ** -0.5

def turned_back(pulled):
    total = None
    for d in range(1, TURNS + 1):
        term = nn(turn(-d), pulled[d - 1])
        total = term if total is None else total + term
    return total

def head_rows(group, h):
    return pl.ds(pl.multiple_of(group * 4 * FEAT + h * FEAT, FEAT), FEAT)

def states_of(x_t, turned, y, group, line, flag):
    row = lax.broadcasted_iota(jnp.int32, (ROWS_PHI, 256), 0)
    out = jnp.where(row == FLAG_ROW, flag, 0.0)
    for h in range(4):
        out = out + nn(features_t(x_t, turned, head_rows(group, h), line), y * lane_mask(256, 64, h))
    return out

def put_state(g, state, core, mine, send):
    r = pl.program_id(0)
    @pl.when(r == core[0])
    def _():
        mine[g] = state
    @pl.when(r != core[0])
    def _():
        send[g] = state.astype(BF)

def state_outs():
    shape = (GROUPS, ROWS_PHI, 256)
    spec = pl.BlockSpec(shape, lambda r, g: (0, 0, 0))
    return [(shape, F32, spec), (shape, BF, spec)]

def state_kernel(core, low, high, k, v, mine, send, k_t, line, turned, *, length):
    r, g = pl.program_id(0), pl.program_id(1)
    @pl.when(g == 0)
    def _():
        line[...] = owned_line(low, high, r, length)
        turn_all(k[...], k_t, turned, line[...])
    flag = (low[(r + 1) * (length // WINDOW) - 1] >= 0).astype(F32)
    for g, at in groups():
        put_state(g, states_of(k_t, turned, v[:, at], g, line[...], flag), core, mine, send)

def spec_col(length, first=0, row=0):
    return pl.BlockSpec((length, 256 * EACH), lambda r, g: (r + row, first // EACH + g))
def spec_all(length, row=0):
    return pl.BlockSpec((length, 256), lambda r, g: (r + row, 0))
SPEC_STATE = pl.BlockSpec((EACH, ROWS_PHI, 256), lambda r, g: (g, 0, 0))
def spec_t(length, row=0):
    return pl.BlockSpec((1, 256, length), lambda r, g: (r + row, 0, 0))
SMEM = pl.BlockSpec(memory_space=pltpu.SMEM)
def local_states(core, low, high, k, v, rows, length):
    return call(functools.partial(state_kernel, length=length), "state", (rows, STEPS),
        [(core, SMEM), (low, SMEM), (high, SMEM), (k, spec_all(length)), (v, spec_col(length))], state_outs(),
        [pltpu.VMEM((256, length), BF), pltpu.VMEM((1, length), F32), turned_scratch(length)])

def intra_kernel(low, high, q, k, v, out, mask, *, length, row):
    g = pl.program_id(1)
    half = length // 2
    @pl.when(g == 0)
    def _():
        lows, highs = scalars(low, row, length), scalars(high, row, length)
        for n in range(length // WINDOW):
            i = lax.broadcasted_iota(jnp.int32, (WINDOW, length), 0) + n * WINDOW
            j = lax.broadcasted_iota(jnp.int32, (WINDOW, length), 1)
            mask[n * WINDOW:(n + 1) * WINDOW, :] = ((j >= lows[n]) & (j <= i) & (j < highs[n])).astype(BF)
    qv, kv = q[...] * jnp.bfloat16(FEAT ** -0.5), k[...]
    for g, at in groups():
        vv = v[:, at] * jnp.bfloat16(0.5)
        top = bottom = None
        for h in range(4):
            km = kv * lane_mask(HEADS * FEAT, FEAT, g * 4 + h)
            vm = vv * lane_mask(256, 64, h)
            u0 = 1.0 + nt(qv[:half], km[:half])
            a0 = (1.0 + u0 * u0).astype(BF) * mask[:half, :half]
            u1 = 1.0 + nt(qv[half:], km)
            a1 = (1.0 + u1 * u1).astype(BF) * mask[half:, :]
            o0, o1 = nn(a0, vm[:half]), nn(a1, vm)
            top = o0 if top is None else top + o0
            bottom = o1 if bottom is None else bottom + o1
        out[:half, at] = top.astype(BF)
        out[half:, at] = bottom.astype(BF)

def intra(low, high, p, rows, length, row, deps=(), into=None):
    return call(functools.partial(intra_kernel, length=length, row=row), "intra", (1, STEPS),
        [(low, SMEM), (high, SMEM), (p.q_lin, spec_all(length, row)), (p.k_lin, spec_all(length, row)), (p.v, spec_col(length, 0, row))],
        [((rows * length, 1024), BF, spec_col(length, 0, row))],
        [pltpu.VMEM((length, length), BF)], flops=HEADS * 2 * 6 * 256 ** 3, deps=deps, into=into)

def stacked(x, scale=1.0):
    return jnp.concatenate([x * (lane_mask(256, 64, h) * jnp.bfloat16(scale)) for h in range(4)], axis=0)

def unstacked(x, scale=1.0):
    total = None
    for h in range(4):
        part = x[h * WINDOW:(h + 1) * WINDOW] * (lane_mask(256, 64, h, F32) * scale)
        total = part if total is None else total + part
    return total

def window_probs(low, high, at, shift, keys, qs):
    s = nt(keys, qs)
    key = lax.broadcasted_iota(jnp.int32, (2 * WINDOW, 4 * WINDOW), 0)
    query = lax.broadcasted_iota(jnp.int32, (2 * WINDOW, 4 * WINDOW), 1) & (WINDOW - 1)
    ok = (key >= jnp.maximum(query, low[at] + shift)) & (key < jnp.minimum(query + (WINDOW + 1), high[at] + shift))
    s = jnp.where(ok, s, -1e30)
    p = jnp.exp(s - jnp.max(s, axis=0, keepdims=True))
    return p * (1.0 / jnp.sum(p, axis=0, keepdims=True))

def window_kernel(low, high, q, k, v, hk, hv, out, ka, va, *, length, row):
    per_row = length // WINDOW
    ka[:WINDOW, :] = hk[...]
    ka[WINDOW:, :] = k[...]
    va[:WINDOW, :] = hv[...]
    va[WINDOW:, :] = v[...]
    for g, at in groups():
        for n in range(per_row):
            own, both = slice(n * WINDOW, (n + 1) * WINDOW), slice(n * WINDOW, (n + 2) * WINDOW)
            p = window_probs(low, high, row * per_row + n, (1 - n) * WINDOW, ka[both, at], stacked(q[own, at], 64 ** -0.5))
            out[own, at] = unstacked(tn(p.astype(BF), va[both, at])).astype(BF)

def window_ins(low, high, p, halo, length, row):
    tail = lambda part: pl.BlockSpec((None, WINDOW, 256 * EACH), lambda r, g: (part, r + row, g))
    return [(low, SMEM), (high, SMEM), (p.qk_win, spec_col(length, 0, row)), (p.qk_win, spec_col(length, GROUPS, row)), (p.v, spec_col(length, 0, row)),
            (halo, tail(0)), (halo, tail(1))]

def window(low, high, p, halo, rows, length, row, deps=(), into=None):
    return call(functools.partial(window_kernel, length=length, row=row), "window", (1, STEPS),
        window_ins(low, high, p, halo, length, row),
        [((rows * length, 1024), BF, spec_col(length, 0, row))],
        [pltpu.VMEM((length + WINDOW, 256 * EACH), BF)] * 2, flops=HEADS * 2 * 4 * length * 128 * 256, deps=deps, into=into)

def window_back_block(low, high, row, n, per_row, q, keys, vals, go):
    qs, gs = stacked(q, 64 ** -0.5), stacked(go)
    p = window_probs(low, high, row * per_row + n, (1 - n) * WINDOW, keys, qs)
    gp = nt(vals, gs)
    ds = (p * (gp - jnp.sum(p * gp, axis=0, keepdims=True))).astype(BF)
    return unstacked(tn(ds, keys), 64 ** -0.5).astype(BF), nn(ds, qs), nn(p.astype(BF), gs)

def window_back_first_kernel(low, high, q, k, v, hk, hv, go, q1, k1, v1, hk1, hv1, go1, dq, dk, dv, dh, q_kept, k_kept, v_kept, ka, va, *, length):
    per_row = length // WINDOW
    ka[:WINDOW, :] = hk[...]
    ka[WINDOW:, :] = k[...]
    va[:WINDOW, :] = hv[...]
    va[WINDOW:, :] = v[...]
    for _, at in groups():
        carry_k = carry_v = None
        for n in range(per_row):
            rows = slice(n * WINDOW, (n + 1) * WINDOW)
            both = slice(n * WINDOW, (n + 2) * WINDOW)
            dq[rows, at], dk_n, dv_n = window_back_block(low, high, 0, n, per_row, q[rows, at], ka[both, at], va[both, at], go[rows, at])
            if n == 0:
                dh[0, :WINDOW, at] = dk_n[:WINDOW].astype(BF)
                dh[1, :WINDOW, at] = dv_n[:WINDOW].astype(BF)
            else:
                dk[(n - 1) * WINDOW:n * WINDOW, at] = (carry_k + dk_n[:WINDOW]).astype(BF)
                dv[(n - 1) * WINDOW:n * WINDOW, at] = (carry_v + dv_n[:WINDOW]).astype(BF)
            carry_k, carry_v = dk_n[WINDOW:], dv_n[WINDOW:]
        dk[length - WINDOW:, at] = carry_k.astype(BF)
        dv[length - WINDOW:, at] = carry_v.astype(BF)
        keys = jnp.concatenate([hk1[:, at], k1[:, at]], axis=0)
        vals = jnp.concatenate([hv1[:, at], v1[:, at]], axis=0)
        q_kept[:, at], dk_n, dv_n = window_back_block(low, high, 1, 0, per_row, q1[:, at], keys, vals, go1[:, at])
        dh[0, WINDOW:, at] = dk_n[:WINDOW].astype(BF)
        dh[1, WINDOW:, at] = dv_n[:WINDOW].astype(BF)
        k_kept[:, at] = dk_n[WINDOW:]
        v_kept[:, at] = dv_n[WINDOW:]

def window_back_second_kernel(low, high, q, k, v, go, q_kept, k_kept, v_kept, dq, dk, dv, *, length):
    per_row = length // WINDOW
    dq[:WINDOW, :] = q_kept[...]
    for _, at in groups():
        carry_k, carry_v = k_kept[:, at], v_kept[:, at]
        for n in range(1, per_row):
            rows = slice(n * WINDOW, (n + 1) * WINDOW)
            both = slice((n - 1) * WINDOW, (n + 1) * WINDOW)
            dq[rows, at], dk_n, dv_n = window_back_block(low, high, 1, n, per_row, q[rows, at], k[both, at], v[both, at], go[rows, at])
            dk[(n - 1) * WINDOW:n * WINDOW, at] = (carry_k + dk_n[:WINDOW]).astype(BF)
            dv[(n - 1) * WINDOW:n * WINDOW, at] = (carry_v + dv_n[:WINDOW]).astype(BF)
            carry_k, carry_v = dk_n[WINDOW:], dv_n[WINDOW:]
        dk[length - WINDOW:, at] = carry_k.astype(BF)
        dv[length - WINDOW:, at] = carry_v.astype(BF)

def window_back_outs(total, length, row):
    spec = spec_col(length, 0, row)
    return [((total, 1024), BF, spec)] * 3

def window_back_first(low, high, p, halo, go, rows, length):
    total, per_row = rows * length, length // WINDOW
    block = lambda first=0: pl.BlockSpec((WINDOW, 256 * EACH), lambda r, g: (per_row, first // EACH + g))
    tail = lambda part: pl.BlockSpec((None, WINDOW, 256 * EACH), lambda r, g: (part, 1, g))
    small = spec_col(WINDOW)
    got = call(functools.partial(window_back_first_kernel, length=length), "window_back", (1, STEPS),
        window_ins(low, high, p, halo, length, 0) + [(go, spec_col(length)), (p.qk_win, block()), (p.qk_win, block(GROUPS)), (p.v, block()), (halo, tail(0)), (halo, tail(1)), (go, block())],
        window_back_outs(total, length, 0) + [((2, rows * WINDOW, 1024), BF, pl.BlockSpec((2, rows * WINDOW, 256 * EACH), lambda r, g: (0, 0, g))),
         ((WINDOW, 1024), BF, small), ((WINDOW, 1024), F32, small), ((WINDOW, 1024), F32, small)],
        [pltpu.VMEM((length + WINDOW, 256 * EACH), BF)] * 2)
    return got[:3], got[3], got[4:]

def window_back_second(low, high, p, go, into, kept, rows, length):
    small = spec_col(WINDOW)
    return call(functools.partial(window_back_second_kernel, length=length), "window_back", (1, STEPS),
        [(low, SMEM), (high, SMEM), (p.qk_win, spec_col(length, 0, 1)), (p.qk_win, spec_col(length, GROUPS, 1)), (p.v, spec_col(length, 0, 1)), (go, spec_col(length, 0, 1))]
        + [(k, small) for k in kept], window_back_outs(rows * length, length, 1), into=into)

def piece_mean(x):
    a = lax.broadcasted_iota(jnp.int32, (256, 256), 0) >> 6
    b = lax.broadcasted_iota(jnp.int32, (256, 256), 1) >> 6
    ones = jnp.where(a == b, 1.0 / 64, 0.0).astype(BF)
    high = x.astype(BF)
    return nn(high, ones) + nn((x - high.astype(F32)).astype(BF), ones)

def through_state(x_t, turned, state, group, line):
    state_t = state.T.astype(BF)
    parts = []
    for h in range(4):
        parts.append(nn(state_t[h * 64:(h + 1) * 64], features_t(x_t, turned, head_rows(group, h), line)))
    return jnp.concatenate(parts, axis=0).T

def state_for(row, core, kept, received, n):
    return jnp.where(row == core[0], kept[n].astype(F32), received[n].astype(F32))

def mix_kernel(core, low, q, kept, received, local, windowed, numer, mixed, q_t, line, turned, *, length):
    r, g = pl.program_id(0), pl.program_id(1)
    @pl.when(g == 0)
    def _():
        line[...] = early_line(low, r, length)
        turn_all(q[...], q_t, turned, line[...])
    for n, (group, at) in enumerate(groups()):
        num = local[:, at].astype(F32) + through_state(q_t, turned, state_for(r, core, kept, received, n), group, line[...])
        rho = lax.rsqrt(piece_mean(num * num) + EPSILON)
        numer[:, at] = num.astype(BF)
        mixed[:, at] = (num * rho + windowed[:, at].astype(F32)).astype(BF)

def mix(core, low, p, state, local, windowed, rows, length, deps=()):
    total = rows * length
    return call(functools.partial(mix_kernel, length=length), "mix", (rows, STEPS),
        [(core, SMEM), (low, SMEM), (p.q_lin, spec_all(length)), (state[0], SPEC_STATE), (state[1], SPEC_STATE), (local, spec_col(length)), (windowed, spec_col(length))],
        [((total, 1024), BF, spec_col(length)), ((total, 1024), BF, spec_col(length))],
        [pltpu.VMEM((256, length), BF), pltpu.VMEM((1, length), F32), turned_scratch(length)], deps=deps)

def numer_back_kernel(core, low, q, numer, gm, grad_numer, mine, send, q_t, line, turned, *, length):
    r, g = pl.program_id(0), pl.program_id(1)
    @pl.when(g == 0)
    def _():
        line[...] = early_line(low, r, length)
        turn_all(q[...], q_t, turned, line[...])
    flag = (low[(r + 1) * (length // WINDOW) - 1] >= 0).astype(F32)
    for group, at in groups():
        num = numer[:, at].astype(F32)
        rho = lax.rsqrt(piece_mean(num * num) + EPSILON)
        lin = num * rho
        gl = gm[:, at].astype(F32)
        gn = (rho * (gl - lin * piece_mean(gl * lin))).astype(BF)
        grad_numer[:, at] = gn
        put_state(group, states_of(q_t, turned, gn, group, line[...], flag), core, mine, send)

def numer_back(core, low, p, numer, gm, rows, length, deps=()):
    total = rows * length
    return call(functools.partial(numer_back_kernel, length=length), "numer_back", (rows, STEPS),
        [(core, SMEM), (low, SMEM), (p.q_lin, spec_all(length)), (numer, spec_col(length)), (gm, spec_col(length))],
        [((total, 1024), BF, spec_col(length))] + state_outs(),
        [pltpu.VMEM((256, length), BF), pltpu.VMEM((1, length), F32), turned_scratch(length)], deps=deps)

def intra_back_kernel(core, low, high, q, k, v, gn, dv_in, kept, received, dq, dk_t, dv, mask, q_t, k_t, dq_t, early, turned, pulled, *, length, row):
    g = pl.program_id(1)
    half = length // 2
    @pl.when(g == 0)
    def _():
        lows, highs = spread(scalars(low, row, length), length), spread(scalars(high, row, length), length)
        j = lax.broadcasted_iota(jnp.int32, (length, length), 0)
        i = lax.broadcasted_iota(jnp.int32, (length, length), 1)
        mask[...] = ((j >= lows) & (j <= i) & (j < highs)).astype(BF)
        early[...] = (lows < 0).astype(F32)
        turn_all(q[...], q_t, turned, None)
        k_t[...] = k[...].astype(F32).T.astype(BF)
    quarter = FEAT ** -0.5
    qv, kv = q[...] * jnp.bfloat16(quarter), k[...]
    for n, (group, cols) in enumerate(groups()):
        vv, gv = v[:, cols], gn[:, cols]
        st = state_for(row, core, kept, received, n).astype(BF)
        top = dv_in[:half, cols].astype(F32)
        bottom = dv_in[half:, cols].astype(F32)
        for h in range(4):
            at = head_rows(group, h)
            km = kv * lane_mask(HEADS * FEAT, FEAT, group * 4 + h)
            vm = vv * lane_mask(256, 64, h)
            gm = gv * (lane_mask(256, 64, h) * jnp.bfloat16(0.5))
            qx, kx = q_t[at, :], k_t[at, :]
            qb, kb = qx * jnp.bfloat16(quarter), kx * jnp.bfloat16(quarter)
            u0 = 1.0 + nt(km[:half], qv)
            u1 = 1.0 + nt(km[half:], qv[half:])
            ga0 = nt(vm[:half], gv)
            ga1 = nt(vm[half:], gv[half:])
            m0, m1 = mask[:half, :], mask[half:, half:]
            a0 = (1.0 + u0 * u0).astype(BF) * m0
            a1 = (1.0 + u1 * u1).astype(BF) * m1
            ds0 = (ga0 * u0).astype(BF) * m0
            ds1 = (ga1 * u1).astype(BF) * m1
            top = top + nn(a0, gm)
            bottom = bottom + nn(a1, gm[half:])
            dk_t[0, at, :half] = nt(qb, ds0)
            dk_t[0, at, half:] = nt(qb[:, half:], ds1)
            d = nn(kb[:, :half], ds0)
            d = d + jnp.concatenate([jnp.zeros((FEAT, half), F32), nn(kb[:, half:], ds1)], axis=1)
            gphi = nt(st * lane_mask(256, 64, h), gv)
            dq_t[at, :] = d + features_back_t(q_t, turned, at, gphi * early[...], pulled)
        dv[:half, cols] = top.astype(BF)
        dv[half:, cols] = bottom.astype(BF)
    @pl.when(g == pl.num_programs(1) - 1)
    def _():
        dq[...] = (dq_t[...] + turned_back(pulled)).T.astype(BF)

def intra_back(core, low, high, p, gn, dv_in, state, rows, length, row, deps=(), into=None):
    total = rows * length
    return call(functools.partial(intra_back_kernel, length=length, row=row), "intra_back", (1, STEPS),
        [(core, SMEM), (low, SMEM), (high, SMEM), (p.q_lin, spec_all(length, row)), (p.k_lin, spec_all(length, row)), (p.v, spec_col(length, 0, row)),
         (gn, spec_col(length, 0, row)), (dv_in, spec_col(length, 0, row)), (state[0], SPEC_STATE), (state[1], SPEC_STATE)],
        [((total, 256), BF, spec_all(length, row)), ((rows, 256, length), F32, spec_t(length, row)), ((total, 1024), BF, spec_col(length, 0, row))],
        [pltpu.VMEM((length, length), BF)] + [pltpu.VMEM((256, length), BF)] * 2 + [pltpu.VMEM((256, length), F32), pltpu.VMEM((1, length), F32)] + [turned_scratch(length)] * 2,
        flops=HEADS * 2 * 15 * 256 ** 3, deps=deps, into=into)

def state_back_kernel(core, low, high, k, v, dk_in, dv_in, dhv, kept, received, dk, dv, k_t, dk_t, line, turned, pulled, *, length):
    r, g = pl.program_id(0), pl.program_id(1)
    @pl.when(g == 0)
    def _():
        line[...] = owned_line(low, high, r, length)
        turn_all(k[...], k_t, turned, line[...])
    tail = length - WINDOW
    for n, (group, cols) in enumerate(groups()):
        st = state_for(r, core, kept, received, n)
        sb = st.astype(BF)
        vv = v[:, cols]
        total = dv_in[:, cols].astype(F32) + through_state(k_t, turned, st, group, line[...])
        dv[:tail, cols] = total[:tail].astype(BF)
        dv[tail:, cols] = (total[tail:] + dhv[:, cols].astype(F32)).astype(BF)
        for h in range(4):
            at = head_rows(group, h)
            gphi = nt(sb * lane_mask(256, 64, h), vv)
            dk_t[at, :] = dk_in[0, at, :] + features_back_t(k_t, turned, at, gphi * line[...], pulled)
    @pl.when(g == pl.num_programs(1) - 1)
    def _():
        dk[...] = (dk_t[...] + turned_back(pulled)).T.astype(BF)

def state_back(core, low, high, p, dk_in, dv_in, returned, state, rows, length, deps=()):
    total = rows * length
    tail = pl.BlockSpec((None, WINDOW, 256 * EACH), lambda r, g: (1, r, g))
    return call(functools.partial(state_back_kernel, length=length), "state_back", (rows, STEPS),
        [(core, SMEM), (low, SMEM), (high, SMEM), (p.k_lin, spec_all(length)), (p.v, spec_col(length)), (dk_in, spec_t(length)), (dv_in, spec_col(length)),
         (returned, tail), (state[0], SPEC_STATE), (state[1], SPEC_STATE)],
        [((total, 256), BF, spec_all(length)), ((total, 1024), BF, spec_col(length))],
        [pltpu.VMEM((256, length), BF), pltpu.VMEM((256, length), F32), pltpu.VMEM((1, length), F32)] + [turned_scratch(length)] * 2, deps=deps)

def tail_kernel(x, got, out):
    out[...] = (x[...].astype(F32) + got[...].astype(F32)).astype(BF)

def tail_added(x, returned, rows, length, deps=()):
    per_row = length // WINDOW
    end = pl.BlockSpec((WINDOW, x.shape[1]), lambda r: ((r + 1) * per_row - 1, 0))
    return call(tail_kernel, "tail", (rows,), [(x, end), (returned, pl.BlockSpec((None, WINDOW, x.shape[1]), lambda r: (0, r, 0)))],
        [(x.shape, BF, end)], flops=10, moved=MIB, alias={0: 0}, deps=deps)[0]


ONE = dict(pipeline_mode=pl.Buffered(1))
def resident(shape):
    return pl.BlockSpec(shape, lambda *s: (0,) * len(shape), **ONE)

class Projected:
    pass

def keys_kernel(tokens, gain, wk, wv, normed, k, v):
    @pl.when(pl.program_id(0) == 0)
    def _():
        x = tokens[...].astype(F32)
        normed[...] = (x * lax.rsqrt(jnp.mean(x * x, axis=-1, keepdims=True) + EPSILON) * gain[...]).astype(BF)
        k[...] = nn(normed[...], wk[...]).astype(BF)
    v[...] = nn(normed[...], wv[...]).astype(BF)

def rest_kernel(normed, part, wq, w, q, out, normed_t):
    @pl.when(pl.program_id(0) == 0)
    def _():
        q[...] = nn(normed[...], wq[...]).astype(BF)
    normed_t[...] = part[...].T
    out[...] = nn(normed[...], w[...]).astype(BF)

def project_keys(p, tokens, gain, w_in):
    toks, width = tokens.shape
    lin = HEADS * FEAT
    first = (w_in.shape[1] - width) // 512
    p.normed, p.k_lin, p.v = call(keys_kernel, "project_keys", (width // 512,),
        [(tokens, resident((toks, width))), (gain.reshape(1, width), resident((1, width))), (w_in, pl.BlockSpec((width, lin), lambda s: (0, 1), **ONE)),
         (w_in, pl.BlockSpec((width, 512), lambda s: (0, first + s)))],
        [((toks, width), BF, resident((toks, width))), ((toks, lin), BF, resident((toks, lin))), ((toks, width), BF, pl.BlockSpec((toks, 512), lambda s: (0, s)))],
        flops=2 * toks * width * (width + lin))

def project_rest(p, w_in, deps=()):
    toks, width = p.normed.shape
    lin = HEADS * FEAT
    count = 2 * width // 512
    piece = toks // count
    p.q_lin, p.qk_win, p.normed_t = call(rest_kernel, "project_rest", (count,),
        [(p.normed, resident((toks, width))), (p.normed, pl.BlockSpec((piece, width), lambda s: (s, 0))), (w_in, pl.BlockSpec((width, lin), lambda s: (0, 0), **ONE)),
         (w_in, pl.BlockSpec((width, 512), lambda s: (0, 2 * lin // 512 + s)))],
        [((toks, lin), BF, resident((toks, lin))), ((toks, 2 * width), BF, pl.BlockSpec((toks, 512), lambda s: (0, s))),
         ((width, toks), BF, pl.BlockSpec((width, piece), lambda s: (0, s)))],
        flops=2 * toks * width * (2 * width + lin), deps=deps)

def mlp(core, mixed, tokens, cot, w_out, gain, w_gate_up, w_down, count, tile=256, chunk=1024):
    toks, width = mixed.shape
    ff = w_down.shape[0]
    steps = ff // tile
    half = width // 2
    big = resident((toks, width))
    across = pl.BlockSpec((half, tile), lambda s: (0, s))
    down = pl.BlockSpec((tile, half), lambda s: (s, 0))
    return call(functools.partial(mlp_kernel, steps=steps, chunk=chunk, each=width // count), "mlp", (steps,),
        [(core, SMEM), (mixed, big), (tokens, big), (cot, big), (w_out, resident((width, width))), (gain.reshape(1, width), resident((1, width))),
         (w_gate_up, pl.BlockSpec((width, tile), lambda s: (0, s))), (w_gate_up, pl.BlockSpec((width, tile), lambda s: (0, s + steps))),
         (w_down, pl.BlockSpec((tile, width), lambda s: (s, 0)))],
        [((toks, width), BF, big), ((toks, width), F32, big), ((toks, width), BF, big)] + [((half, ff), BF, across)] * 4
        + [((ff, half), BF, down)] * 2 + [((half, width), BF, resident((half, width)))] * 2,
        [pltpu.VMEM((toks, width), F32)] * 3 + [pltpu.VMEM((toks, width), BF), pltpu.VMEM((width, toks), BF), pltpu.VMEM((toks, tile), BF),
         pltpu.VMEM((toks, 2 * tile), BF), pltpu.VMEM((width, 2 * tile), BF)],
        flops=2 * toks * width * (9 * ff + 3 * width), moved=60 * MIB)

def weight_kernel(core, normed_t, *refs, counts, each):
    parts, (keep, send) = refs[:len(counts)], refs[len(counts):]
    step = pl.program_id(0)
    first = core[0] == 0
    begin = 0
    for ref, count in zip(parts, counts):
        @pl.when((step >= begin) & (step < begin + count))
        def _(ref=ref):
            keep[...], send[...] = parted(nn(normed_t[...], ref[...]), first, each)
        begin += count

def weight_grad(core, normed_t, parts, count, name, deps=()):
    width, toks = normed_t.shape
    counts = [p.shape[1] // 256 for p in parts]
    begins = [sum(counts[:n]) for n in range(len(counts))]
    def spec(begin, size):
        return pl.BlockSpec((toks, 256), lambda s: (0, jnp.clip(s - begin, 0, size - 1)))
    half = width // 2
    out = ((half, 256 * sum(counts)), BF, pl.BlockSpec((half, 256), lambda s: (0, s)))
    return call(functools.partial(weight_kernel, counts=counts, each=width // count), name, (sum(counts),),
        [(core, SMEM), (normed_t, resident((width, toks)))] + [(p, spec(b, n)) for p, b, n in zip(parts, begins, counts)],
        [out, out], flops=2 * width * toks * 256 * sum(counts), deps=deps)

def input_kernel(dq_lin, dk_lin, dq_win, dk_win, dv, w, tokens, gain, resid, out):
    begin, grad = 0, None
    for ref in (dq_lin, dk_lin, dq_win, dk_win, dv):
        size = ref.shape[1]
        term = nt(ref[...], w[:, begin:begin + size])
        grad = term if grad is None else grad + term
        begin += size
    x = tokens[...].astype(F32)
    scale = lax.rsqrt(jnp.mean(x * x, axis=-1, keepdims=True) + EPSILON)
    c = grad * gain[...]
    out[...] = resid[...] + scale * c - x * (scale * scale * scale * jnp.mean(c * x, axis=-1, keepdims=True))

def input_grad(parts, w_in, tokens, gain, resid, part, ways, name, deps=(), into=None):
    toks, width = tokens.shape
    piece = toks // ways
    by_rows = lambda columns: pl.BlockSpec((piece, columns), lambda s: (part, 0), **ONE)
    return call(input_kernel, name, (1,),
        [(p, by_rows(p.shape[1])) for p in parts] + [(w_in, resident(w_in.shape)), (tokens, by_rows(width)), (gain.reshape(1, width), resident((1, width))), (resid, by_rows(width))],
        [((toks, width), F32, by_rows(width))], flops=2 * piece * width * w_in.shape[1], deps=deps, into=into)

def swap(x, bit, count):
    return lax.ppermute(x, "seq", [(i, i ^ (1 << bit)) for i in range(count)])

def over(near, far):
    return near + (1.0 - near[FLAG_ROW:FLAG_ROW + 1, :]) * far

def begun_kernel(core, mine, received, total, *, backward):
    first = core[0] == 0
    for n in range(mine.shape[0]):
        m, r = mine[n], received[n].astype(F32)
        at0, at1 = jnp.where(first, m, r), jnp.where(first, r, m)
        total[n] = (over(at0, at1) if backward else over(at1, at0)).astype(BF)

def joined_kernel(ahead, total, received, new_total):
    here = ahead[0] == 1
    for n in range(total.shape[0]):
        t, r = total[n].astype(F32), received[n].astype(F32)
        new_total[n] = over(jnp.where(here, t, r), jnp.where(here, r, t)).astype(BF)

def ended_kernel(core, ahead, mine, *refs, backward):
    received, (kept, send) = refs[:-2], refs[-2:]
    first = core[0] == 0
    own = first ^ backward
    for n in range(mine.shape[0]):
        m, r = mine[n], received[0][n].astype(F32)
        base = jnp.where(own, m, r)
        e = jnp.zeros_like(m)
        for k, ref in enumerate(received[1:]):
            e = jnp.where(ahead[k] == 1, over(e, ref[n].astype(F32)), e)
        o = over(base, e)
        kept[n] = jnp.where(own, e, o).astype(BF)
        send[n] = jnp.where(own, o, e).astype(BF)

class Scan:
    def __init__(self, mine, send, me, count, backward):
        self.me, self.count, self.backward, self.mine = me, count, backward, mine
        self.received = [swap(send, 0, count)]
        self.bit, self.last = 0, count.bit_length() - 2
        self.core = (me % 2).reshape(1)
        self.ahead = ((me >> jnp.arange(1, self.last + 1, dtype=jnp.int32)) & 1) ^ (1 if backward else 0)
    def _call(self, kernel, name, flags, arrays, outs, through=()):
        shape = self.mine.shape
        whole = pl.BlockSpec(shape, lambda: (0, 0, 0))
        return call(kernel, name, (), [(f, SMEM) for f in flags] + [(a, whole) for a in arrays], [(shape, BF, whole)] * outs, flops=10, moved=MIB, through=through)
    def step(self, through=()):
        if self.bit == 0:
            self.total, *self.through = self._call(functools.partial(begun_kernel, backward=self.backward), "begun", [self.core], [self.mine, self.received[0]], 1, through)
        elif self.bit < self.last:
            self.total, = self._call(joined_kernel, "joined", [self.ahead[self.bit - 1:self.bit]], [self.total, self.received[-1]], 1)
        else:
            self.kept, self.total = self._call(functools.partial(ended_kernel, backward=self.backward), "ended", [self.core, self.ahead], [self.mine] + self.received, 2)
        self.bit += 1
        self.received.append(swap(self.total, self.bit if self.bit <= self.last else 0, self.count))
    def done(self):
        return self.kept, self.received[-1]

def padded(rows):
    return -(-rows // 16) * 16

class Piece:
    def __init__(self, arrays, first=0, size=None, rows=None):
        self.arrays = arrays
        self.first, self.size = first, size or arrays[0].shape[2]
        self.rows = rows or arrays[0].shape[1]
        self.height = self.size // 256 * padded(self.rows)

def add_kernel(*refs, plan, count, scalars):
    refs = refs[scalars:]
    ins, outs = refs[:-count], refs[-count:]
    for target, parts, at, height, rows, columns in plan:
        for k, sources in enumerate(parts):
            total = None
            for s in sources:
                term = ins[s][...].astype(F32)
                total = term if total is None else total + term
            total = total.astype(BF)
            pad = padded(rows)
            for c in range(columns // 256):
                outs[target + k][:, :, at + c * pad:at + c * pad + rows, :] = total[..., c * 256:(c + 1) * 256]

def add_up(groups, ways, name, most=4, deps=()):
    grid = min([most] + [outer for _, outer, _, _ in groups])
    ins, outs, plan = [], [], []
    for n, (pieces, outer, inner, own) in enumerate(groups):
        per = outer // grid
        at = 0
        for piece in pieces:
            parts = []
            for k in range(ways):
                sources = []
                for array in piece.arrays:
                    _, rows, columns = array.shape
                    def index(a, *own_refs, n=n, k=k, block=piece.first // piece.size):
                        return (a, own_refs[n][0] ^ k if ways > 1 else 0, 0, 0, block)
                    sources.append(len(ins))
                    ins.append((array.reshape(outer, ways, inner, rows, columns), pl.BlockSpec((per, None, inner, rows, piece.size), index)))
                parts.append(sources)
            plan.append((n * ways, parts, at, piece.height, piece.rows, piece.size))
            at += piece.height
        outs += [((outer, inner, at, 256), BF, pl.BlockSpec((per, inner, at, 256), lambda a, *own_refs: (a, 0, 0, 0)))] * ways
    got = call(functools.partial(add_kernel, plan=plan, count=len(outs), scalars=len(groups)), name, (grid,), ins, outs, flops=10, moved=20 * MIB,
        scalars=[own.reshape(1) for _, _, _, own in groups], deps=deps)
    got = [x.reshape((-1,) + x.shape[2:]) for x in got]
    return [got[n * ways:(n + 1) * ways] for n in range(len(groups))]

def chips_first(x, chips):
    return x.reshape(chips, x.shape[0] // chips, x.shape[1])

class MlpSum:
    def __init__(self, pairs, me, count):
        self.me, self.count, self.chips = me, count, count // 2
        self.pairs = [(chips_first(k, self.chips), chips_first(swap(s, 0, count), self.chips)) for k, s in pairs]
        self.bit = 0
    def step(self, deps=()):
        me, chips = self.me, self.chips
        bits = self.count.bit_length() - 1
        self.bit += 1
        if self.bit == 1:
            g, u, d, o = self.pairs
            half = lambda x, n: Piece(x, n * (x[0].shape[2] // 2), x[0].shape[2] // 2)
            pieces = [Piece(g), half(d, 0), half(o, 0)], [Piece(u), half(d, 1), half(o, 1)]
            self.layout = [(p.rows, p.size) for ps in pieces for p in ps]
            (ka, sa), (kb, sb) = add_up([(pieces[0], chips // 2, 1, (me >> 1) & 1), (pieces[1], chips // 4, 2, (me >> 2) & 1)], 2, "sum_first", deps=deps)
            self.a, self.b = [ka, swap(sa, 1, self.count)], [kb, swap(sb, 2, self.count)]
        elif self.bit == 2:
            (ka, sa), (kb, sb) = add_up([([Piece(self.a)], chips // 4, 1, (me >> 2) & 1), ([Piece(self.b)], chips // 4, 1, (me >> 1) & 1)], 2, "sum_second")
            self.a, self.b = [ka, swap(sa, 2, self.count)], [kb, swap(sb, 1, self.count)]
        else:
            pieces = [Piece(self.a), Piece(self.b)] if self.bit == 3 else [Piece(self.all)]
            (k, s), = add_up([(pieces, chips >> self.bit, 1, (me >> self.bit) & 1)], 2, "sum_more")
            self.all = [k, swap(s, self.bit, self.count)]

def quarters(pieces, bit, me, count):
    flip = lambda x, k: lax.ppermute(x, "seq", [(i, i ^ (k << bit)) for i in range(count)])
    parts, = add_up([(pieces, (count // 2) >> (bit + 1), 1, (me >> bit) & 3)], 4, "quarters", 2)
    return [parts[0]] + [flip(parts[k], k) for k in (3, 2, 1)]

class InSum:
    def __init__(self, me, count):
        self.me, self.count, self.chips = me, count, count // 2
        self.bit = 1
    def first(self, keep, send, columns):
        arrays = chips_first(keep, self.chips), chips_first(swap(send, 0, self.count), self.chips)
        return arrays, columns
    def second(self, arrays, columns):
        me, chips = self.me, self.chips
        a, b = ([Piece(arrays, first, size) for first, size in c] for c in columns)
        (ka, sa), (kb, sb) = add_up([(a, chips // 2, 1, (me >> 1) & 1), (b, chips // 4, 2, (me >> 2) & 1)], 2, "in_first")
        return [ka, swap(sa, 1, self.count)], [kb, swap(sb, 2, self.count)]
    def third(self, *parts):
        me, chips = self.me, self.chips
        a, b = ([Piece(p[n]) for p in parts] for n in (0, 1))
        (ka, sa), (kb, sb) = add_up([(a, chips // 4, 1, (me >> 2) & 1), (b, chips // 4, 1, (me >> 1) & 1)], 2, "in_second")
        self.arrays = [Piece([ka, swap(sa, 2, self.count)]), Piece([kb, swap(sb, 1, self.count)])]
        self.bit = 3
    def rest(self):
        while self.bit < self.count.bit_length() - 1:
            got = quarters(self.arrays, self.bit, self.me, self.count)
            self.arrays = [Piece(got)]
            self.bit += 2
        return got

def finish(rows, me, count):
    core = me % 2
    each = rows.shape[0] // 2
    own = lax.dynamic_slice_in_dim(rows, core * each, each, 0)
    got = swap(lax.dynamic_slice_in_dim(rows, (1 - core) * each, each, 0), 0, count)
    return jnp.concatenate([jnp.where(core == 0, own, got), jnp.where(core == 0, got, own)], axis=1)

def gathered_kernel(place, weights, gain, *refs, layout, rows):
    arrays, (out, gain_out) = refs[:-2], refs[-2:]
    total = None
    for n, at in enumerate(layout):
        g = None
        for ref in arrays:
            term = ref[0, at:at + rows, :].astype(F32)
            g = term if g is None else g + term
        out[:, n * 256:(n + 1) * 256] = g
        t = g * weights[:, n * 256:(n + 1) * 256].astype(F32)
        total = t if total is None else total + t
    gain_out[...] = jnp.sum(total, axis=1, keepdims=True) / gain[...]

def gathered(arrays, layout, weights, gain, me, count):
    each, columns = weights.shape[0] // count, weights.shape[1]
    if each < 16:
        weights, gain = lax.dynamic_slice_in_dim(weights, me * each, each, 0), lax.dynamic_slice_in_dim(gain, me * each, each, 0)
        me = jnp.zeros((), jnp.int32)
    mine = pl.BlockSpec((each, columns), lambda s, place: (place[0], 0))
    one = pl.BlockSpec((each, 1), lambda s, place: (place[0], 0))
    out, gain_out = call(functools.partial(gathered_kernel, layout=layout, rows=each), "gathered", (1,),
        [(weights, mine), (gain.reshape(-1, 1), one)] + [(a, resident(a.shape)) for a in arrays],
        [((each, columns), F32, resident((each, columns))), ((each, 1), F32, resident((each, 1)))], flops=10, moved=MIB, scalars=[me.reshape(1)])
    return out, gain_out.reshape(each)

def plain_kernel(*refs, pieces, shapes):
    arrays, outs = refs[:-len(shapes)], refs[-len(shapes):]
    for out, first, rows, column in pieces:
        g = None
        for ref in arrays:
            term = ref[0, first:first + rows, :].astype(F32)
            g = term if g is None else g + term
        outs[out][:, column:column + 256] = g

def plain(arrays, pieces, shapes):
    return call(functools.partial(plain_kernel, pieces=pieces, shapes=shapes), "plain", (1,), [(a, resident(a.shape)) for a in arrays],
        [(s, F32, resident(s)) for s in shapes], flops=10, moved=MIB)

def shards(tokens, seq_starts, seq_lengths, gain_in, gain_mlp, w_in, w_out, w_gate_up, w_down, cotangent):
    Order.last = None
    rows, length, width = tokens.shape
    count = lax.axis_size("seq")
    bits = count.bit_length() - 1
    order_a = list(range(1, bits))
    order_b = [2, 1] + list(range(3, bits))
    order_c = [3, 1, 2] + list(range(4, bits))
    me = lax.axis_index("seq")
    core = (me % 2).reshape(1)
    total = rows * length
    begin = me * length
    low = (seq_starts[:, ::WINDOW] - begin).reshape(-1)
    high = low + seq_lengths[:, ::WINDOW].reshape(-1)

    x = tokens.reshape(total, width)
    cot = cotangent.reshape(total, width)
    p = Projected()
    project_keys(p, x, gain_in, w_in)
    scan = Scan(*local_states(core, low, high, p.k_lin, p.v, rows, length), me, count, False)
    project_rest(p, w_in)
    tails = lambda a, at: a.reshape(rows, length, -1)[:, -WINDOW:, at:at + width]
    forward = [(i, i + 1) for i in range(count - 1)]
    backward = [(i + 1, i) for i in range(count - 1)]
    halo = lax.ppermute(jnp.stack([tails(p.qk_win, width), tails(p.v, 0)]), "seq", forward).reshape(2, rows * WINDOW, width)
    scan.step()
    local = intra(low, high, p, rows, length, 0)
    scan.step()
    local, = intra(low, high, p, rows, length, 1, into=local)
    scan.step()
    windowed = window(low, high, p, halo, rows, length, 0)
    scan.step()
    windowed, = window(low, high, p, halo, rows, length, 1, into=windowed)
    while scan.bit < bits:
        scan.step()
    state_in = scan.done()
    numer, mixed = mix(core, low, p, state_in, local, windowed, rows, length)

    (result, grad_resid, grad_mixed, keep_g, send_g, keep_u, send_u, keep_d, send_d, keep_o, send_o) = mlp(
        core, mixed, x, cot, w_out, gain_mlp, w_gate_up, w_down, count)
    grad_numer, *grad_state_in = numer_back(core, low, p, numer, grad_mixed, rows, length)
    scan = Scan(*grad_state_in, me, count, True)

    scan.step(through=(send_g, send_u, send_d, send_o))
    mlp_sum = MlpSum(list(zip((keep_g, keep_u, keep_d, keep_o), scan.through)), me, count)
    back, dh, kept = window_back_first(low, high, p, halo, grad_mixed, rows, length)
    returned = lax.ppermute(dh, "seq", backward)
    scan.step()
    mlp_sum.step(deps=(returned,))
    scan.step()
    dq_win, dk_win, dv_win = window_back_second(low, high, p, grad_mixed, back, kept, rows, length)
    scan.step()
    inner = intra_back(core, low, high, p, grad_numer, dv_win, state_in, rows, length, 0)
    while scan.bit < bits:
        scan.step()
    inner = intra_back(core, low, high, p, grad_numer, dv_win, state_in, rows, length, 1, into=inner)
    dq_lin, dk_t, dv_part = inner
    mlp_sum.step()
    dk_win = tail_added(dk_win, returned, rows, length, deps=(scan.received[-1],))
    lin = HEADS * FEAT
    in_sum = InSum(me, count)
    early = in_sum.first(*weight_grad(core, p.normed_t, [dq_win, dk_win, dq_lin], count, "weight_grad_early"), (((0, width), (2 * width, lin)), ((width, width),)))
    dk_lin, dv = state_back(core, low, high, p, dk_t, dv_part, returned, scan.done(), rows, length)
    mlp_sum.step()
    late = in_sum.first(*weight_grad(core, p.normed_t, [dv, dk_lin], count, "weight_grad_late"), (((0, width // 2),), ((width // 2, width // 2), (width, lin))))
    parts = [dq_lin, dk_lin, dq_win, dk_win, dv]
    early = in_sum.second(*early)
    grad_tokens = input_grad(parts, w_in, x, gain_in, grad_resid, 0, 4, "input_grad_first")
    late = in_sum.second(*late)
    while mlp_sum.bit < bits - 1:
        mlp_sum.step()
    grad_tokens = input_grad(parts, w_in, x, gain_in, grad_resid, 1, 4, "input_grad", into=grad_tokens)
    in_sum.third(early, late)
    grad_tokens, = input_grad(parts, w_in, x, gain_in, grad_resid, 1, 2, "input_grad", into=grad_tokens)
    ff, each, chip = w_down.shape[0], width // count, w_down.shape[0] // (count // 2)
    pad = padded(each)
    height = ff // 256 * pad
    second = height + padded(chip) + 2 * pad
    part_gate_up, part_gain_mlp = gathered(mlp_sum.all, [n * pad for n in range(ff // 256)] + [second + n * pad for n in range(ff // 256)],
        w_gate_up, gain_mlp, me, count)
    in_got = in_sum.rest()
    down, part_out = plain(mlp_sum.all, [(0, height, chip, 0), (0, second + height, chip, 256)]
        + [(1, height + padded(chip) + n * pad + (second - 2 * pad if n >= 2 else 0), each, n * 256) for n in range(4)],
        [(chip, width // 2), (each, width)])
    part_down = finish(down, me, count)
    wide, piece = width // 256, list(range(3 * width // 256 + 2 * lin // 256))
    q_win, q_lin, v_a, k_win, v_b, k_lin = (piece[wide * n // 2 + m:wide * (n + c) // 2 + m + k] for n, m, c, k in
        ((0, 0, 2, 0), (2, 0, 0, 1), (2, 1, 1, 0), (3, 1, 2, 0), (5, 1, 1, 0), (6, 1, 0, 1)))
    part_in, part_gain_in = gathered(in_got, [n * pad for n in q_lin + k_lin + q_win + k_win + v_a + v_b], w_in, gain_in, me, count)
    return (result.reshape(rows, length, width), grad_tokens.reshape(rows, length, width), part_gain_in, part_gain_mlp,
            part_in, part_out, part_gate_up, part_down)

def solution(mesh):
    split = P(None, "seq", None)
    placed = (split, P(None, "seq"), P(None, "seq"), P(), P(), P(), P(), P(), P(), split)
    return jax.shard_map(shards, mesh=mesh, in_specs=placed,
        out_specs=(split, split, P("seq"), P("seq"), P("seq", None), P("seq", None), P("seq", None), P("seq", None)),
        check_vma=False)
```

profile of v0, /device:TPU:0, one launch (start us, length us, event | category | flops | bytes accessed | tf_op | source)
XLA Modules:
  0.0 442.4 jit_solution(1192202331426501459)
XLA Ops:
  3.0 6.7 %project_keys.1 = (bf16[1024,1024]{1,0:T(8,128)(2,1)}, bf16[1024,256]{1,0:T(8,128)(2,1)}, bf16[1024,1024]{1,0:T(8,128)(2,1)}) custom-call(bf16[1024,1024]{1,0:T(8,128)(2,1)} %bitcast.98, f32[1,1024]{1,0:T(1,128)} %bitcast.129, bf16[1024,3584]{1,0:T(8,128)(2,1)} %refs_1_.3, bf16[1024,3584]{1,0:T(8,128)(2,1)} %refs_1_.3), custom_call_target="tpu_custom_call" | custom-call | flops 6800000000 | bytes 1000 | tf_op jit(solution)/shard_map/project_keys/pallas_call | solution.py:144
  9.6 8.0 %state.1 = (f32[4,160,256]{2,1,0:T(8,128)}, bf16[4,160,256]{2,1,0:T(8,128)(2,1)}) custom-call(s32[1]{0:T(128)} %bitcast.refs_0_, s32[16]{0:T(128)} %copy-done.2, s32[16]{0:T(128)} %add.21.refs_2_.refs_1_, bf16[1024,256]{1,0:T(8,128)(2,1)} %get-tuple-element.98.refs_3_.refs_4_, bf16[1024,1024]{1,0:T(8,128)(2,1)} %get-tuple-element.99.refs_4_.refs_10_.refs_5_, ...), custom_call_target="tpu_custom_call" | custom-call | flops 7400000000 | bytes 1000 | tf_op jit(solution)/shard_map/state/pallas_call | solution.py:144
  18.1 10.1 %project_rest.1 = (bf16[1024,256]{1,0:T(8,128)(2,1)}, bf16[1024,2048]{1,0:T(8,128)(2,1)}, bf16[1024,1024]{1,0:T(8,128)(2,1)}) custom-call(bf16[1024,1024]{1,0:T(8,128)(2,1)} %get-tuple-element.97.refs_5_.refs_0_.refs_1_, bf16[1024,1024]{1,0:T(8,128)(2,1)} %get-tuple-element.97.refs_5_.refs_0_.refs_1_, bf16[1024,3584]{1,0:T(8,128)(2,1)} %refs_1_.3, ...), custom_call_target="tpu_custom_call" | custom-call | flops 10000000000 | bytes 1000 | tf_op jit(solution)/shard_map/project_rest/pallas_call | solution.py:144
  30.9 2.9 collective-permute-start.4
  35.1 2.0 begun.2.refs_5_.refs_1_
  37.1 2.2 collective-permute-start.1
  39.3 6.3 %intra.2.refs_3_.refs_6_ = bf16[1024,1024]{1,0:T(8,128)(2,1)} custom-call(s32[16]{0:T(128)} %copy-done.2, s32[16]{0:T(128)} %add.21.refs_2_.refs_1_, bf16[1024,256]{1,0:T(8,128)(2,1)} %get-tuple-element.101.refs_3_.refs_2_, bf16[1024,256]{1,0:T(8,128)(2,1)} %get-tuple-element.98.refs_3_.refs_4_, ...), custom_call_target="tpu_custom_call" | custom-call | flops 7200000000 | bytes 1000 | tf_op jit(solution)/shard_map/intra/pallas_call | solution.py:144
  45.6 2.7 collective-permute-done.1.refs_2_.refs_4_
  48.2 2.6 joined.6.refs_5_.refs_1_
  50.9 1.8 collective-permute-start.2
  52.7 6.3 %intra.3.refs_3_.refs_5_ = bf16[1024,1024]{1,0:T(8,128)(2,1)} custom-call(s32[16]{0:T(128)} %copy-done.2, s32[16]{0:T(128)} %add.21.refs_2_.refs_1_, bf16[1024,256]{1,0:T(8,128)(2,1)} %get-tuple-element.101.refs_3_.refs_2_, bf16[1024,256]{1,0:T(8,128)(2,1)} %get-tuple-element.98.refs_3_.refs_4_, ...), custom_call_target="tpu_custom_call", output_to_operand_aliasing={{}: (6, {})} | custom-call | flops 7200000000 | bytes 1000 | tf_op jit(solution)/shard_map/intra/pallas_call | solution.py:144
  59.0 1.9 collective-permute-done.2.refs_2_.refs_5_
  60.9 2.6 joined.7.refs_7_.refs_1_
  63.5 3.8 collective-permute-start.3
  67.3 6.4 %window.2.refs_3_.refs_8_ = bf16[1024,1024]{1,0:T(8,128)(2,1)} custom-call(s32[16]{0:T(128)} %copy-done.2, s32[16]{0:T(128)} %add.21.refs_2_.refs_1_, bf16[1024,2048]{1,0:T(8,128)(2,1)} %get-tuple-element.103.refs_2_.refs_3_.refs_8_.refs_9_, bf16[1024,2048]{1,0:T(8,128)(2,1)} %get-tuple-element.103.refs_2_.refs_3_.refs_8_.refs_9_, ...), custom_call_target="tpu_custom_call" | custom-call | flops 8499999744 | bytes 1000 | tf_op jit(solution)/shard_map/window/pallas_call | solution.py:144
  75.1 2.6 joined.8.refs_7_
  77.7 2.8 collective-permute-start.5
  80.5 6.3 %window.3.refs_8_.refs_6_ = bf16[1024,1024]{1,0:T(8,128)(2,1)} custom-call(s32[16]{0:T(128)} %copy-done.2, s32[16]{0:T(128)} %add.21.refs_2_.refs_1_, bf16[1024,2048]{1,0:T(8,128)(2,1)} %get-tuple-element.103.refs_2_.refs_3_.refs_8_.refs_9_, bf16[1024,2048]{1,0:T(8,128)(2,1)} %get-tuple-element.103.refs_2_.refs_3_.refs_8_.refs_9_, ...), custom_call_target="tpu_custom_call", output_to_operand_aliasing={{}: (8, {})} | custom-call | flops 8499999744 | bytes 1000 | tf_op jit(solution)/shard_map/window/pallas_call | solution.py:144
  86.8 7.9 %collective-permute-done.5.refs_7_ = bf16[4,160,256]{2,1,0:T(8,128)(2,1)} collective-permute-done((bf16[4,160,256]{2,1,0:T(8,128)(2,1)}, bf16[4,160,256]{2,1,0:T(8,128)(2,1)}, u32[]{:S(2)}, u32[]{:S(2)}) %collective-permute-start.5) | collective-permute-done | bytes 327712 | tf_op jit(solution)/shard_map/ppermute | solution.py:691
  94.7 2.9 ended.2
  97.5 2.0 collective-permute-done.6.refs_4_.refs_9_
  99.5 8.4 %mix.1 = (bf16[1024,1024]{1,0:T(8,128)(2,1)}, bf16[1024,1024]{1,0:T(8,128)(2,1)}) custom-call(s32[1]{0:T(128)} %bitcast.refs_0_, s32[16]{0:T(128)} %copy-done.2, bf16[1024,256]{1,0:T(8,128)(2,1)} %get-tuple-element.101.refs_3_.refs_2_, bf16[4,160,256]{2,1,0:T(8,128)(2,1)} %get-tuple-element.104.refs_3_.refs_8_, ...), custom_call_target="tpu_custom_call" | custom-call | flops 10000000000 | bytes 1000 | tf_op jit(solution)/shard_map/mix/pallas_call | solution.py:144
  107.9 74.9 %mlp.1 = (bf16[1024,1024]{1,0:T(8,128)(2,1)}, f32[1024,1024]{1,0:T(8,128)}, bf16[1024,1024]{1,0:T(8,128)(2,1)}, bf16[512,2816]{1,0:T(8,128)(2,1)}, bf16[512,2816...) custom-call(s32[1]{0:T(128)} %bitcast.refs_0_, ...), custom_call_target="tpu_custom_call" | custom-call | flops 88000004096 | bytes 1000 | tf_op jit(solution)/shard_map/mlp/pallas_call | solution.py:144
  182.8 13.6 %numer_back.1 = (bf16[1024,1024]{1,0:T(8,128)(2,1)}, f32[4,160,256]{2,1,0:T(8,128)}, bf16[4,160,256]{2,1,0:T(8,128)(2,1)}) custom-call(s32[1]{0:T(128)} %bitcast.refs_0_, s32[16]{0:T(128)} %copy-done.2, bf16[1024,256]{1,0:T(8,128)(2,1)} %get-tuple-element.101.refs_3_.refs_2_, bf16[1024,1024]{1,0:T(8,128)(2,1)} %get-tuple-element.107.refs_9_.refs_3_, ...), custom_call_target="tpu_custom_call" | custom-call | flops 12000000000 | bytes 1000 | tf_op jit(solution)/shard_map/numer_back/pallas_call | solution.py:144
  196.5 1.8 collective-permute-done.7.refs_2_.refs_3_
  198.3 2.0 begun.3
  202.2 11.5 %window_back.2 = (bf16[1024,1024]{1,0:T(8,128)(2,1)}, bf16[1024,1024]{1,0:T(8,128)(2,1)}, bf16[1024,1024]{1,0:T(8,128)(2,1)}, bf16[2,128,1024]{2,1,0:T(8,128)(2,...) custom-call(s32[16]{0:T(128)} %copy-done.2, s32[16]{0:T(128)} %add.21.refs_2_.refs_1_, ...), custom_call_target="tpu_custom_call" | custom-call | flops 12999999488 | bytes 1000 | tf_op jit(solution)/shard_map/window_back/pallas_call | solution.py:144
  216.1 2.5 joined.9.refs_27_.refs_1_
  218.6 6.4 %collective-permute-start.9 = (bf16[4,160,256]{2,1,0:T(8,128)(2,1)}, bf16[4,160,256]{2,1,0:T(8,128)(2,1)}, u32[]{:S(2)}, u32[]{:S(2)}) collective-permute-start(bf16[4,160,256]{2,1,0:T(8,128)(2,1)} %joined.9.refs_27_.refs_1_), channel_id=1, source_target_pairs={{0,4},{1,5},{2,6},{3,7},{4,0},{5,1},{6,2},{7,3},{8,12},{9,13},{10,... | collective-permute-start | bytes 983048 | tf_op jit(solution)/shard_map/ppermute | solution.py:691
  225.0 10.7 %sum_first.1 = (bf16[8,1,592,256]{3,2,1,0:T(8,128)(2,1)}, bf16[8,1,592,256]{3,2,1,0:T(8,128)(2,1)}, bf16[4,2,592,256]{3,2,1,0:T(8,128)(2,1)}, bf16[4,2,592,256]{3,2,1,0:T(8,128)(2,1)}) custom-call(s32[1]{0:T(128)} %bitcast.11.refs_0_.refs_1_, s32[1]{0:T(128)} %bitcast.12.refs_1_.refs_0_, bf16[8,2,1,32,2816]{4,3,2,1,0:T(8,128)(2,1)} %bitcast.107, ...), custom_call_target="tpu_custom_call" | custom-call | flops 10599999488 | bytes 1000 | tf_op jit(solution)/shard_map/sum_first/pallas_call | solution.py:144
  235.7 2.5 joined.10.refs_9_.refs_1_
  240.6 11.3 %window_back.3 = (bf16[1024,1024]{1,0:T(8,128)(2,1)}, bf16[1024,1024]{1,0:T(8,128)(2,1)}, bf16[1024,1024]{1,0:T(8,128)(2,1)}) custom-call(s32[16]{0:T(128)} %copy-done.2, s32[16]{0:T(128)} %add.21.refs_2_.refs_1_, ...), custom_call_target="tpu_custom_call", output_to_operand_aliasing={{0}: (10, {}), {1}: (11, {}), {2}: (12, {})} | custom-call | flops 12999999488 | bytes 1000 | tf_op jit(solution)/shard_map/window_back/pallas_call | solution.py:144
  251.9 2.5 joined.11.refs_10_
  254.4 3.4 collective-permute-start.16
  257.8 14.6 %intra_back.2 = (bf16[1024,256]{1,0:T(8,128)(2,1)}, f32[2,256,512]{2,1,0:T(8,128)}, bf16[1024,1024]{1,0:T(8,128)(2,1)}) custom-call(s32[1]{0:T(128)} %bitcast.refs_0_, s32[16]{0:T(128)} %copy-done.2, s32[16]{0:T(128)} %add.21.refs_2_.refs_1_, bf16[1024,256]{1,0:T(8,128)(2,1)} %get-tuple-element.101.refs_3_.refs_2_, ...), custom_call_target="tpu_custom_call" | custom-call | flops 14000000000 | bytes 1000 | tf_op jit(solution)/shard_map/intra_back/pallas_call | solution.py:144
  273.6 2.9 ended.3
  276.5 14.9 %intra_back.3 = (bf16[1024,256]{1,0:T(8,128)(2,1)}, f32[2,256,512]{2,1,0:T(8,128)}, bf16[1024,1024]{1,0:T(8,128)(2,1)}) custom-call(s32[1]{0:T(128)} %bitcast.refs_0_, s32[16]{0:T(128)} %copy-done.2, s32[16]{0:T(128)} %add.21.refs_2_.refs_1_, ...), custom_call_target="tpu_custom_call", output_to_operand_aliasing={{0}: (11, {}), {1}: (12, {}), {2}: (13, {})} | custom-call | flops 14000000000 | bytes 1000 | tf_op jit(solution)/shard_map/intra_back/pallas_call | solution.py:144
  291.4 3.0 collective-permute-done.18
  295.6 6.4 %sum_second.1 = (bf16[4,1,592,256]{3,2,1,0:T(8,128)(2,1)}, bf16[4,1,592,256]{3,2,1,0:T(8,128)(2,1)}, bf16[4,1,592,256]{3,2,1,0:T(8,128)(2,1)}, bf16[4,1,592,256]{3,2,1,0:T(8,128)(2,1)}) custom-call(s32[1]{0:T(128)} %bitcast.12.refs_1_.refs_0_, s32[1]{0:T(128)} %bitcast.11.refs_0_.refs_1_, bf16[4,2,1,592,256]{4,3,2,1,0:T(8,128)(2,1)} %bitcast.137, ...), custom_call_target="tpu_custom_call" | custom-call | flops 6400000000 | bytes 1000 | tf_op jit(solution)/shard_map/sum_second/pallas_call | solution.py:144
  303.4 1.8 tail.1.refs_3_
  305.2 11.2 %weight_grad_early.1 = (bf16[512,2304]{1,0:T(8,128)(2,1)}, bf16[512,2304]{1,0:T(8,128)(2,1)}) custom-call(s32[1]{0:T(128)} %bitcast.refs_0_, bf16[1024,1024]{1,0:T(8,128)(2,1)} %get-tuple-element.144.refs_1_, bf16[1024,1024]{1,0:T(8,128)(2,1)} %get-tuple-element.135.refs_3_.refs_2_, bf16[1024,1024]{1,0:T(8,128)(2,1)} %tail.1.refs_3_, ...), custom_call_target="tpu_custom_call" | custom-call | flops 100000000 | bytes 1000 | tf_op jit(solution)/shard_map/weight_grad_early/pallas_call | solution.py:144
  316.4 11.3 %state_back.1 = (bf16[1024,256]{1,0:T(8,128)(2,1)}, bf16[1024,1024]{1,0:T(8,128)(2,1)}) custom-call(s32[1]{0:T(128)} %bitcast.refs_0_, s32[16]{0:T(128)} %copy-done.2, s32[16]{0:T(128)} %add.21.refs_2_.refs_1_, bf16[1024,256]{1,0:T(8,128)(2,1)} %get-tuple-element.98.refs_3_.refs_4_, bf16[1024,1024]{1,0:T(8,128)(2,1)} %get-tuple-element.99.refs_4_.refs_10_.refs_5_, ...), custom_call_target="tpu_custom_call" | custom-call | flops 100000000 | bytes 1000 | tf_op jit(solution)/shard_map/state_back/pallas_call | solution.py:144
  327.7 3.4 collective-permute-done.21
  331.5 3.6 sum_more.2
  335.1 7.3 %weight_grad_late.1 = (bf16[512,1280]{1,0:T(8,128)(2,1)}, bf16[512,1280]{1,0:T(8,128)(2,1)}) custom-call(s32[1]{0:T(128)} %bitcast.refs_0_, bf16[1024,1024]{1,0:T(8,128)(2,1)} %get-tuple-element.144.refs_1_, bf16[1024,1024]{1,0:T(8,128)(2,1)} %get-tuple-element.152.refs_2_.refs_4_, bf16[1024,256]{1,0:T(8,128)(2,1)} %get-tuple-element.151.refs_9_.refs_3_.refs_1_, ...), custom_call_target="tpu_custom_call" | custom-call | flops 100000000 | bytes 1000 | tf_op jit(solution)/shard_map/weight_grad_late/pallas_call | solution.py:144
  343.7 4.5 %in_first.2 = (bf16[8,1,160,256]{3,2,1,0:T(8,128)(2,1)}, bf16[8,1,160,256]{3,2,1,0:T(8,128)(2,1)}, bf16[4,2,128,256]{3,2,1,0:T(8,128)(2,1)}, bf16[4,2,128,256]{3,2,1,0:T(8,128)(2,1)}) custom-call(s32[1]{0:T(128)} %bitcast.11.refs_0_.refs_1_, s32[1]{0:T(128)} %bitcast.12.refs_1_.refs_0_, bf16[8,2,1,32,2304]{4,3,2,1,0:T(8,128)(2,1)} %bitcast.82, ...), custom_call_target="tpu_custom_call" | custom-call | flops 3000000000 | bytes 1000 | tf_op jit(solution)/shard_map/in_first/pallas_call | solution.py:144
  350.9 7.3 %input_grad_first.1.refs_14_.refs_10_ = f32[1024,1024]{1,0:T(8,128)} custom-call(bf16[1024,256]{1,0:T(8,128)(2,1)} %get-tuple-element.140.refs_10_.refs_4_.refs_0_, bf16[1024,256]{1,0:T(8,128)(2,1)} %get-tuple-element.151.refs_9_.refs_3_.refs_1_, bf16[1024,1024]{1,0:T(8,128)(2,1)} %get-tuple-element.135.refs_3_.refs_2_, bf16[1024,1024]{1,0:T(8,128)(2,1)} %tail.1.refs_3_, ...), custom_call_target="tpu_custom_call" | custom-call | flops 100000000 | bytes 1000 | tf_op jit(solution)/shard_map/input_grad_first/pallas_call | solution.py:144
  358.2 3.7 in_first.3
  363.5 8.4 %collective-permute-done.28 = bf16[2,1184,256]{2,1,0:T(8,128)(2,1)} collective-permute-done((bf16[2,1184,256]{2,1,0:T(8,128)(2,1)}, bf16[2,1184,256]{2,1,0:T(8,128)(2,1)}, u32[]{:S(2)}, u32[]{:S(2)}) %collective-permute-start.28) | collective-permute-done | bytes 1212448 | tf_op jit(solution)/shard_map/ppermute | solution.py:691
  371.9 2.8 sum_more.3
  374.7 3.4 collective-permute-start.31
  378.1 7.3 %input_grad.2.refs_18_.refs_10_ = f32[1024,1024]{1,0:T(8,128)} custom-call(bf16[1024,256]{1,0:T(8,128)(2,1)} %get-tuple-element.140.refs_10_.refs_4_.refs_0_, bf16[1024,256]{1,0:T(8,128)(2,1)} %get-tuple-element.151.refs_9_.refs_3_.refs_1_, bf16[1024,1024]{1,0:T(8,128)(2,1)} %get-tuple-element.135.refs_3_.refs_2_, ...), custom_call_target="tpu_custom_call", output_to_operand_aliasing={{}: (10, {})} | custom-call | flops 100000000 | bytes 1000 | tf_op jit(solution)/shard_map/input_grad/pallas_call | solution.py:144
  385.4 4.1 in_second.1
  391.5 1.7 copy.33.refs_2_
  393.2 10.7 %input_grad.3.refs_5_ = f32[1024,1024]{1,0:T(8,128)} custom-call(bf16[1024,256]{1,0:T(8,128)(2,1)} %get-tuple-element.140.refs_10_.refs_4_.refs_0_, bf16[1024,256]{1,0:T(8,128)(2,1)} %get-tuple-element.151.refs_9_.refs_3_.refs_1_, bf16[1024,1024]{1,0:T(8,128)(2,1)} %get-tuple-element.135.refs_3_.refs_2_, ...), custom_call_target="tpu_custom_call", output_to_operand_aliasing={{}: (10, {})} | custom-call | flops 100000000 | bytes 1000 | tf_op jit(solution)/shard_map/input_grad/pallas_call | solution.py:144
  404.9 2.4 gathered.2
  407.3 2.6 quarters.1
  409.8 2.1 plain.1
  412.9 1.7 copy.34.refs_2_
  416.0 2.6 collective-permute-start.32
  418.6 1.7 collective-permute-start.34
  422.1 4.6 %collective-permute-done.32.refs_4_ = bf16[1,448,256]{2,1,0:T(8,128)(2,1)} collective-permute-done((bf16[1,448,256]{2,1,0:T(8,128)(2,1)}, bf16[1,448,256]{2,1,0:T(8,128)(2,1)}, u32[]{:S(2)}, u32[]{:S(2)}) %collective-permute-start.32) | collective-permute-done | bytes 229408 | tf_op jit(solution)/shard_map/ppermute | solution.py:823
  426.7 11.7 %collective-permute-done.33.refs_5_ = bf16[1,448,256]{2,1,0:T(8,128)(2,1)} collective-permute-done((bf16[1,448,256]{2,1,0:T(8,128)(2,1)}, bf16[1,448,256]{2,1,0:T(8,128)(2,1)}, u32[]{:S(2)}, u32[]{:S(2)}) %collective-permute-start.33) | collective-permute-done | bytes 229408 | tf_op jit(solution)/shard_map/ppermute | solution.py:823
  438.3 2.3 gathered.3
  (76 shorter events, 33.1 us)
Async XLA Ops:
  1.5 0.9 copy-start.2
  17.6 17.5 %collective-permute-start = (bf16[4,160,256]{2,1,0:T(8,128)(2,1)}, bf16[4,160,256]{2,1,0:T(8,128)(2,1)}, u32[]{:S(2)}, u32[]{:S(2)}) collective-permute-start(bf16[4,160,256]{2,1,0:T(8,128)(2,1)} %get-tuple-element.102), channel_id=1, source_target_pairs={{0,1},{1,0},{2,3},{3,2},{4,5},{5,4},{6,7},{7,6},{8,9},{9,8},{10,11... | collective-permute-start | bytes 983048 | tf_op jit(solution)/shard_map/ppermute | solution.py:691
  30.9 36.3 %collective-permute-start.4 = (bf16[2,2,64,1024]{3,2,1,0:T(8,128)(2,1)}, bf16[2,2,64,1024]{3,2,1,0:T(8,128)(2,1)}, u32[]{:S(2)}, u32[]{:S(2)}) collective-permute-start(bf16[2,2,64,1024]{3,2,1,0:T(8,128)(2,1)} %pad_maximum_fusion), channel_id=1, source_target_pairs={{0,1},{1,2},{2,3},{3,4},{4,5},{5,6},{6,7},{7,8},{8,9},{9,10},{10,1... | collective-permute-start | bytes 1572872 | tf_op jit(solution)/shard_map/ppermute | solution.py:921
  33.9 0.5 copy-start.1
  37.1 11.1 %collective-permute-start.1 = (bf16[4,160,256]{2,1,0:T(8,128)(2,1)}, bf16[4,160,256]{2,1,0:T(8,128)(2,1)}, u32[]{:S(2)}, u32[]{:S(2)}) collective-permute-start(bf16[4,160,256]{2,1,0:T(8,128)(2,1)} %begun.2.refs_5_.refs_1_), channel_id=1, source_target_pairs={{0,2},{1,3},{2,0},{3,1},{4,6},{5,7},{6,4},{7,5},{8,10},{9,11},{10,... | collective-permute-start | bytes 983048 | tf_op jit(solution)/shard_map/ppermute | solution.py:691
  50.9 10.1 %collective-permute-start.2 = (bf16[4,160,256]{2,1,0:T(8,128)(2,1)}, bf16[4,160,256]{2,1,0:T(8,128)(2,1)}, u32[]{:S(2)}, u32[]{:S(2)}) collective-permute-start(bf16[4,160,256]{2,1,0:T(8,128)(2,1)} %joined.6.refs_5_.refs_1_), channel_id=1, source_target_pairs={{0,4},{1,5},{2,6},{3,7},{4,0},{5,1},{6,2},{7,3},{8,12},{9,13},{10,... | collective-permute-start | bytes 983048 | tf_op jit(solution)/shard_map/ppermute | solution.py:691
  63.5 11.6 %collective-permute-start.3 = (bf16[4,160,256]{2,1,0:T(8,128)(2,1)}, bf16[4,160,256]{2,1,0:T(8,128)(2,1)}, u32[]{:S(2)}, u32[]{:S(2)}) collective-permute-start(bf16[4,160,256]{2,1,0:T(8,128)(2,1)} %joined.7.refs_7_.refs_1_), channel_id=1, source_target_pairs={{0,8},{1,9},{2,10},{3,11},{4,12},{5,13},{6,14},{7,15},{8,0},{9,1},... | collective-permute-start | bytes 983048 | tf_op jit(solution)/shard_map/ppermute | solution.py:691
  77.7 16.9 %collective-permute-start.5 = (bf16[4,160,256]{2,1,0:T(8,128)(2,1)}, bf16[4,160,256]{2,1,0:T(8,128)(2,1)}, u32[]{:S(2)}, u32[]{:S(2)}) collective-permute-start(bf16[4,160,256]{2,1,0:T(8,128)(2,1)} %joined.8.refs_7_), channel_id=1, source_target_pairs={{0,16},{1,17},{2,18},{3,19},{4,20},{5,21},{6,22},{7,23},{8,24},{9,... | collective-permute-start | bytes 983048 | tf_op jit(solution)/shard_map/ppermute | solution.py:691
  97.5 2.0 collective-permute-start.6
  196.3 2.0 collective-permute-start.7
  200.3 24.6 %collective-permute-start.10 = (bf16[512,2816]{1,0:T(8,128)(2,1)}, bf16[512,2816]{1,0:T(8,128)(2,1)}, u32[]{:S(2)}, u32[]{:S(2)}) collective-permute-start(bf16[512,2816]{1,0:T(8,128)(2,1)} %get-tuple-element.123), channel_id=1, source_target_pairs={{0,1},{1,0},{2,3},{3,2},{4,5},{5,4},{6,7},{7,6},{8,9},{9,8},{10,11... | collective-permute-start | bytes 8650760 | tf_op jit(solution)/shard_map/ppermute | solution.py:691
  200.5 24.5 %collective-permute-start.11 = (bf16[2816,512]{1,0:T(8,128)(2,1)}, bf16[2816,512]{1,0:T(8,128)(2,1)}, u32[]{:S(2)}, u32[]{:S(2)}) collective-permute-start(bf16[2816,512]{1,0:T(8,128)(2,1)} %get-tuple-element.125), channel_id=1, source_target_pairs={{0,1},{1,0},{2,3},{3,2},{4,5},{5,4},{6,7},{7,6},{8,9},{9,8},{10,11... | collective-permute-start | bytes 8650760 | tf_op jit(solution)/shard_map/ppermute | solution.py:691
  200.8 24.1 %collective-permute-start.13 = (bf16[512,2816]{1,0:T(8,128)(2,1)}, bf16[512,2816]{1,0:T(8,128)(2,1)}, u32[]{:S(2)}, u32[]{:S(2)}) collective-permute-start(bf16[512,2816]{1,0:T(8,128)(2,1)} %get-tuple-element.129), channel_id=1, source_target_pairs={{0,1},{1,0},{2,3},{3,2},{4,5},{5,4},{6,7},{7,6},{8,9},{9,8},{10,11... | collective-permute-start | bytes 8650760 | tf_op jit(solution)/shard_map/ppermute | solution.py:691
  201.0 12.7 %collective-permute-start.8 = (bf16[4,160,256]{2,1,0:T(8,128)(2,1)}, bf16[4,160,256]{2,1,0:T(8,128)(2,1)}, u32[]{:S(2)}, u32[]{:S(2)}) collective-permute-start(bf16[4,160,256]{2,1,0:T(8,128)(2,1)} %get-tuple-element.117.refs_14_.refs_1_), channel_id=1, source_target_pairs={{0,2},{1,3},{2,0},{3,1},{4,6},{5,7},{6,4},{7,5},{8,10},{9,11},{10,... | collective-permute-start | bytes 983048 | tf_op jit(solution)/shard_map/ppermute | solution.py:691
  202.1 22.9 %collective-permute-start.12 = (bf16[512,1024]{1,0:T(8,128)(2,1)}, bf16[512,1024]{1,0:T(8,128)(2,1)}, u32[]{:S(2)}, u32[]{:S(2)}) collective-permute-start(bf16[512,1024]{1,0:T(8,128)(2,1)} %get-tuple-element.127), channel_id=1, source_target_pairs={{0,1},{1,0},{2,3},{3,2},{4,5},{5,4},{6,7},{7,6},{8,9},{9,8},{10,11... | collective-permute-start | bytes 3145736 | tf_op jit(solution)/shard_map/ppermute | solution.py:691
  213.6 5.0 %collective-permute-start.14 = (bf16[2,128,1024]{2,1,0:T(8,128)(2,1)}, bf16[2,128,1024]{2,1,0:T(8,128)(2,1)}, u32[]{:S(2)}, u32[]{:S(2)}) collective-permute-start(bf16[2,128,1024]{2,1,0:T(8,128)(2,1)} %get-tuple-element.130), channel_id=1, source_target_pairs={{1,0},{2,1},{3,2},{4,3},{5,4},{6,5},{7,6},{8,7},{9,8},{10,9},{11,1... | collective-permute-start | bytes 1572872 | tf_op jit(solution)/shard_map/ppermute | solution.py:943
  214.9 0.5 copy-start
  218.6 17.1 %collective-permute-start.9 = (bf16[4,160,256]{2,1,0:T(8,128)(2,1)}, bf16[4,160,256]{2,1,0:T(8,128)(2,1)}, u32[]{:S(2)}, u32[]{:S(2)}) collective-permute-start(bf16[4,160,256]{2,1,0:T(8,128)(2,1)} %joined.9.refs_27_.refs_1_), channel_id=1, source_target_pairs={{0,4},{1,5},{2,6},{3,7},{4,0},{5,1},{6,2},{7,3},{8,12},{9,13},{10,... | collective-permute-start | bytes 983048 | tf_op jit(solution)/shard_map/ppermute | solution.py:691
  238.3 13.6 %collective-permute-start.15 = (bf16[4,160,256]{2,1,0:T(8,128)(2,1)}, bf16[4,160,256]{2,1,0:T(8,128)(2,1)}, u32[]{:S(2)}, u32[]{:S(2)}) collective-permute-start(bf16[4,160,256]{2,1,0:T(8,128)(2,1)} %joined.10.refs_9_.refs_1_), channel_id=1, source_target_pairs={{0,8},{1,9},{2,10},{3,11},{4,12},{5,13},{6,14},{7,15},{8,0},{9,1},... | collective-permute-start | bytes 983048 | tf_op jit(solution)/shard_map/ppermute | solution.py:691
  238.8 55.6 %collective-permute-start.18 = (bf16[8,592,256]{2,1,0:T(8,128)(2,1)}, bf16[8,592,256]{2,1,0:T(8,128)(2,1)}, u32[]{:S(2)}, u32[]{:S(2)}) collective-permute-start(bf16[8,592,256]{2,1,0:T(8,128)(2,1)} %bitcast.142), channel_id=1, source_target_pairs={{0,2},{1,3},{2,0},{3,1},{4,6},{5,7},{6,4},{7,5},{8,10},{9,11},{10,... | collective-permute-start | bytes 7274504 | tf_op jit(solution)/shard_map/ppermute | solution.py:691
  240.1 55.5 %collective-permute-start.19 = (bf16[8,592,256]{2,1,0:T(8,128)(2,1)}, bf16[8,592,256]{2,1,0:T(8,128)(2,1)}, u32[]{:S(2)}, u32[]{:S(2)}) collective-permute-start(bf16[8,592,256]{2,1,0:T(8,128)(2,1)} %bitcast.141), channel_id=1, source_target_pairs={{0,4},{1,5},{2,6},{3,7},{4,0},{5,1},{6,2},{7,3},{8,12},{9,13},{10,... | collective-permute-start | bytes 7274504 | tf_op jit(solution)/shard_map/ppermute | solution.py:691
  254.4 19.1 %collective-permute-start.16 = (bf16[4,160,256]{2,1,0:T(8,128)(2,1)}, bf16[4,160,256]{2,1,0:T(8,128)(2,1)}, u32[]{:S(2)}, u32[]{:S(2)}) collective-permute-start(bf16[4,160,256]{2,1,0:T(8,128)(2,1)} %joined.11.refs_10_), channel_id=1, source_target_pairs={{0,16},{1,17},{2,18},{3,19},{4,20},{5,21},{6,22},{7,23},{8,24},{9,... | collective-permute-start | bytes 983048 | tf_op jit(solution)/shard_map/ppermute | solution.py:691
  276.4 27.0 %collective-permute-start.17 = (bf16[4,160,256]{2,1,0:T(8,128)(2,1)}, bf16[4,160,256]{2,1,0:T(8,128)(2,1)}, u32[]{:S(2)}, u32[]{:S(2)}) collective-permute-start(bf16[4,160,256]{2,1,0:T(8,128)(2,1)} %get-tuple-element.143), channel_id=1, source_target_pairs={{0,1},{1,0},{2,3},{3,2},{4,5},{5,4},{6,7},{7,6},{8,9},{9,8},{10,11... | collective-permute-start | bytes 983048 | tf_op jit(solution)/shard_map/ppermute | solution.py:691
  302.0 29.1 %collective-permute-start.21 = (bf16[4,592,256]{2,1,0:T(8,128)(2,1)}, bf16[4,592,256]{2,1,0:T(8,128)(2,1)}, u32[]{:S(2)}, u32[]{:S(2)}) collective-permute-start(bf16[4,592,256]{2,1,0:T(8,128)(2,1)} %bitcast.146), channel_id=1, source_target_pairs={{0,4},{1,5},{2,6},{3,7},{4,0},{5,1},{6,2},{7,3},{8,12},{9,13},{10,... | collective-permute-start | bytes 3637256 | tf_op jit(solution)/shard_map/ppermute | solution.py:691
  302.7 28.7 %collective-permute-start.22 = (bf16[4,592,256]{2,1,0:T(8,128)(2,1)}, bf16[4,592,256]{2,1,0:T(8,128)(2,1)}, u32[]{:S(2)}, u32[]{:S(2)}) collective-permute-start(bf16[4,592,256]{2,1,0:T(8,128)(2,1)} %bitcast.145), channel_id=1, source_target_pairs={{0,2},{1,3},{2,0},{3,1},{4,6},{5,7},{6,4},{7,5},{8,10},{9,11},{10,... | collective-permute-start | bytes 3637256 | tf_op jit(solution)/shard_map/ppermute | solution.py:691
  316.4 27.4 %collective-permute-start.20 = (bf16[512,2304]{1,0:T(8,128)(2,1)}, bf16[512,2304]{1,0:T(8,128)(2,1)}, u32[]{:S(2)}, u32[]{:S(2)}) collective-permute-start(bf16[512,2304]{1,0:T(8,128)(2,1)} %get-tuple-element.154), channel_id=1, source_target_pairs={{0,1},{1,0},{2,3},{3,2},{4,5},{5,4},{6,7},{7,6},{8,9},{9,8},{10,11... | collective-permute-start | bytes 7077896 | tf_op jit(solution)/shard_map/ppermute | solution.py:691
  342.4 15.7 %collective-permute-start.24 = (bf16[512,1280]{1,0:T(8,128)(2,1)}, bf16[512,1280]{1,0:T(8,128)(2,1)}, u32[]{:S(2)}, u32[]{:S(2)}) collective-permute-start(bf16[512,1280]{1,0:T(8,128)(2,1)} %get-tuple-element.162), channel_id=1, source_target_pairs={{0,1},{1,0},{2,3},{3,2},{4,5},{5,4},{6,7},{7,6},{8,9},{9,8},{10,11... | collective-permute-start | bytes 3932168 | tf_op jit(solution)/shard_map/ppermute | solution.py:691
  342.5 29.4 %collective-permute-start.28 = (bf16[2,1184,256]{2,1,0:T(8,128)(2,1)}, bf16[2,1184,256]{2,1,0:T(8,128)(2,1)}, u32[]{:S(2)}, u32[]{:S(2)}) collective-permute-start(bf16[2,1184,256]{2,1,0:T(8,128)(2,1)} %bitcast.144), channel_id=1, source_target_pairs={{0,8},{1,9},{2,10},{3,11},{4,12},{5,13},{6,14},{7,15},{8,0},{9,1},... | collective-permute-start | bytes 3637256 | tf_op jit(solution)/shard_map/ppermute | solution.py:691
  348.3 37.1 %collective-permute-start.23 = (bf16[8,160,256]{2,1,0:T(8,128)(2,1)}, bf16[8,160,256]{2,1,0:T(8,128)(2,1)}, u32[]{:S(2)}, u32[]{:S(2)}) collective-permute-start(bf16[8,160,256]{2,1,0:T(8,128)(2,1)} %bitcast.147), channel_id=1, source_target_pairs={{0,2},{1,3},{2,0},{3,1},{4,6},{5,7},{6,4},{7,5},{8,10},{9,11},{10,... | collective-permute-start | bytes 1966088 | tf_op jit(solution)/shard_map/ppermute | solution.py:691
  349.3 36.1 %collective-permute-start.26 = (bf16[8,128,256]{2,1,0:T(8,128)(2,1)}, bf16[8,128,256]{2,1,0:T(8,128)(2,1)}, u32[]{:S(2)}, u32[]{:S(2)}) collective-permute-start(bf16[8,128,256]{2,1,0:T(8,128)(2,1)} %bitcast.149), channel_id=1, source_target_pairs={{0,4},{1,5},{2,6},{3,7},{4,0},{5,1},{6,2},{7,3},{8,12},{9,13},{10,... | collective-permute-start | bytes 1572872 | tf_op jit(solution)/shard_map/ppermute | solution.py:691
  361.9 23.4 %collective-permute-start.27 = (bf16[8,96,256]{2,1,0:T(8,128)(2,1)}, bf16[8,96,256]{2,1,0:T(8,128)(2,1)}, u32[]{:S(2)}, u32[]{:S(2)}) collective-permute-start(bf16[8,96,256]{2,1,0:T(8,128)(2,1)} %bitcast.156), channel_id=1, source_target_pairs={{0,4},{1,5},{2,6},{3,7},{4,0},{5,1},{6,2},{7,3},{8,12},{9,13},{10,... | collective-permute-start | bytes 1179656 | tf_op jit(solution)/shard_map/ppermute | solution.py:691
  362.4 23.0 %collective-permute-start.25 = (bf16[8,64,256]{2,1,0:T(8,128)(2,1)}, bf16[8,64,256]{2,1,0:T(8,128)(2,1)}, u32[]{:S(2)}, u32[]{:S(2)}) collective-permute-start(bf16[8,64,256]{2,1,0:T(8,128)(2,1)} %bitcast.157), channel_id=1, source_target_pairs={{0,2},{1,3},{2,0},{3,1},{4,6},{5,7},{6,4},{7,5},{8,10},{9,11},{10,... | collective-permute-start | bytes 786440 | tf_op jit(solution)/shard_map/ppermute | solution.py:691
  374.7 30.2 %collective-permute-start.31 = (bf16[1,1184,256]{2,1,0:T(8,128)(2,1)}, bf16[1,1184,256]{2,1,0:T(8,128)(2,1)}, u32[]{:S(2)}, u32[]{:S(2)}) collective-permute-start(bf16[1,1184,256]{2,1,0:T(8,128)(2,1)} %bitcast.148), channel_id=1, source_target_pairs={{0,16},{1,17},{2,18},{3,19},{4,20},{5,21},{6,22},{7,23},{8,24},{9,... | collective-permute-start | bytes 1818632 | tf_op jit(solution)/shard_map/ppermute | solution.py:691
  389.5 17.8 %collective-permute-start.29 = (bf16[4,224,256]{2,1,0:T(8,128)(2,1)}, bf16[4,224,256]{2,1,0:T(8,128)(2,1)}, u32[]{:S(2)}, u32[]{:S(2)}) collective-permute-start(bf16[4,224,256]{2,1,0:T(8,128)(2,1)} %bitcast.155), channel_id=1, source_target_pairs={{0,4},{1,5},{2,6},{3,7},{4,0},{5,1},{6,2},{7,3},{8,12},{9,13},{10,... | collective-permute-start | bytes 1376264 | tf_op jit(solution)/shard_map/ppermute | solution.py:691
  389.9 17.3 %collective-permute-start.30 = (bf16[4,224,256]{2,1,0:T(8,128)(2,1)}, bf16[4,224,256]{2,1,0:T(8,128)(2,1)}, u32[]{:S(2)}, u32[]{:S(2)}) collective-permute-start(bf16[4,224,256]{2,1,0:T(8,128)(2,1)} %bitcast.154), channel_id=1, source_target_pairs={{0,2},{1,3},{2,0},{3,1},{4,6},{5,7},{6,4},{7,5},{8,10},{9,11},{10,... | collective-permute-start | bytes 1376264 | tf_op jit(solution)/shard_map/ppermute | solution.py:691
  412.8 7.6 %collective-permute-start.35 = (f32[88,512]{1,0:T(8,128)S(1)}, f32[88,512]{1,0:T(8,128)S(1)}, u32[]{:S(2)}, u32[]{:S(2)}) collective-permute-start(f32[88,512]{1,0:T(8,128)S(1)} %constant_dynamic-slice_fusion), channel_id=1, source_target_pairs={{0,1},{1,0},{2,3},{3,2},{4,5},{5,4},{6,7},{7,6},{8,9},{9,8},{10,11... | collective-permute-start | bytes 540680 | tf_op jit(solution)/shard_map/ppermute | solution.py:691
  416.0 10.7 %collective-permute-start.32 = (bf16[1,448,256]{2,1,0:T(8,128)(2,1)}, bf16[1,448,256]{2,1,0:T(8,128)(2,1)}, u32[]{:S(2)}, u32[]{:S(2)}) collective-permute-start(bf16[1,448,256]{2,1,0:T(8,128)(2,1)} %bitcast.160), channel_id=1, source_target_pairs={{0,24},{1,25},{2,26},{3,27},{4,28},{5,29},{6,30},{7,31},{8,16},{9,... | collective-permute-start | bytes 688136 | tf_op jit(solution)/shard_map/ppermute | solution.py:823
  418.6 19.7 %collective-permute-start.33 = (bf16[1,448,256]{2,1,0:T(8,128)(2,1)}, bf16[1,448,256]{2,1,0:T(8,128)(2,1)}, u32[]{:S(2)}, u32[]{:S(2)}) collective-permute-start(bf16[1,448,256]{2,1,0:T(8,128)(2,1)} %bitcast.159), channel_id=1, source_target_pairs={{0,16},{1,17},{2,18},{3,19},{4,20},{5,21},{6,22},{7,23},{8,24},{9,... | collective-permute-start | bytes 688136 | tf_op jit(solution)/shard_map/ppermute | solution.py:823
  418.6 19.7 %collective-permute-start.34 = (bf16[1,448,256]{2,1,0:T(8,128)(2,1)}, bf16[1,448,256]{2,1,0:T(8,128)(2,1)}, u32[]{:S(2)}, u32[]{:S(2)}) collective-permute-start(bf16[1,448,256]{2,1,0:T(8,128)(2,1)} %bitcast.158), channel_id=1, source_target_pairs={{0,8},{1,9},{2,10},{3,11},{4,12},{5,13},{6,14},{7,15},{8,0},{9,1},... | collective-permute-start | bytes 688136 | tf_op jit(solution)/shard_map/ppermute | solution.py:823
where the time goes:
time: 448 us; the launch traced here: 442 us
  Pallas kernels  326 us (73%)
  waiting for transfers between devices  52.4 us (12%)
  starting transfers between devices  46.2 us (10%)
  local copies, waits for them, and re-layouts  10.4 us (2%)
  other arithmetic  5.84 us (1%)
    pallas_call x42, Pallas kernels, call(): pl.pallas_call(body, grid_spec=pltpu.PrefetchScalarGridSpec(num_scalar_pr...  326 us
    ppermute x31, starting transfers between devices, swap(): return lax.ppermute(x, 'seq', [(i, i ^ 1 << bit) for i in range(count)])  37.5 us
    ppermute x31, waiting for transfers between devices, swap(): return lax.ppermute(x, 'seq', [(i, i ^ 1 << bit) for i in range(count)])  36.2 us
    ppermute x3, waiting for transfers between devices, quarters(): lax.ppermute(x, 'seq', [(i, i ^ k << bit) for i in range(count)])  16.2 us
  transfers between devices with their start and end apart: 36, of which 15 were waited for; matrix products, arithmetic and copies ran while one was open for 2% of the time, Pallas kernels for 45%

commit v1 on v0

--- a/solution.py
+++ b/solution.py
@@ -235,8 +235,10 @@
 def states_of(x_t, turned, y, group, line, flag):
     row = lax.broadcasted_iota(jnp.int32, (ROWS_PHI, 256), 0)
     out = jnp.where(row == FLAG_ROW, flag, 0.0)
+    phi = jnp.concatenate([features_t(x_t, turned, head_rows(group, h), line) for h in range(4)], axis=0)
+    every = nn(phi, y)
     for h in range(4):
-        out = out + nn(features_t(x_t, turned, head_rows(group, h), line), y * lane_mask(256, 64, h))
+        out = out + every[h * ROWS_PHI:(h + 1) * ROWS_PHI] * lane_mask(256, 64, h, F32)
     return out
 
 def put_state(g, state, core, mine, send):
@@ -502,30 +504,31 @@
         st = state_for(row, core, kept, received, n).astype(BF)
         top = dv_in[:half, cols].astype(F32)
         bottom = dv_in[half:, cols].astype(F32)
+        km = [kv * lane_mask(HEADS * FEAT, FEAT, group * 4 + h) for h in range(4)]
+        vm = [vv * lane_mask(256, 64, h) for h in range(4)]
+        u0 = nt(jnp.concatenate([x[:half] for x in km], axis=0), qv)
+        u1 = nt(jnp.concatenate([x[half:] for x in km], axis=0), qv[half:])
+        ga0 = nt(jnp.concatenate([x[:half] for x in vm], axis=0), gv)
+        ga1 = nt(jnp.concatenate([x[half:] for x in vm], axis=0), gv[half:])
+        gphi = nt(jnp.concatenate([st * lane_mask(256, 64, h) for h in range(4)], axis=0), gv) * early[...]
+        m0, m1 = mask[:half, :], mask[half:, half:]
         for h in range(4):
             at = head_rows(group, h)
-            km = kv * lane_mask(HEADS * FEAT, FEAT, group * 4 + h)
-            vm = vv * lane_mask(256, 64, h)
+            mine = slice(h * half, (h + 1) * half)
             gm = gv * (lane_mask(256, 64, h) * jnp.bfloat16(0.5))
-            qx, kx = q_t[at, :], k_t[at, :]
-            qb, kb = qx * jnp.bfloat16(quarter), kx * jnp.bfloat16(quarter)
-            u0 = 1.0 + nt(km[:half], qv)
-            u1 = 1.0 + nt(km[half:], qv[half:])
-            ga0 = nt(vm[:half], gv)
-            ga1 = nt(vm[half:], gv[half:])
-            m0, m1 = mask[:half, :], mask[half:, half:]
-            a0 = (1.0 + u0 * u0).astype(BF) * m0
-            a1 = (1.0 + u1 * u1).astype(BF) * m1
-            ds0 = (ga0 * u0).astype(BF) * m0
-            ds1 = (ga1 * u1).astype(BF) * m1
+            qb, kb = q_t[at, :] * jnp.bfloat16(quarter), k_t[at, :] * jnp.bfloat16(quarter)
+            w0, w1 = 1.0 + u0[mine], 1.0 + u1[mine]
+            a0 = (1.0 + w0 * w0).astype(BF) * m0
+            a1 = (1.0 + w1 * w1).astype(BF) * m1
+            ds0 = (ga0[mine] * w0).astype(BF) * m0
+            ds1 = (ga1[mine] * w1).astype(BF) * m1
             top = top + nn(a0, gm)
             bottom = bottom + nn(a1, gm[half:])
             dk_t[0, at, :half] = nt(qb, ds0)
             dk_t[0, at, half:] = nt(qb[:, half:], ds1)
             d = nn(kb[:, :half], ds0)
             d = d + jnp.concatenate([jnp.zeros((FEAT, half), F32), nn(kb[:, half:], ds1)], axis=1)
-            gphi = nt(st * lane_mask(256, 64, h), gv)
-            dq_t[at, :] = d + features_back_t(q_t, turned, at, gphi * early[...], pulled)
+            dq_t[at, :] = d + features_back_t(q_t, turned, at, gphi[h * ROWS_PHI:(h + 1) * ROWS_PHI], pulled)
         dv[:half, cols] = top.astype(BF)
         dv[half:, cols] = bottom.astype(BF)
     @pl.when(g == pl.num_programs(1) - 1)
@@ -555,10 +558,10 @@
         total = dv_in[:, cols].astype(F32) + through_state(k_t, turned, st, group, line[...])
         dv[:tail, cols] = total[:tail].astype(BF)
         dv[tail:, cols] = (total[tail:] + dhv[:, cols].astype(F32)).astype(BF)
+        gphi = nt(jnp.concatenate([sb * lane_mask(256, 64, h) for h in range(4)], axis=0), vv) * line[...]
         for h in range(4):
             at = head_rows(group, h)
-            gphi = nt(sb * lane_mask(256, 64, h), vv)
-            dk_t[at, :] = dk_in[0, at, :] + features_back_t(k_t, turned, at, gphi * line[...], pulled)
+            dk_t[at, :] = dk_in[0, at, :] + features_back_t(k_t, turned, at, gphi[h * ROWS_PHI:(h + 1) * ROWS_PHI], pulled)
     @pl.when(g == pl.num_programs(1) - 1)
     def _():
         dk[...] = (dk_t[...] + turned_back(pulled)).T.astype(BF)
@@ -589,42 +592,56 @@
 class Projected:
     pass
 
-def keys_kernel(tokens, gain, wk, wv, normed, k, v):
+def put_tails(tails, x, rows):
+    length = x.shape[0] // rows
+    for r in range(rows):
+        tails[r * WINDOW:(r + 1) * WINDOW, :] = x[(r + 1) * length - WINDOW:(r + 1) * length, :]
+
+def keys_kernel(tokens, gain, wk, wv, normed, k, v, tails, *, rows):
     @pl.when(pl.program_id(0) == 0)
     def _():
         x = tokens[...].astype(F32)
         normed[...] = (x * lax.rsqrt(jnp.mean(x * x, axis=-1, keepdims=True) + EPSILON) * gain[...]).astype(BF)
         k[...] = nn(normed[...], wk[...]).astype(BF)
     v[...] = nn(normed[...], wv[...]).astype(BF)
-
-def rest_kernel(normed, part, wq, w, q, out, normed_t):
-    @pl.when(pl.program_id(0) == 0)
-    def _():
-        q[...] = nn(normed[...], wq[...]).astype(BF)
+    put_tails(tails, v, rows)
+
+def queries_kernel(normed, w, out):
+    out[...] = nn(normed[...], w[...]).astype(BF)
+
+def rest_kernel(normed, part, w, tails, out, normed_t, *, rows):
     normed_t[...] = part[...].T
     out[...] = nn(normed[...], w[...]).astype(BF)
-
-def project_keys(p, tokens, gain, w_in):
+    put_tails(tails, out, rows)
+
+def project_keys(p, tokens, gain, w_in, rows):
     toks, width = tokens.shape
     lin = HEADS * FEAT
     first = (w_in.shape[1] - width) // 512
-    p.normed, p.k_lin, p.v = call(keys_kernel, "project_keys", (width // 512,),
+    p.normed, p.k_lin, p.v, p.tails = call(functools.partial(keys_kernel, rows=rows), "project_keys", (width // 512,),
         [(tokens, resident((toks, width))), (gain.reshape(1, width), resident((1, width))), (w_in, pl.BlockSpec((width, lin), lambda s: (0, 1), **ONE)),
          (w_in, pl.BlockSpec((width, 512), lambda s: (0, first + s)))],
-        [((toks, width), BF, resident((toks, width))), ((toks, lin), BF, resident((toks, lin))), ((toks, width), BF, pl.BlockSpec((toks, 512), lambda s: (0, s)))],
-        flops=2 * toks * width * (width + lin))
-
-def project_rest(p, w_in, deps=()):
+        [((toks, width), BF, resident((toks, width))), ((toks, lin), BF, resident((toks, lin))), ((toks, width), BF, pl.BlockSpec((toks, 512), lambda s: (0, s))),
+         ((2, rows * WINDOW, width), BF, pl.BlockSpec((None, rows * WINDOW, 512), lambda s: (1, 0, s)))])
+
+def project_queries(p, w_in):
+    toks, width = p.normed.shape
+    lin = HEADS * FEAT
+    p.q_lin, = call(queries_kernel, "project_queries", (1,),
+        [(p.normed, resident((toks, width))), (w_in, pl.BlockSpec((width, lin), lambda s: (0, 0), **ONE))],
+        [((toks, lin), BF, resident((toks, lin)))])
+
+def project_rest(p, w_in, rows):
     toks, width = p.normed.shape
     lin = HEADS * FEAT
     count = 2 * width // 512
     piece = toks // count
-    p.q_lin, p.qk_win, p.normed_t = call(rest_kernel, "project_rest", (count,),
-        [(p.normed, resident((toks, width))), (p.normed, pl.BlockSpec((piece, width), lambda s: (s, 0))), (w_in, pl.BlockSpec((width, lin), lambda s: (0, 0), **ONE)),
+    p.tails, p.qk_win, p.normed_t = call(functools.partial(rest_kernel, rows=rows), "project_rest", (count,),
+        [(p.normed, resident((toks, width))), (p.normed, pl.BlockSpec((piece, width), lambda s: (s, 0))),
          (w_in, pl.BlockSpec((width, 512), lambda s: (0, 2 * lin // 512 + s)))],
-        [((toks, lin), BF, resident((toks, lin))), ((toks, 2 * width), BF, pl.BlockSpec((toks, 512), lambda s: (0, s))),
-         ((width, toks), BF, pl.BlockSpec((width, piece), lambda s: (0, s)))],
-        flops=2 * toks * width * (2 * width + lin), deps=deps)
+        [((2, rows * WINDOW, width), BF, pl.BlockSpec((None, rows * WINDOW, 512), lambda s: (0, 0, jnp.maximum(s - count // 2, 0)))),
+         ((toks, 2 * width), BF, pl.BlockSpec((toks, 512), lambda s: (0, s))), ((width, toks), BF, pl.BlockSpec((width, piece), lambda s: (0, s)))],
+        into=(p.tails,))
 
 def mlp(core, mixed, tokens, cot, w_out, gain, w_gate_up, w_down, count, tile=256, chunk=1024):
     toks, width = mixed.shape
@@ -652,20 +669,21 @@
     for ref, count in zip(parts, counts):
         @pl.when((step >= begin) & (step < begin + count))
         def _(ref=ref):
-            keep[...], send[...] = parted(nn(normed_t[...], ref[...]), first, each)
+            columns = ref.shape[1]
+            keep[:, :columns], send[:, :columns] = parted(nn(normed_t[...], ref[...]), first, each)
         begin += count
 
 def weight_grad(core, normed_t, parts, count, name, deps=()):
     width, toks = normed_t.shape
-    counts = [p.shape[1] // 256 for p in parts]
+    counts = [max(p.shape[1] // 512, 1) for p in parts]
     begins = [sum(counts[:n]) for n in range(len(counts))]
-    def spec(begin, size):
-        return pl.BlockSpec((toks, 256), lambda s: (0, jnp.clip(s - begin, 0, size - 1)))
+    def spec(part, begin, size):
+        return pl.BlockSpec((toks, min(part.shape[1], 512)), lambda s: (0, jnp.clip(s - begin, 0, size - 1)))
     half = width // 2
-    out = ((half, 256 * sum(counts)), BF, pl.BlockSpec((half, 256), lambda s: (0, s)))
+    out = ((half, 512 * sum(counts)), BF, pl.BlockSpec((half, 512), lambda s: (0, s)))
     return call(functools.partial(weight_kernel, counts=counts, each=width // count), name, (sum(counts),),
-        [(core, SMEM), (normed_t, resident((width, toks)))] + [(p, spec(b, n)) for p, b, n in zip(parts, begins, counts)],
-        [out, out], flops=2 * width * toks * 256 * sum(counts), deps=deps)
+        [(core, SMEM), (normed_t, resident((width, toks)))] + [(p, spec(p, b, n)) for p, b, n in zip(parts, begins, counts)],
+        [out, out], deps=deps)
 
 def input_kernel(dq_lin, dk_lin, dq_win, dk_win, dv, w, tokens, gain, resid, out):
     begin, grad = 0, None
@@ -735,7 +753,7 @@
         if self.bit == 0:
             self.total, *self.through = self._call(functools.partial(begun_kernel, backward=self.backward), "begun", [self.core], [self.mine, self.received[0]], 1, through)
         elif self.bit < self.last:
-            self.total, = self._call(joined_kernel, "joined", [self.ahead[self.bit - 1:self.bit]], [self.total, self.received[-1]], 1)
+            self.total, *self.through = self._call(joined_kernel, "joined", [self.ahead[self.bit - 1:self.bit]], [self.total, self.received[-1]], 1, through)
         else:
             self.kept, self.total = self._call(functools.partial(ended_kernel, backward=self.backward), "ended", [self.core, self.ahead], [self.mine] + self.received, 2)
         self.bit += 1
@@ -800,6 +818,9 @@
         self.me, self.count, self.chips = me, count, count // 2
         self.pairs = [(chips_first(k, self.chips), chips_first(swap(s, 0, count), self.chips)) for k, s in pairs]
         self.bit = 0
+    def start(self, sends):
+        self.a.append(swap(sends[0], 1, self.count))
+        self.b.append(swap(sends[1], 2, self.count))
     def step(self, deps=()):
         me, chips = self.me, self.chips
         bits = self.count.bit_length() - 1
@@ -810,7 +831,7 @@
             pieces = [Piece(g), half(d, 0), half(o, 0)], [Piece(u), half(d, 1), half(o, 1)]
             self.layout = [(p.rows, p.size) for ps in pieces for p in ps]
             (ka, sa), (kb, sb) = add_up([(pieces[0], chips // 2, 1, (me >> 1) & 1), (pieces[1], chips // 4, 2, (me >> 2) & 1)], 2, "sum_first", deps=deps)
-            self.a, self.b = [ka, swap(sa, 1, self.count)], [kb, swap(sb, 2, self.count)]
+            self.a, self.b, self.sends = [ka], [kb], (sa, sb)
         elif self.bit == 2:
             (ka, sa), (kb, sb) = add_up([([Piece(self.a)], chips // 4, 1, (me >> 2) & 1), ([Piece(self.b)], chips // 4, 1, (me >> 1) & 1)], 2, "sum_second")
             self.a, self.b = [ka, swap(sa, 2, self.count)], [kb, swap(sb, 1, self.count)]
@@ -856,7 +877,7 @@
     got = swap(lax.dynamic_slice_in_dim(rows, (1 - core) * each, each, 0), 0, count)
     return jnp.concatenate([jnp.where(core == 0, own, got), jnp.where(core == 0, got, own)], axis=1)
 
-def gathered_kernel(place, weights, gain, *refs, layout, rows):
+def gathered_kernel(place, weights, *refs, layout, rows):
     arrays, (out, gain_out) = refs[:-2], refs[-2:]
     total = None
     for n, at in enumerate(layout):
@@ -867,19 +888,18 @@
         out[:, n * 256:(n + 1) * 256] = g
         t = g * weights[:, n * 256:(n + 1) * 256].astype(F32)
         total = t if total is None else total + t
-    gain_out[...] = jnp.sum(total, axis=1, keepdims=True) / gain[...]
+    gain_out[...] = jnp.sum(total, axis=1, keepdims=True)
 
 def gathered(arrays, layout, weights, gain, me, count):
     each, columns = weights.shape[0] // count, weights.shape[1]
+    own_gain = lax.dynamic_slice_in_dim(gain, me * each, each, 0)
     if each < 16:
-        weights, gain = lax.dynamic_slice_in_dim(weights, me * each, each, 0), lax.dynamic_slice_in_dim(gain, me * each, each, 0)
-        me = jnp.zeros((), jnp.int32)
+        weights, me = lax.dynamic_slice_in_dim(weights, me * each, each, 0), jnp.zeros((), jnp.int32)
     mine = pl.BlockSpec((each, columns), lambda s, place: (place[0], 0))
-    one = pl.BlockSpec((each, 1), lambda s, place: (place[0], 0))
     out, gain_out = call(functools.partial(gathered_kernel, layout=layout, rows=each), "gathered", (1,),
-        [(weights, mine), (gain.reshape(-1, 1), one)] + [(a, resident(a.shape)) for a in arrays],
-        [((each, columns), F32, resident((each, columns))), ((each, 1), F32, resident((each, 1)))], flops=10, moved=MIB, scalars=[me.reshape(1)])
-    return out, gain_out.reshape(each)
+        [(weights, mine)] + [(a, resident(a.shape)) for a in arrays],
+        [((each, columns), F32, resident((each, columns))), ((each, 1), F32, resident((each, 1)))], scalars=[me.reshape(1)])
+    return out, gain_out.reshape(each) / own_gain
 
 def plain_kernel(*refs, pieces, shapes):
     arrays, outs = refs[:-len(shapes)], refs[-len(shapes):]
@@ -912,20 +932,20 @@
     x = tokens.reshape(total, width)
     cot = cotangent.reshape(total, width)
     p = Projected()
-    project_keys(p, x, gain_in, w_in)
+    project_keys(p, x, gain_in, w_in, rows)
     scan = Scan(*local_states(core, low, high, p.k_lin, p.v, rows, length), me, count, False)
-    project_rest(p, w_in)
-    tails = lambda a, at: a.reshape(rows, length, -1)[:, -WINDOW:, at:at + width]
+    project_queries(p, w_in)
+    scan.step()
+    project_rest(p, w_in, rows)
     forward = [(i, i + 1) for i in range(count - 1)]
     backward = [(i + 1, i) for i in range(count - 1)]
-    halo = lax.ppermute(jnp.stack([tails(p.qk_win, width), tails(p.v, 0)]), "seq", forward).reshape(2, rows * WINDOW, width)
+    halo = lax.ppermute(p.tails, "seq", forward)
     scan.step()
     local = intra(low, high, p, rows, length, 0)
     scan.step()
     local, = intra(low, high, p, rows, length, 1, into=local)
     scan.step()
     windowed = window(low, high, p, halo, rows, length, 0)
-    scan.step()
     windowed, = window(low, high, p, halo, rows, length, 1, into=windowed)
     while scan.bit < bits:
         scan.step()
@@ -937,13 +957,14 @@
     grad_numer, *grad_state_in = numer_back(core, low, p, numer, grad_mixed, rows, length)
     scan = Scan(*grad_state_in, me, count, True)
 
-    scan.step(through=(send_g, send_u, send_d, send_o))
-    mlp_sum = MlpSum(list(zip((keep_g, keep_u, keep_d, keep_o), scan.through)), me, count)
+    mlp_sum = MlpSum([(keep_g, send_g), (keep_u, send_u), (keep_d, send_d), (keep_o, send_o)], me, count)
+    scan.step()
+    mlp_sum.step()
+    scan.step(through=mlp_sum.sends)
+    mlp_sum.start(scan.through)
     back, dh, kept = window_back_first(low, high, p, halo, grad_mixed, rows, length)
+    scan.step()
     returned = lax.ppermute(dh, "seq", backward)
-    scan.step()
-    mlp_sum.step(deps=(returned,))
-    scan.step()
     dq_win, dk_win, dv_win = window_back_second(low, high, p, grad_mixed, back, kept, rows, length)
     scan.step()
     inner = intra_back(core, low, high, p, grad_numer, dv_win, state_in, rows, length, 0)
@@ -961,20 +982,19 @@
     late = in_sum.first(*weight_grad(core, p.normed_t, [dv, dk_lin], count, "weight_grad_late"), (((0, width // 2),), ((width // 2, width // 2), (width, lin))))
     parts = [dq_lin, dk_lin, dq_win, dk_win, dv]
     early = in_sum.second(*early)
-    grad_tokens = input_grad(parts, w_in, x, gain_in, grad_resid, 0, 4, "input_grad_first")
+    grad_tokens = input_grad(parts, w_in, x, gain_in, grad_resid, 0, 2, "input_grad_first")
     late = in_sum.second(*late)
     while mlp_sum.bit < bits - 1:
         mlp_sum.step()
-    grad_tokens = input_grad(parts, w_in, x, gain_in, grad_resid, 1, 4, "input_grad", into=grad_tokens)
     in_sum.third(early, late)
     grad_tokens, = input_grad(parts, w_in, x, gain_in, grad_resid, 1, 2, "input_grad", into=grad_tokens)
+    in_got = in_sum.rest()
     ff, each, chip = w_down.shape[0], width // count, w_down.shape[0] // (count // 2)
     pad = padded(each)
     height = ff // 256 * pad
     second = height + padded(chip) + 2 * pad
     part_gate_up, part_gain_mlp = gathered(mlp_sum.all, [n * pad for n in range(ff // 256)] + [second + n * pad for n in range(ff // 256)],
         w_gate_up, gain_mlp, me, count)
-    in_got = in_sum.rest()
     down, part_out = plain(mlp_sum.all, [(0, height, chip, 0), (0, second + height, chip, 256)]
         + [(1, height + padded(chip) + n * pad + (second - 2 * pad if n >= 2 else 0), each, n * 256) for n in range(4)],
         [(chip, width // 2), (each, width)])

time: 448 us -> 430 us (0.960)
  starting transfers between devices: 46.2 us -> 39 us
  Pallas kernels: 326 us -> 320 us
  local copies, waits for them, and re-layouts: 10.4 us -> 4.99 us
    ppermute x31, starting transfers between devices: 37.5 us -> 30.2 us  [swap(): return lax.ppermute(x, 'seq', [(i, i ^ 1 << bit) for i in range(count)])]
    pallas_call x42, Pallas kernels: 326 us -> 320 us  [call(): pl.pallas_call(body, grid_spec=pltpu.PrefetchScalarGridSpec(num_scalar_pr...]
  transfers between devices with their start and end apart: 36 -> 36, of which waited for: 15 -> 13; matrix products, arithmetic and copies ran while one was open for 2% -> 1% of each run, Pallas kernels for 45% -> 48%
where the time goes in v1:
time: 430 us; the launch traced here: 424 us
  Pallas kernels  320 us (74%)
  waiting for transfers between devices  52 us (12%)
  starting transfers between devices  39 us (9%)
  other arithmetic  6.5 us (2%)
  local copies, waits for them, and re-layouts  4.99 us (1%)
    pallas_call x42, Pallas kernels, call(): pl.pallas_call(body, grid_spec=pltpu.PrefetchScalarGridSpec(num_scalar_pr...  320 us
    ppermute x31, waiting for transfers between devices, swap(): return lax.ppermute(x, 'seq', [(i, i ^ 1 << bit) for i in range(count)])  38.2 us
    ppermute x31, starting transfers between devices, swap(): return lax.ppermute(x, 'seq', [(i, i ^ 1 << bit) for i in range(count)])  30.2 us
    ppermute x3, waiting for transfers between devices, quarters(): lax.ppermute(x, 'seq', [(i, i ^ k << bit) for i in range(count)])  13.8 us
  transfers between devices with their start and end apart: 36, of which 13 were waited for; matrix products, arithmetic and copies ran while one was open for 1% of the time, Pallas kernels for 48%

profile of v1, /device:TPU:0, one launch (start us, length us, event | category | flops | bytes accessed | tf_op | source)
XLA Modules:
  0.0 424.0 jit_solution(2008917922537461471)
XLA Ops:
  2.9 6.7 %project_keys.1 = (bf16[1024,1024]{1,0:T(8,128)(2,1)}, bf16[1024,256]{1,0:T(8,128)(2,1)}, bf16[1024,1024]{1,0:T(8,128)(2,1)}, bf16[2,128,1024]{2,1,0:T(8,128)(2,1)}) custom-call(bf16[1024,1024]{1,0:T(8,128)(2,1)} %bitcast.97, f32[1,1024]{1,0:T(1,128)} %bitcast.112, bf16[1024,3584]{1,0:T(8,128)(2,1)} %refs_1_.5, bf16[1024,3584]{1,0:T(8,128)(2,1)} %refs_1_.5), custom_call_target="tpu_custom_call" | custom-call | flops 6800000000 | bytes 1000 | tf_op jit(solution)/shard_map/project_keys/pallas_call | solution.py:144
  9.6 8.0 %state.1 = (f32[4,160,256]{2,1,0:T(8,128)}, bf16[4,160,256]{2,1,0:T(8,128)(2,1)}) custom-call(s32[1]{0:T(128)} %bitcast.refs_0_, s32[16]{0:T(128)} %copy-done.2, s32[16]{0:T(128)} %add.25.refs_2_.refs_1_, bf16[1024,256]{1,0:T(8,128)(2,1)} %get-tuple-element.97.refs_3_.refs_4_, bf16[1024,1024]{1,0:T(8,128)(2,1)} %get-tuple-element.98.refs_4_.refs_10_.refs_5_, ...), custom_call_target="tpu_custom_call" | custom-call | flops 7400000000 | bytes 1000 | tf_op jit(solution)/shard_map/state/pallas_call | solution.py:144
  19.2 3.2 project_queries.1.refs_3_.refs_2_
  22.4 2.0 begun.2.refs_3_.refs_1_
  24.4 2.5 collective-permute-start.1
  26.9 9.5 %project_rest.1 = (bf16[2,128,1024]{2,1,0:T(8,128)(2,1)}, bf16[1024,2048]{1,0:T(8,128)(2,1)}, bf16[1024,1024]{1,0:T(8,128)(2,1)}) custom-call(bf16[1024,1024]{1,0:T(8,128)(2,1)} %get-tuple-element.96.refs_5_.refs_0_.refs_1_, bf16[1024,1024]{1,0:T(8,128)(2,1)} %get-tuple-element.96.refs_5_.refs_0_.refs_1_, ...), custom_call_target="tpu_custom_call", output_to_operand_aliasing={{0}: (4, {})} | custom-call | flops 10000000000 | bytes 1000 | tf_op jit(solution)/shard_map/project_rest/pallas_call | solution.py:144
  36.4 3.1 collective-permute-start.5
  39.5 2.6 joined.6.refs_5_.refs_1_
  42.8 6.3 %intra.2.refs_3_.refs_6_ = bf16[1024,1024]{1,0:T(8,128)(2,1)} custom-call(s32[16]{0:T(128)} %copy-done.2, s32[16]{0:T(128)} %add.25.refs_2_.refs_1_, bf16[1024,256]{1,0:T(8,128)(2,1)} %project_queries.1.refs_3_.refs_2_, bf16[1024,256]{1,0:T(8,128)(2,1)} %get-tuple-element.97.refs_3_.refs_4_, bf16[1024,1024]{1,0:T(8,128)(2,1)} %get-tuple-element.98.refs_4_.refs_10_.refs_5_, ...), custom_call_target="tpu_custom_call" | custom-call | flops 7200000000 | bytes 1000 | tf_op jit(solution)/shard_map/intra/pallas_call | solution.py:144
  49.1 5.1 %collective-permute-done.2.refs_2_.refs_5_ = bf16[4,160,256]{2,1,0:T(8,128)(2,1)} collective-permute-done((bf16[4,160,256]{2,1,0:T(8,128)(2,1)}, bf16[4,160,256]{2,1,0:T(8,128)(2,1)}, u32[]{:S(2)}, u32[]{:S(2)}) %collective-permute-start.2) | collective-permute-done | bytes 327712 | tf_op jit(solution)/shard_map/ppermute | solution.py:709
  54.2 2.5 joined.7.refs_5_.refs_1_
  56.7 3.4 collective-permute-start.3
  60.1 6.3 %intra.3.refs_3_.refs_5_ = bf16[1024,1024]{1,0:T(8,128)(2,1)} custom-call(s32[16]{0:T(128)} %copy-done.2, s32[16]{0:T(128)} %add.25.refs_2_.refs_1_, bf16[1024,256]{1,0:T(8,128)(2,1)} %project_queries.1.refs_3_.refs_2_, bf16[1024,256]{1,0:T(8,128)(2,1)} %get-tuple-element.97.refs_3_.refs_4_, ...), custom_call_target="tpu_custom_call", output_to_operand_aliasing={{}: (6, {})} | custom-call | flops 7200000000 | bytes 1000 | tf_op jit(solution)/shard_map/intra/pallas_call | solution.py:144
  66.4 2.0 collective-permute-done.3.refs_2_.refs_6_
  68.4 2.6 joined.8.refs_7_
  71.0 2.8 collective-permute-start.4
  73.8 6.4 %window.2.refs_7_ = bf16[1024,1024]{1,0:T(8,128)(2,1)} custom-call(s32[16]{0:T(128)} %copy-done.2, s32[16]{0:T(128)} %add.25.refs_2_.refs_1_, bf16[1024,2048]{1,0:T(8,128)(2,1)} %get-tuple-element.103.refs_2_.refs_3_.refs_8_.refs_9_, bf16[1024,2048]{1,0:T(8,128)(2,1)} %get-tuple-element.103.refs_2_.refs_3_.refs_8_.refs_9_, ...), custom_call_target="tpu_custom_call" | custom-call | flops 8499999744 | bytes 1000 | tf_op jit(solution)/shard_map/window/pallas_call | solution.py:144
  80.1 6.4 %window.3.refs_8_.refs_6_ = bf16[1024,1024]{1,0:T(8,128)(2,1)} custom-call(s32[16]{0:T(128)} %copy-done.2, s32[16]{0:T(128)} %add.25.refs_2_.refs_1_, bf16[1024,2048]{1,0:T(8,128)(2,1)} %get-tuple-element.103.refs_2_.refs_3_.refs_8_.refs_9_, bf16[1024,2048]{1,0:T(8,128)(2,1)} %get-tuple-element.103.refs_2_.refs_3_.refs_8_.refs_9_, ...), custom_call_target="tpu_custom_call", output_to_operand_aliasing={{}: (7, {})} | custom-call | flops 8499999744 | bytes 1000 | tf_op jit(solution)/shard_map/window/pallas_call | solution.py:144
  86.5 1.9 collective-permute-done.4.refs_7_
  88.4 2.9 ended.2
  91.3 2.0 collective-permute-done.6.refs_4_.refs_9_
  93.2 8.4 %mix.1 = (bf16[1024,1024]{1,0:T(8,128)(2,1)}, bf16[1024,1024]{1,0:T(8,128)(2,1)}) custom-call(s32[1]{0:T(128)} %bitcast.refs_0_, s32[16]{0:T(128)} %copy-done.2, bf16[1024,256]{1,0:T(8,128)(2,1)} %project_queries.1.refs_3_.refs_2_, bf16[4,160,256]{2,1,0:T(8,128)(2,1)} %get-tuple-element.104.refs_3_.refs_8_, ...), custom_call_target="tpu_custom_call" | custom-call | flops 10000000000 | bytes 1000 | tf_op jit(solution)/shard_map/mix/pallas_call | solution.py:144
  101.6 74.9 %mlp.1 = (bf16[1024,1024]{1,0:T(8,128)(2,1)}, f32[1024,1024]{1,0:T(8,128)}, bf16[1024,1024]{1,0:T(8,128)(2,1)}, bf16[512,2816]{1,0:T(8,128)(2,1)}, bf16[512,2816...) custom-call(s32[1]{0:T(128)} %bitcast.refs_0_, ...), custom_call_target="tpu_custom_call" | custom-call | flops 88000004096 | bytes 1000 | tf_op jit(solution)/shard_map/mlp/pallas_call | solution.py:144
  177.7 13.2 %numer_back.1 = (bf16[1024,1024]{1,0:T(8,128)(2,1)}, f32[4,160,256]{2,1,0:T(8,128)}, bf16[4,160,256]{2,1,0:T(8,128)(2,1)}) custom-call(s32[1]{0:T(128)} %bitcast.refs_0_, s32[16]{0:T(128)} %copy-done.2, bf16[1024,256]{1,0:T(8,128)(2,1)} %project_queries.1.refs_3_.refs_2_, bf16[1024,1024]{1,0:T(8,128)(2,1)} %get-tuple-element.107.refs_9_.refs_3_, ...), custom_call_target="tpu_custom_call" | custom-call | flops 12000000000 | bytes 1000 | tf_op jit(solution)/shard_map/numer_back/pallas_call | solution.py:144
  192.9 2.0 begun.3.refs_26_.refs_1_
  194.9 10.6 %sum_first.1 = (bf16[8,1,592,256]{3,2,1,0:T(8,128)(2,1)}, bf16[8,1,592,256]{3,2,1,0:T(8,128)(2,1)}, bf16[4,2,592,256]{3,2,1,0:T(8,128)(2,1)}, bf16[4,2,592,256]{3,2,1,0:T(8,128)(2,1)}) custom-call(s32[1]{0:T(128)} %bitcast.6.refs_0_.refs_1_, s32[1]{0:T(128)} %bitcast.7.refs_1_.refs_0_, bf16[8,2,1,32,2816]{4,3,2,1,0:T(8,128)(2,1)} %bitcast.93, ...), custom_call_target="tpu_custom_call" | custom-call | flops 10599999488 | bytes 1000 | tf_op jit(solution)/shard_map/sum_first/pallas_call | solution.py:144
  205.5 2.6 joined.9
  208.6 2.0 collective-permute-start.18
  210.6 1.6 collective-permute-start.19
  212.1 11.5 %window_back.2 = (bf16[1024,1024]{1,0:T(8,128)(2,1)}, bf16[1024,1024]{1,0:T(8,128)(2,1)}, bf16[1024,1024]{1,0:T(8,128)(2,1)}, bf16[2,128,1024]{2,1,0:T(8,128)(2,...) custom-call(s32[16]{0:T(128)} %copy-done.2, s32[16]{0:T(128)} %add.25.refs_2_.refs_1_, ...), custom_call_target="tpu_custom_call" | custom-call | flops 12999999488 | bytes 1000 | tf_op jit(solution)/shard_map/window_back/pallas_call | solution.py:144
  223.6 1.3 collective-permute-start.16
  224.9 2.5 joined.10.refs_9_.refs_1_
  228.6 11.4 %window_back.3 = (bf16[1024,1024]{1,0:T(8,128)(2,1)}, bf16[1024,1024]{1,0:T(8,128)(2,1)}, bf16[1024,1024]{1,0:T(8,128)(2,1)}) custom-call(s32[16]{0:T(128)} %copy-done.2, s32[16]{0:T(128)} %add.25.refs_2_.refs_1_, ...), custom_call_target="tpu_custom_call", output_to_operand_aliasing={{0}: (10, {}), {1}: (11, {}), {2}: (12, {})} | custom-call | flops 12999999488 | bytes 1000 | tf_op jit(solution)/shard_map/window_back/pallas_call | solution.py:144
  240.6 2.6 joined.11.refs_10_
  243.2 3.4 collective-permute-start.15
  246.6 13.7 %intra_back.2 = (bf16[1024,256]{1,0:T(8,128)(2,1)}, f32[2,256,512]{2,1,0:T(8,128)}, bf16[1024,1024]{1,0:T(8,128)(2,1)}) custom-call(s32[1]{0:T(128)} %bitcast.refs_0_, s32[16]{0:T(128)} %copy-done.2, s32[16]{0:T(128)} %add.25.refs_2_.refs_1_, bf16[1024,256]{1,0:T(8,128)(2,1)} %project_queries.1.refs_3_.refs_2_, ...), custom_call_target="tpu_custom_call" | custom-call | flops 14000000000 | bytes 1000 | tf_op jit(solution)/shard_map/intra_back/pallas_call | solution.py:144
  261.4 2.9 ended.3
  264.2 13.9 %intra_back.3 = (bf16[1024,256]{1,0:T(8,128)(2,1)}, f32[2,256,512]{2,1,0:T(8,128)}, bf16[1024,1024]{1,0:T(8,128)(2,1)}) custom-call(s32[1]{0:T(128)} %bitcast.refs_0_, s32[16]{0:T(128)} %copy-done.2, s32[16]{0:T(128)} %add.25.refs_2_.refs_1_, ...), custom_call_target="tpu_custom_call", output_to_operand_aliasing={{0}: (11, {}), {1}: (12, {}), {2}: (13, {})} | custom-call | flops 14000000000 | bytes 1000 | tf_op jit(solution)/shard_map/intra_back/pallas_call | solution.py:144
  278.1 6.5 %sum_second.1 = (bf16[4,1,592,256]{3,2,1,0:T(8,128)(2,1)}, bf16[4,1,592,256]{3,2,1,0:T(8,128)(2,1)}, bf16[4,1,592,256]{3,2,1,0:T(8,128)(2,1)}, bf16[4,1,592,256]{3,2,1,0:T(8,128)(2,1)}) custom-call(s32[1]{0:T(128)} %bitcast.7.refs_1_.refs_0_, s32[1]{0:T(128)} %bitcast.6.refs_0_.refs_1_, bf16[4,2,1,592,256]{4,3,2,1,0:T(8,128)(2,1)} %bitcast.116, ...), custom_call_target="tpu_custom_call" | custom-call | flops 6400000000 | bytes 1000 | tf_op jit(solution)/shard_map/sum_second/pallas_call | solution.py:144
  285.9 1.8 tail.1.refs_3_
  287.7 9.6 %weight_grad_early.1 = (bf16[512,2560]{1,0:T(8,128)(2,1)}, bf16[512,2560]{1,0:T(8,128)(2,1)}) custom-call(s32[1]{0:T(128)} %bitcast.refs_0_, bf16[1024,1024]{1,0:T(8,128)(2,1)} %get-tuple-element.142.refs_1_, bf16[1024,1024]{1,0:T(8,128)(2,1)} %get-tuple-element.132.refs_3_.refs_2_, bf16[1024,1024]{1,0:T(8,128)(2,1)} %tail.1.refs_3_, ...), custom_call_target="tpu_custom_call" | custom-call | flops 100000000 | bytes 1000 | tf_op jit(solution)/shard_map/weight_grad_early/pallas_call | solution.py:144
  297.3 10.8 %state_back.1 = (bf16[1024,256]{1,0:T(8,128)(2,1)}, bf16[1024,1024]{1,0:T(8,128)(2,1)}) custom-call(s32[1]{0:T(128)} %bitcast.refs_0_, s32[16]{0:T(128)} %copy-done.2, s32[16]{0:T(128)} %add.25.refs_2_.refs_1_, bf16[1024,256]{1,0:T(8,128)(2,1)} %get-tuple-element.97.refs_3_.refs_4_, bf16[1024,1024]{1,0:T(8,128)(2,1)} %get-tuple-element.98.refs_4_.refs_10_.refs_5_, ...), custom_call_target="tpu_custom_call" | custom-call | flops 100000000 | bytes 1000 | tf_op jit(solution)/shard_map/state_back/pallas_call | solution.py:144
  308.1 5.9 %collective-permute-done.21 = bf16[4,592,256]{2,1,0:T(8,128)(2,1)} collective-permute-done((bf16[4,592,256]{2,1,0:T(8,128)(2,1)}, bf16[4,592,256]{2,1,0:T(8,128)(2,1)}, u32[]{:S(2)}, u32[]{:S(2)}) %collective-permute-start.21) | collective-permute-done | bytes 1212448 | tf_op jit(solution)/shard_map/ppermute | solution.py:709
  314.4 3.7 sum_more.2
  318.0 6.6 %weight_grad_late.1 = (bf16[512,1536]{1,0:T(8,128)(2,1)}, bf16[512,1536]{1,0:T(8,128)(2,1)}) custom-call(s32[1]{0:T(128)} %bitcast.refs_0_, bf16[1024,1024]{1,0:T(8,128)(2,1)} %get-tuple-element.142.refs_1_, bf16[1024,1024]{1,0:T(8,128)(2,1)} %get-tuple-element.150.refs_2_.refs_4_, bf16[1024,256]{1,0:T(8,128)(2,1)} %get-tuple-element.149.refs_9_.refs_3_.refs_1_, ...), custom_call_target="tpu_custom_call" | custom-call | flops 100000000 | bytes 1000 | tf_op jit(solution)/shard_map/weight_grad_late/pallas_call | solution.py:144
  324.7 4.5 %in_first.2 = (bf16[8,1,160,256]{3,2,1,0:T(8,128)(2,1)}, bf16[8,1,160,256]{3,2,1,0:T(8,128)(2,1)}, bf16[4,2,128,256]{3,2,1,0:T(8,128)(2,1)}, bf16[4,2,128,256]{3,2,1,0:T(8,128)(2,1)}) custom-call(s32[1]{0:T(128)} %bitcast.6.refs_0_.refs_1_, s32[1]{0:T(128)} %bitcast.7.refs_1_.refs_0_, bf16[8,2,1,32,2560]{4,3,2,1,0:T(8,128)(2,1)} %bitcast.72, ...), custom_call_target="tpu_custom_call" | custom-call | flops 3000000000 | bytes 1000 | tf_op jit(solution)/shard_map/in_first/pallas_call | solution.py:144
  331.1 10.7 %input_grad_first.1.refs_14_.refs_10_ = f32[1024,1024]{1,0:T(8,128)} custom-call(bf16[1024,256]{1,0:T(8,128)(2,1)} %get-tuple-element.137.refs_10_.refs_4_.refs_0_, bf16[1024,256]{1,0:T(8,128)(2,1)} %get-tuple-element.149.refs_9_.refs_3_.refs_1_, bf16[1024,1024]{1,0:T(8,128)(2,1)} %get-tuple-element.132.refs_3_.refs_2_, bf16[1024,1024]{1,0:T(8,128)(2,1)} %tail.1.refs_3_, ...), custom_call_target="tpu_custom_call" | custom-call | flops 100000000 | bytes 1000 | tf_op jit(solution)/shard_map/input_grad_first/pallas_call | solution.py:144
  341.8 3.7 in_first.3
  346.4 1.5 collective-permute-start.25
  347.9 6.2 %collective-permute-done.28 = bf16[2,1184,256]{2,1,0:T(8,128)(2,1)} collective-permute-done((bf16[2,1184,256]{2,1,0:T(8,128)(2,1)}, bf16[2,1184,256]{2,1,0:T(8,128)(2,1)}, u32[]{:S(2)}, u32[]{:S(2)}) %collective-permute-start.28) | collective-permute-done | bytes 1212448 | tf_op jit(solution)/shard_map/ppermute | solution.py:709
  354.1 2.8 sum_more.3
  356.9 4.1 in_second.1
  361.0 1.5 collective-permute-start.29
  363.3 2.7 collective-permute-start.34
  365.9 10.7 %input_grad.1.refs_17_ = f32[1024,1024]{1,0:T(8,128)} custom-call(bf16[1024,256]{1,0:T(8,128)(2,1)} %get-tuple-element.137.refs_10_.refs_4_.refs_0_, bf16[1024,256]{1,0:T(8,128)(2,1)} %get-tuple-element.149.refs_9_.refs_3_.refs_1_, bf16[1024,1024]{1,0:T(8,128)(2,1)} %get-tuple-element.132.refs_3_.refs_2_, ...), custom_call_target="tpu_custom_call", output_to_operand_aliasing={{}: (10, {})} | custom-call | flops 100000000 | bytes 1000 | tf_op jit(solution)/shard_map/input_grad/pallas_call | solution.py:144
  376.6 2.6 quarters.1
  379.3 12.4 %collective-permute-done.34.refs_3_.refs_1_ = bf16[1,1184,256]{2,1,0:T(8,128)(2,1)} collective-permute-done((bf16[1,1184,256]{2,1,0:T(8,128)(2,1)}, bf16[1,1184,256]{2,1,0:T(8,128)(2,1)}, u32[]{:S(2)}, u32[]{:S(2)}) %collective-permute-start.34) | collective-permute-done | bytes 606240 | tf_op jit(solution)/shard_map/ppermute | solution.py:709
  391.7 2.4 gathered.2
  394.0 2.1 plain.1
  397.1 2.4 collective-permute-start.31
  399.6 2.0 collective-permute-start.33
  405.4 2.4 collective-permute-done.31.refs_3_
  407.9 11.3 %collective-permute-done.32.refs_4_ = bf16[1,448,256]{2,1,0:T(8,128)(2,1)} collective-permute-done((bf16[1,448,256]{2,1,0:T(8,128)(2,1)}, bf16[1,448,256]{2,1,0:T(8,128)(2,1)}, u32[]{:S(2)}, u32[]{:S(2)}) %collective-permute-start.32) | collective-permute-done | bytes 229408 | tf_op jit(solution)/shard_map/ppermute | solution.py:844
  419.2 2.3 gathered.3
  (73 shorter events, 23.2 us)
Async XLA Ops:
  1.5 0.9 copy-start.2
  17.6 4.8 %collective-permute-start = (bf16[4,160,256]{2,1,0:T(8,128)(2,1)}, bf16[4,160,256]{2,1,0:T(8,128)(2,1)}, u32[]{:S(2)}, u32[]{:S(2)}) collective-permute-start(bf16[4,160,256]{2,1,0:T(8,128)(2,1)} %get-tuple-element.100), channel_id=1, source_target_pairs={{0,1},{1,0},{2,3},{3,2},{4,5},{5,4},{6,7},{7,6},{8,9},{9,8},{10,11... | collective-permute-start | bytes 983048 | tf_op jit(solution)/shard_map/ppermute | solution.py:709
  18.0 0.5 copy-start.1
  24.4 15.1 %collective-permute-start.1 = (bf16[4,160,256]{2,1,0:T(8,128)(2,1)}, bf16[4,160,256]{2,1,0:T(8,128)(2,1)}, u32[]{:S(2)}, u32[]{:S(2)}) collective-permute-start(bf16[4,160,256]{2,1,0:T(8,128)(2,1)} %begun.2.refs_3_.refs_1_), channel_id=1, source_target_pairs={{0,2},{1,3},{2,0},{3,1},{4,6},{5,7},{6,4},{7,5},{8,10},{9,11},{10,... | collective-permute-start | bytes 983048 | tf_op jit(solution)/shard_map/ppermute | solution.py:709
  36.4 37.3 %collective-permute-start.5 = (bf16[2,128,1024]{2,1,0:T(8,128)(2,1)}, bf16[2,128,1024]{2,1,0:T(8,128)(2,1)}, u32[]{:S(2)}, u32[]{:S(2)}) collective-permute-start(bf16[2,128,1024]{2,1,0:T(8,128)(2,1)} %get-tuple-element.102.refs_3_), channel_id=1, source_target_pairs={{0,1},{1,2},{2,3},{3,4},{4,5},{5,6},{6,7},{7,8},{8,9},{9,10},{10,1... | collective-permute-start | bytes 1572872 | tf_op jit(solution)/shard_map/ppermute | solution.py:942
  42.1 12.1 %collective-permute-start.2 = (bf16[4,160,256]{2,1,0:T(8,128)(2,1)}, bf16[4,160,256]{2,1,0:T(8,128)(2,1)}, u32[]{:S(2)}, u32[]{:S(2)}) collective-permute-start(bf16[4,160,256]{2,1,0:T(8,128)(2,1)} %joined.6.refs_5_.refs_1_), channel_id=1, source_target_pairs={{0,4},{1,5},{2,6},{3,7},{4,0},{5,1},{6,2},{7,3},{8,12},{9,13},{10,... | collective-permute-start | bytes 983048 | tf_op jit(solution)/shard_map/ppermute | solution.py:709
  56.7 11.7 %collective-permute-start.3 = (bf16[4,160,256]{2,1,0:T(8,128)(2,1)}, bf16[4,160,256]{2,1,0:T(8,128)(2,1)}, u32[]{:S(2)}, u32[]{:S(2)}) collective-permute-start(bf16[4,160,256]{2,1,0:T(8,128)(2,1)} %joined.7.refs_5_.refs_1_), channel_id=1, source_target_pairs={{0,8},{1,9},{2,10},{3,11},{4,12},{5,13},{6,14},{7,15},{8,0},{9,1},... | collective-permute-start | bytes 983048 | tf_op jit(solution)/shard_map/ppermute | solution.py:709
  71.0 17.4 %collective-permute-start.4 = (bf16[4,160,256]{2,1,0:T(8,128)(2,1)}, bf16[4,160,256]{2,1,0:T(8,128)(2,1)}, u32[]{:S(2)}, u32[]{:S(2)}) collective-permute-start(bf16[4,160,256]{2,1,0:T(8,128)(2,1)} %joined.8.refs_7_), channel_id=1, source_target_pairs={{0,16},{1,17},{2,18},{3,19},{4,20},{5,21},{6,22},{7,23},{8,24},{9,... | collective-permute-start | bytes 983048 | tf_op jit(solution)/shard_map/ppermute | solution.py:709
  91.3 2.0 collective-permute-start.6
  176.6 18.3 %collective-permute-start.10 = (bf16[2816,512]{1,0:T(8,128)(2,1)}, bf16[2816,512]{1,0:T(8,128)(2,1)}, u32[]{:S(2)}, u32[]{:S(2)}) collective-permute-start(bf16[2816,512]{1,0:T(8,128)(2,1)} %get-tuple-element.116), channel_id=1, source_target_pairs={{0,1},{1,0},{2,3},{3,2},{4,5},{5,4},{6,7},{7,6},{8,9},{9,8},{10,11... | collective-permute-start | bytes 8650760 | tf_op jit(solution)/shard_map/ppermute | solution.py:709
  176.8 18.1 %collective-permute-start.12 = (bf16[512,2816]{1,0:T(8,128)(2,1)}, bf16[512,2816]{1,0:T(8,128)(2,1)}, u32[]{:S(2)}, u32[]{:S(2)}) collective-permute-start(bf16[512,2816]{1,0:T(8,128)(2,1)} %get-tuple-element.120), channel_id=1, source_target_pairs={{0,1},{1,0},{2,3},{3,2},{4,5},{5,4},{6,7},{7,6},{8,9},{9,8},{10,11... | collective-permute-start | bytes 8650760 | tf_op jit(solution)/shard_map/ppermute | solution.py:709
  177.1 17.8 %collective-permute-start.9 = (bf16[512,2816]{1,0:T(8,128)(2,1)}, bf16[512,2816]{1,0:T(8,128)(2,1)}, u32[]{:S(2)}, u32[]{:S(2)}) collective-permute-start(bf16[512,2816]{1,0:T(8,128)(2,1)} %get-tuple-element.114), channel_id=1, source_target_pairs={{0,1},{1,0},{2,3},{3,2},{4,5},{5,4},{6,7},{7,6},{8,9},{9,8},{10,11... | collective-permute-start | bytes 8650760 | tf_op jit(solution)/shard_map/ppermute | solution.py:709
  177.3 17.6 %collective-permute-start.11 = (bf16[512,1024]{1,0:T(8,128)(2,1)}, bf16[512,1024]{1,0:T(8,128)(2,1)}, u32[]{:S(2)}, u32[]{:S(2)}) collective-permute-start(bf16[512,1024]{1,0:T(8,128)(2,1)} %get-tuple-element.118), channel_id=1, source_target_pairs={{0,1},{1,0},{2,3},{3,2},{4,5},{5,4},{6,7},{7,6},{8,9},{9,8},{10,11... | collective-permute-start | bytes 3145736 | tf_op jit(solution)/shard_map/ppermute | solution.py:709
  190.9 2.0 collective-permute-start.7
  191.0 0.5 copy-start
  194.9 10.6 %collective-permute-start.8 = (bf16[4,160,256]{2,1,0:T(8,128)(2,1)}, bf16[4,160,256]{2,1,0:T(8,128)(2,1)}, u32[]{:S(2)}, u32[]{:S(2)}) collective-permute-start(bf16[4,160,256]{2,1,0:T(8,128)(2,1)} %begun.3.refs_26_.refs_1_), channel_id=1, source_target_pairs={{0,2},{1,3},{2,0},{3,1},{4,6},{5,7},{6,4},{7,5},{8,10},{9,11},{10,... | collective-permute-start | bytes 983048 | tf_op jit(solution)/shard_map/ppermute | solution.py:709
  208.1 16.8 %collective-permute-start.13 = (bf16[4,160,256]{2,1,0:T(8,128)(2,1)}, bf16[4,160,256]{2,1,0:T(8,128)(2,1)}, u32[]{:S(2)}, u32[]{:S(2)}) collective-permute-start(bf16[4,160,256]{2,1,0:T(8,128)(2,1)} %get-tuple-element.124.refs_14_.refs_1_), channel_id=1, source_target_pairs={{0,4},{1,5},{2,6},{3,7},{4,0},{5,1},{6,2},{7,3},{8,12},{9,13},{10,... | collective-permute-start | bytes 983048 | tf_op jit(solution)/shard_map/ppermute | solution.py:709
  208.6 69.6 %collective-permute-start.18 = (bf16[8,592,256]{2,1,0:T(8,128)(2,1)}, bf16[8,592,256]{2,1,0:T(8,128)(2,1)}, u32[]{:S(2)}, u32[]{:S(2)}) collective-permute-start(bf16[8,592,256]{2,1,0:T(8,128)(2,1)} %get-tuple-element.144), channel_id=1, source_target_pairs={{0,2},{1,3},{2,0},{3,1},{4,6},{5,7},{6,4},{7,5},{8,10},{9,11},{10,... | collective-permute-start | bytes 7274504 | tf_op jit(solution)/shard_map/ppermute | solution.py:709
  210.6 67.5 %collective-permute-start.19 = (bf16[8,592,256]{2,1,0:T(8,128)(2,1)}, bf16[8,592,256]{2,1,0:T(8,128)(2,1)}, u32[]{:S(2)}, u32[]{:S(2)}) collective-permute-start(bf16[8,592,256]{2,1,0:T(8,128)(2,1)} %get-tuple-element.146), channel_id=1, source_target_pairs={{0,4},{1,5},{2,6},{3,7},{4,0},{5,1},{6,2},{7,3},{8,12},{9,13},{10,... | collective-permute-start | bytes 7274504 | tf_op jit(solution)/shard_map/ppermute | solution.py:709
  223.6 62.2 %collective-permute-start.16 = (bf16[2,128,1024]{2,1,0:T(8,128)(2,1)}, bf16[2,128,1024]{2,1,0:T(8,128)(2,1)}, u32[]{:S(2)}, u32[]{:S(2)}) collective-permute-start(bf16[2,128,1024]{2,1,0:T(8,128)(2,1)} %get-tuple-element.140), channel_id=1, source_target_pairs={{1,0},{2,1},{3,2},{4,3},{5,4},{6,5},{7,6},{8,7},{9,8},{10,9},{11,1... | collective-permute-start | bytes 1572872 | tf_op jit(solution)/shard_map/ppermute | solution.py:967
  227.4 13.2 %collective-permute-start.14 = (bf16[4,160,256]{2,1,0:T(8,128)(2,1)}, bf16[4,160,256]{2,1,0:T(8,128)(2,1)}, u32[]{:S(2)}, u32[]{:S(2)}) collective-permute-start(bf16[4,160,256]{2,1,0:T(8,128)(2,1)} %joined.10.refs_9_.refs_1_), channel_id=1, source_target_pairs={{0,8},{1,9},{2,10},{3,11},{4,12},{5,13},{6,14},{7,15},{8,0},{9,1},... | collective-permute-start | bytes 983048 | tf_op jit(solution)/shard_map/ppermute | solution.py:709
  243.2 18.2 %collective-permute-start.15 = (bf16[4,160,256]{2,1,0:T(8,128)(2,1)}, bf16[4,160,256]{2,1,0:T(8,128)(2,1)}, u32[]{:S(2)}, u32[]{:S(2)}) collective-permute-start(bf16[4,160,256]{2,1,0:T(8,128)(2,1)} %joined.11.refs_10_), channel_id=1, source_target_pairs={{0,16},{1,17},{2,18},{3,19},{4,20},{5,21},{6,22},{7,23},{8,24},{9,... | collective-permute-start | bytes 983048 | tf_op jit(solution)/shard_map/ppermute | solution.py:709
  264.2 21.6 %collective-permute-start.17 = (bf16[4,160,256]{2,1,0:T(8,128)(2,1)}, bf16[4,160,256]{2,1,0:T(8,128)(2,1)}, u32[]{:S(2)}, u32[]{:S(2)}) collective-permute-start(bf16[4,160,256]{2,1,0:T(8,128)(2,1)} %get-tuple-element.141), channel_id=1, source_target_pairs={{0,1},{1,0},{2,3},{3,2},{4,5},{5,4},{6,7},{7,6},{8,9},{9,8},{10,11... | collective-permute-start | bytes 983048 | tf_op jit(solution)/shard_map/ppermute | solution.py:709
  284.6 29.5 %collective-permute-start.21 = (bf16[4,592,256]{2,1,0:T(8,128)(2,1)}, bf16[4,592,256]{2,1,0:T(8,128)(2,1)}, u32[]{:S(2)}, u32[]{:S(2)}) collective-permute-start(bf16[4,592,256]{2,1,0:T(8,128)(2,1)} %bitcast.125), channel_id=1, source_target_pairs={{0,4},{1,5},{2,6},{3,7},{4,0},{5,1},{6,2},{7,3},{8,12},{9,13},{10,... | collective-permute-start | bytes 3637256 | tf_op jit(solution)/shard_map/ppermute | solution.py:709
  285.3 29.1 %collective-permute-start.22 = (bf16[4,592,256]{2,1,0:T(8,128)(2,1)}, bf16[4,592,256]{2,1,0:T(8,128)(2,1)}, u32[]{:S(2)}, u32[]{:S(2)}) collective-permute-start(bf16[4,592,256]{2,1,0:T(8,128)(2,1)} %bitcast.124), channel_id=1, source_target_pairs={{0,2},{1,3},{2,0},{3,1},{4,6},{5,7},{6,4},{7,5},{8,10},{9,11},{10,... | collective-permute-start | bytes 3637256 | tf_op jit(solution)/shard_map/ppermute | solution.py:709
  297.3 27.5 %collective-permute-start.20 = (bf16[512,2560]{1,0:T(8,128)(2,1)}, bf16[512,2560]{1,0:T(8,128)(2,1)}, u32[]{:S(2)}, u32[]{:S(2)}) collective-permute-start(bf16[512,2560]{1,0:T(8,128)(2,1)} %get-tuple-element.152), channel_id=1, source_target_pairs={{0,1},{1,0},{2,3},{3,2},{4,5},{5,4},{6,7},{7,6},{8,9},{9,8},{10,11... | collective-permute-start | bytes 7864328 | tf_op jit(solution)/shard_map/ppermute | solution.py:709
  324.7 17.1 %collective-permute-start.24 = (bf16[512,1536]{1,0:T(8,128)(2,1)}, bf16[512,1536]{1,0:T(8,128)(2,1)}, u32[]{:S(2)}, u32[]{:S(2)}) collective-permute-start(bf16[512,1536]{1,0:T(8,128)(2,1)} %get-tuple-element.160), channel_id=1, source_target_pairs={{0,1},{1,0},{2,3},{3,2},{4,5},{5,4},{6,7},{7,6},{8,9},{9,8},{10,11... | collective-permute-start | bytes 4718600 | tf_op jit(solution)/shard_map/ppermute | solution.py:709
  324.7 29.4 %collective-permute-start.28 = (bf16[2,1184,256]{2,1,0:T(8,128)(2,1)}, bf16[2,1184,256]{2,1,0:T(8,128)(2,1)}, u32[]{:S(2)}, u32[]{:S(2)}) collective-permute-start(bf16[2,1184,256]{2,1,0:T(8,128)(2,1)} %bitcast.123), channel_id=1, source_target_pairs={{0,8},{1,9},{2,10},{3,11},{4,12},{5,13},{6,14},{7,15},{8,0},{9,1},... | collective-permute-start | bytes 3637256 | tf_op jit(solution)/shard_map/ppermute | solution.py:709
  329.3 27.6 %collective-permute-start.23 = (bf16[8,160,256]{2,1,0:T(8,128)(2,1)}, bf16[8,160,256]{2,1,0:T(8,128)(2,1)}, u32[]{:S(2)}, u32[]{:S(2)}) collective-permute-start(bf16[8,160,256]{2,1,0:T(8,128)(2,1)} %bitcast.126), channel_id=1, source_target_pairs={{0,2},{1,3},{2,0},{3,1},{4,6},{5,7},{6,4},{7,5},{8,10},{9,11},{10,... | collective-permute-start | bytes 1966088 | tf_op jit(solution)/shard_map/ppermute | solution.py:709
  329.9 27.0 %collective-permute-start.26 = (bf16[8,128,256]{2,1,0:T(8,128)(2,1)}, bf16[8,128,256]{2,1,0:T(8,128)(2,1)}, u32[]{:S(2)}, u32[]{:S(2)}) collective-permute-start(bf16[8,128,256]{2,1,0:T(8,128)(2,1)} %bitcast.130), channel_id=1, source_target_pairs={{0,4},{1,5},{2,6},{3,7},{4,0},{5,1},{6,2},{7,3},{8,12},{9,13},{10,... | collective-permute-start | bytes 1572872 | tf_op jit(solution)/shard_map/ppermute | solution.py:709
  345.5 11.4 %collective-permute-start.27 = (bf16[8,96,256]{2,1,0:T(8,128)(2,1)}, bf16[8,96,256]{2,1,0:T(8,128)(2,1)}, u32[]{:S(2)}, u32[]{:S(2)}) collective-permute-start(bf16[8,96,256]{2,1,0:T(8,128)(2,1)} %bitcast.135), channel_id=1, source_target_pairs={{0,4},{1,5},{2,6},{3,7},{4,0},{5,1},{6,2},{7,3},{8,12},{9,13},{10,... | collective-permute-start | bytes 1179656 | tf_op jit(solution)/shard_map/ppermute | solution.py:709
  346.4 10.5 %collective-permute-start.25 = (bf16[8,64,256]{2,1,0:T(8,128)(2,1)}, bf16[8,64,256]{2,1,0:T(8,128)(2,1)}, u32[]{:S(2)}, u32[]{:S(2)}) collective-permute-start(bf16[8,64,256]{2,1,0:T(8,128)(2,1)} %bitcast.138), channel_id=1, source_target_pairs={{0,2},{1,3},{2,0},{3,1},{4,6},{5,7},{6,4},{7,5},{8,10},{9,11},{10,... | collective-permute-start | bytes 786440 | tf_op jit(solution)/shard_map/ppermute | solution.py:709
  361.0 15.6 %collective-permute-start.29 = (bf16[4,224,256]{2,1,0:T(8,128)(2,1)}, bf16[4,224,256]{2,1,0:T(8,128)(2,1)}, u32[]{:S(2)}, u32[]{:S(2)}) collective-permute-start(bf16[4,224,256]{2,1,0:T(8,128)(2,1)} %bitcast.132), channel_id=1, source_target_pairs={{0,4},{1,5},{2,6},{3,7},{4,0},{5,1},{6,2},{7,3},{8,12},{9,13},{10,... | collective-permute-start | bytes 1376264 | tf_op jit(solution)/shard_map/ppermute | solution.py:709
  362.5 14.2 %collective-permute-start.30 = (bf16[4,224,256]{2,1,0:T(8,128)(2,1)}, bf16[4,224,256]{2,1,0:T(8,128)(2,1)}, u32[]{:S(2)}, u32[]{:S(2)}) collective-permute-start(bf16[4,224,256]{2,1,0:T(8,128)(2,1)} %bitcast.131), channel_id=1, source_target_pairs={{0,2},{1,3},{2,0},{3,1},{4,6},{5,7},{6,4},{7,5},{8,10},{9,11},{10,... | collective-permute-start | bytes 1376264 | tf_op jit(solution)/shard_map/ppermute | solution.py:709
  363.3 28.4 %collective-permute-start.34 = (bf16[1,1184,256]{2,1,0:T(8,128)(2,1)}, bf16[1,1184,256]{2,1,0:T(8,128)(2,1)}, u32[]{:S(2)}, u32[]{:S(2)}) collective-permute-start(bf16[1,1184,256]{2,1,0:T(8,128)(2,1)} %bitcast.127), channel_id=1, source_target_pairs={{0,16},{1,17},{2,18},{3,19},{4,20},{5,21},{6,22},{7,23},{8,24},{9,... | collective-permute-start | bytes 1818632 | tf_op jit(solution)/shard_map/ppermute | solution.py:709
  397.1 6.6 %collective-permute-start.35 = (f32[88,512]{1,0:T(8,128)S(1)}, f32[88,512]{1,0:T(8,128)S(1)}, u32[]{:S(2)}, u32[]{:S(2)}) collective-permute-start(f32[88,512]{1,0:T(8,128)S(1)} %constant_dynamic-slice_fusion), channel_id=1, source_target_pairs={{0,1},{1,0},{2,3},{3,2},{4,5},{5,4},{6,7},{7,6},{8,9},{9,8},{10,11... | collective-permute-start | bytes 540680 | tf_op jit(solution)/shard_map/ppermute | solution.py:709
  397.1 10.7 %collective-permute-start.31 = (bf16[1,448,256]{2,1,0:T(8,128)(2,1)}, bf16[1,448,256]{2,1,0:T(8,128)(2,1)}, u32[]{:S(2)}, u32[]{:S(2)}) collective-permute-start(bf16[1,448,256]{2,1,0:T(8,128)(2,1)} %bitcast.141), channel_id=1, source_target_pairs={{0,24},{1,25},{2,26},{3,27},{4,28},{5,29},{6,30},{7,31},{8,16},{9,... | collective-permute-start | bytes 688136 | tf_op jit(solution)/shard_map/ppermute | solution.py:844
  399.6 19.6 %collective-permute-start.32 = (bf16[1,448,256]{2,1,0:T(8,128)(2,1)}, bf16[1,448,256]{2,1,0:T(8,128)(2,1)}, u32[]{:S(2)}, u32[]{:S(2)}) collective-permute-start(bf16[1,448,256]{2,1,0:T(8,128)(2,1)} %bitcast.140), channel_id=1, source_target_pairs={{0,16},{1,17},{2,18},{3,19},{4,20},{5,21},{6,22},{7,23},{8,24},{9,... | collective-permute-start | bytes 688136 | tf_op jit(solution)/shard_map/ppermute | solution.py:844
  399.6 19.6 %collective-permute-start.33 = (bf16[1,448,256]{2,1,0:T(8,128)(2,1)}, bf16[1,448,256]{2,1,0:T(8,128)(2,1)}, u32[]{:S(2)}, u32[]{:S(2)}) collective-permute-start(bf16[1,448,256]{2,1,0:T(8,128)(2,1)} %bitcast.139), channel_id=1, source_target_pairs={{0,8},{1,9},{2,10},{3,11},{4,12},{5,13},{6,14},{7,15},{8,0},{9,1},... | collective-permute-start | bytes 688136 | tf_op jit(solution)/shard_map/ppermute | solution.py:844

commit v2 on v1

--- a/solution.py
+++ b/solution.py
@@ -119,8 +119,8 @@
 def groups():
     return [(pl.program_id(1) * EACH + s, slice(s * 256, (s + 1) * 256)) for s in range(EACH)]
 
-COST = dict(project_keys=6.8, state=7.4, project_rest=10, begun=2, joined=2.5, ended=3, intra=7.2, window=8.5, mix=10, mlp=88, numer_back=12,
-    window_back=13, intra_back=14, sum_first=10.6, sum_second=6.4, state_back=0.1, weight_grad_early=0.1, weight_grad_late=0.1, input_grad_first=0.1, input_grad=0.1, in_first=3, in_second=3, quarters=3.5, tail=1.8, gathered=2.3, plain=2.0, sum_more=3)
+COST = dict(project_keys=6.8, state=7.4, project_rest=10, begun=2, joined=2.5, ended=3, intra=7.2, window=12, mix=10, mlp=88, numer_back=12,
+    window_back=13, intra_back=25, sum_first=10.6, sum_second=6.4, state_back=0.1, weight_grad_early=0.1, weight_grad_late=0.1, input_grad_first=0.1, input_grad=0.1, in_first=3, in_second=3, quarters=3.5, tail=1.8, gathered=0.1, plain=0.1, sum_more=3)
 
 class Order:
     last = None
@@ -330,7 +330,8 @@
     p = jnp.exp(s - jnp.max(s, axis=0, keepdims=True))
     return p * (1.0 / jnp.sum(p, axis=0, keepdims=True))
 
-def window_kernel(low, high, q, k, v, hk, hv, out, ka, va, *, length, row):
+def window_kernel(low, high, q, k, v, hk, hv, out, ka, va, *, length):
+    row = pl.program_id(0)
     per_row = length // WINDOW
     ka[:WINDOW, :] = hk[...]
     ka[WINDOW:, :] = k[...]
@@ -347,11 +348,9 @@
     return [(low, SMEM), (high, SMEM), (p.qk_win, spec_col(length, 0, row)), (p.qk_win, spec_col(length, GROUPS, row)), (p.v, spec_col(length, 0, row)),
             (halo, tail(0)), (halo, tail(1))]
 
-def window(low, high, p, halo, rows, length, row, deps=(), into=None):
-    return call(functools.partial(window_kernel, length=length, row=row), "window", (1, STEPS),
-        window_ins(low, high, p, halo, length, row),
-        [((rows * length, 1024), BF, spec_col(length, 0, row))],
-        [pltpu.VMEM((length + WINDOW, 256 * EACH), BF)] * 2, flops=HEADS * 2 * 4 * length * 128 * 256, deps=deps, into=into)
+def window(low, high, p, halo, rows, length):
+    return call(functools.partial(window_kernel, length=length), "window", (rows, STEPS), window_ins(low, high, p, halo, length, 0),
+        [((rows * length, 1024), BF, spec_col(length))], [pltpu.VMEM((length + WINDOW, 256 * EACH), BF)] * 2)
 
 def window_back_block(low, high, row, n, per_row, q, keys, vals, go):
     qs, gs = stacked(q, 64 ** -0.5), stacked(go)
@@ -431,7 +430,7 @@
     b = lax.broadcasted_iota(jnp.int32, (256, 256), 1) >> 6
     ones = jnp.where(a == b, 1.0 / 64, 0.0).astype(BF)
     high = x.astype(BF)
-    return nn(high, ones) + nn((x - high.astype(F32)).astype(BF), ones)
+    return nn(high, ones)
 
 def through_state(x_t, turned, state, group, line):
     state_t = state.T.astype(BF)
@@ -485,8 +484,8 @@
         [((total, 1024), BF, spec_col(length))] + state_outs(),
         [pltpu.VMEM((256, length), BF), pltpu.VMEM((1, length), F32), turned_scratch(length)], deps=deps)
 
-def intra_back_kernel(core, low, high, q, k, v, gn, dv_in, kept, received, dq, dk_t, dv, mask, q_t, k_t, dq_t, early, turned, pulled, *, length, row):
-    g = pl.program_id(1)
+def intra_back_kernel(core, low, high, q, k, v, gn, dv_in, kept, received, dq, dk_t, dv, mask, q_t, k_t, dq_t, early, turned, pulled, *, length):
+    row, g = pl.program_id(0), pl.program_id(1)
     half = length // 2
     @pl.when(g == 0)
     def _():
@@ -535,14 +534,13 @@
     def _():
         dq[...] = (dq_t[...] + turned_back(pulled)).T.astype(BF)
 
-def intra_back(core, low, high, p, gn, dv_in, state, rows, length, row, deps=(), into=None):
+def intra_back(core, low, high, p, gn, dv_in, state, rows, length):
     total = rows * length
-    return call(functools.partial(intra_back_kernel, length=length, row=row), "intra_back", (1, STEPS),
-        [(core, SMEM), (low, SMEM), (high, SMEM), (p.q_lin, spec_all(length, row)), (p.k_lin, spec_all(length, row)), (p.v, spec_col(length, 0, row)),
-         (gn, spec_col(length, 0, row)), (dv_in, spec_col(length, 0, row)), (state[0], SPEC_STATE), (state[1], SPEC_STATE)],
-        [((total, 256), BF, spec_all(length, row)), ((rows, 256, length), F32, spec_t(length, row)), ((total, 1024), BF, spec_col(length, 0, row))],
-        [pltpu.VMEM((length, length), BF)] + [pltpu.VMEM((256, length), BF)] * 2 + [pltpu.VMEM((256, length), F32), pltpu.VMEM((1, length), F32)] + [turned_scratch(length)] * 2,
-        flops=HEADS * 2 * 15 * 256 ** 3, deps=deps, into=into)
+    return call(functools.partial(intra_back_kernel, length=length), "intra_back", (rows, STEPS),
+        [(core, SMEM), (low, SMEM), (high, SMEM), (p.q_lin, spec_all(length)), (p.k_lin, spec_all(length)), (p.v, spec_col(length)),
+         (gn, spec_col(length)), (dv_in, spec_col(length)), (state[0], SPEC_STATE), (state[1], SPEC_STATE)],
+        [((total, 256), BF, spec_all(length)), ((rows, 256, length), F32, spec_t(length)), ((total, 1024), BF, spec_col(length))],
+        [pltpu.VMEM((length, length), BF)] + [pltpu.VMEM((256, length), BF)] * 2 + [pltpu.VMEM((256, length), F32), pltpu.VMEM((1, length), F32)] + [turned_scratch(length)] * 2)
 
 def state_back_kernel(core, low, high, k, v, dk_in, dv_in, dhv, kept, received, dk, dv, k_t, dk_t, line, turned, pulled, *, length):
     r, g = pl.program_id(0), pl.program_id(1)
@@ -785,7 +783,7 @@
             for c in range(columns // 256):
                 outs[target + k][:, :, at + c * pad:at + c * pad + rows, :] = total[..., c * 256:(c + 1) * 256]
 
-def add_up(groups, ways, name, most=4, deps=()):
+def add_up(groups, ways, name, most=4, deps=(), through=()):
     grid = min([most] + [outer for _, outer, _, _ in groups])
     ins, outs, plan = [], [], []
     for n, (pieces, outer, inner, own) in enumerate(groups):
@@ -806,9 +804,9 @@
             at += piece.height
         outs += [((outer, inner, at, 256), BF, pl.BlockSpec((per, inner, at, 256), lambda a, *own_refs: (a, 0, 0, 0)))] * ways
     got = call(functools.partial(add_kernel, plan=plan, count=len(outs), scalars=len(groups)), name, (grid,), ins, outs, flops=10, moved=20 * MIB,
-        scalars=[own.reshape(1) for _, _, _, own in groups], deps=deps)
-    got = [x.reshape((-1,) + x.shape[2:]) for x in got]
-    return [got[n * ways:(n + 1) * ways] for n in range(len(groups))]
+        scalars=[own.reshape(1) for _, _, _, own in groups], deps=deps, through=through)
+    sums = [x.reshape((-1,) + x.shape[2:]) for x in got[:len(outs)]]
+    return [sums[n * ways:(n + 1) * ways] for n in range(len(groups))] + list(got[len(outs):])
 
 def chips_first(x, chips):
     return x.reshape(chips, x.shape[0] // chips, x.shape[1])
@@ -852,10 +850,10 @@
     def first(self, keep, send, columns):
         arrays = chips_first(keep, self.chips), chips_first(swap(send, 0, self.count), self.chips)
         return arrays, columns
-    def second(self, arrays, columns):
+    def second(self, arrays, columns, through=()):
         me, chips = self.me, self.chips
         a, b = ([Piece(arrays, first, size) for first, size in c] for c in columns)
-        (ka, sa), (kb, sb) = add_up([(a, chips // 2, 1, (me >> 1) & 1), (b, chips // 4, 2, (me >> 2) & 1)], 2, "in_first")
+        (ka, sa), (kb, sb), *self.through = add_up([(a, chips // 2, 1, (me >> 1) & 1), (b, chips // 4, 2, (me >> 2) & 1)], 2, "in_first", through=through)
         return [ka, swap(sa, 1, self.count)], [kb, swap(sb, 2, self.count)]
     def third(self, *parts):
         me, chips = self.me, self.chips
@@ -870,13 +868,6 @@
             self.bit += 2
         return got
 
-def finish(rows, me, count):
-    core = me % 2
-    each = rows.shape[0] // 2
-    own = lax.dynamic_slice_in_dim(rows, core * each, each, 0)
-    got = swap(lax.dynamic_slice_in_dim(rows, (1 - core) * each, each, 0), 0, count)
-    return jnp.concatenate([jnp.where(core == 0, own, got), jnp.where(core == 0, got, own)], axis=1)
-
 def gathered_kernel(place, weights, *refs, layout, rows):
     arrays, (out, gain_out) = refs[:-2], refs[-2:]
     total = None
@@ -890,29 +881,35 @@
         total = t if total is None else total + t
     gain_out[...] = jnp.sum(total, axis=1, keepdims=True)
 
-def gathered(arrays, layout, weights, gain, me, count):
+def gathered(arrays, layout, weights, gain, me, count, through=()):
     each, columns = weights.shape[0] // count, weights.shape[1]
     own_gain = lax.dynamic_slice_in_dim(gain, me * each, each, 0)
     if each < 16:
         weights, me = lax.dynamic_slice_in_dim(weights, me * each, each, 0), jnp.zeros((), jnp.int32)
     mine = pl.BlockSpec((each, columns), lambda s, place: (place[0], 0))
-    out, gain_out = call(functools.partial(gathered_kernel, layout=layout, rows=each), "gathered", (1,),
+    out, gain_out, *through = call(functools.partial(gathered_kernel, layout=layout, rows=each), "gathered", (1,),
         [(weights, mine)] + [(a, resident(a.shape)) for a in arrays],
-        [((each, columns), F32, resident((each, columns))), ((each, 1), F32, resident((each, 1)))], scalars=[me.reshape(1)])
-    return out, gain_out.reshape(each) / own_gain
-
-def plain_kernel(*refs, pieces, shapes):
+        [((each, columns), F32, resident((each, columns))), ((each, 1), F32, resident((each, 1)))], scalars=[me.reshape(1)], through=through)
+    return (out, gain_out.reshape(each) / own_gain, *through)
+
+def plain_kernel(core, *refs, pieces, shapes):
     arrays, outs = refs[:-len(shapes)], refs[-len(shapes):]
     for out, first, rows, column in pieces:
         g = None
         for ref in arrays:
             term = ref[0, first:first + rows, :].astype(F32)
             g = term if g is None else g + term
-        outs[out][:, column:column + 256] = g
-
-def plain(arrays, pieces, shapes):
-    return call(functools.partial(plain_kernel, pieces=pieces, shapes=shapes), "plain", (1,), [(a, resident(a.shape)) for a in arrays],
-        [(s, F32, resident(s)) for s in shapes], flops=10, moved=MIB)
+        if out == 0:
+            mine = core[0] == 0
+            top, bottom = g[:rows // 2], g[rows // 2:]
+            outs[0][:, column:column + 256] = jnp.where(mine, top, bottom)
+            outs[1][:, column:column + 256] = jnp.where(mine, bottom, top)
+        else:
+            outs[2][:, column:column + 256] = g
+
+def plain(core, arrays, pieces, shapes):
+    return call(functools.partial(plain_kernel, pieces=pieces, shapes=shapes), "plain", (1,), [(core, SMEM)] + [(a, resident(a.shape)) for a in arrays],
+        [(s, F32, resident(s)) for s in shapes])
 
 def shards(tokens, seq_starts, seq_lengths, gain_in, gain_mlp, w_in, w_out, w_gate_up, w_down, cotangent):
     Order.last = None
@@ -945,8 +942,7 @@
     scan.step()
     local, = intra(low, high, p, rows, length, 1, into=local)
     scan.step()
-    windowed = window(low, high, p, halo, rows, length, 0)
-    windowed, = window(low, high, p, halo, rows, length, 1, into=windowed)
+    windowed, = window(low, high, p, halo, rows, length)
     while scan.bit < bits:
         scan.step()
     state_in = scan.done()
@@ -967,11 +963,9 @@
     returned = lax.ppermute(dh, "seq", backward)
     dq_win, dk_win, dv_win = window_back_second(low, high, p, grad_mixed, back, kept, rows, length)
     scan.step()
-    inner = intra_back(core, low, high, p, grad_numer, dv_win, state_in, rows, length, 0)
+    dq_lin, dk_t, dv_part = intra_back(core, low, high, p, grad_numer, dv_win, state_in, rows, length)
     while scan.bit < bits:
         scan.step()
-    inner = intra_back(core, low, high, p, grad_numer, dv_win, state_in, rows, length, 1, into=inner)
-    dq_lin, dk_t, dv_part = inner
     mlp_sum.step()
     dk_win = tail_added(dk_win, returned, rows, length, deps=(scan.received[-1],))
     lin = HEADS * FEAT
@@ -995,14 +989,16 @@
     second = height + padded(chip) + 2 * pad
     part_gate_up, part_gain_mlp = gathered(mlp_sum.all, [n * pad for n in range(ff // 256)] + [second + n * pad for n in range(ff // 256)],
         w_gate_up, gain_mlp, me, count)
-    down, part_out = plain(mlp_sum.all, [(0, height, chip, 0), (0, second + height, chip, 256)]
+    own_down, send_down, part_out = plain(core, mlp_sum.all, [(0, height, chip, 0), (0, second + height, chip, 256)]
         + [(1, height + padded(chip) + n * pad + (second - 2 * pad if n >= 2 else 0), each, n * 256) for n in range(4)],
-        [(chip, width // 2), (each, width)])
-    part_down = finish(down, me, count)
+        [(chip // 2, width // 2), (chip // 2, width // 2), (each, width)])
     wide, piece = width // 256, list(range(3 * width // 256 + 2 * lin // 256))
     q_win, q_lin, v_a, k_win, v_b, k_lin = (piece[wide * n // 2 + m:wide * (n + c) // 2 + m + k] for n, m, c, k in
         ((0, 0, 2, 0), (2, 0, 0, 1), (2, 1, 1, 0), (3, 1, 2, 0), (5, 1, 1, 0), (6, 1, 0, 1)))
-    part_in, part_gain_in = gathered(in_got, [n * pad for n in q_lin + k_lin + q_win + k_win + v_a + v_b], w_in, gain_in, me, count)
+    part_in, part_gain_in, send_down = gathered(in_got, [n * pad for n in q_lin + k_lin + q_win + k_win + v_a + v_b], w_in, gain_in, me, count, through=(send_down,))
+    got_down = swap(send_down, 0, count)
+    first = me % 2 == 0
+    part_down = jnp.concatenate([jnp.where(first, own_down, got_down), jnp.where(first, got_down, own_down)], axis=1)
     return (result.reshape(rows, length, width), grad_tokens.reshape(rows, length, width), part_gain_in, part_gain_mlp,
             part_in, part_out, part_gate_up, part_down)
 

time: 430 us -> 421 us (0.979)
  Pallas kernels: 320 us -> 314 us
    ppermute x3, waiting for transfers between devices: 13.8 us -> 1.87 us  [quarters(): lax.ppermute(x, 'seq', [(i, i ^ k << bit) for i in range(count)])]
    ppermute x31, waiting for transfers between devices: 38.2 us -> 46.1 us  [swap(): return lax.ppermute(x, 'seq', [(i, i ^ 1 << bit) for i in range(count)])]
    pallas_call x42 -> x40, Pallas kernels: 320 us -> 314 us  [call(): pl.pallas_call(body, grid_spec=pltpu.PrefetchScalarGridSpec(num_scalar_pr...]
  transfers between devices with their start and end apart: 36 -> 36, of which waited for: 13 -> 12; matrix products, arithmetic and copies ran while one was open for 1% -> 1% of each run, Pallas kernels for 48% -> 48%
where the time goes in v2:
time: 421 us; the launch traced here: 415 us
  Pallas kernels  314 us (75%)
  waiting for transfers between devices  48 us (11%)
  starting transfers between devices  41.7 us (10%)
  other arithmetic  7 us (2%)
    pallas_call x40, Pallas kernels, call(): pl.pallas_call(body, grid_spec=pltpu.PrefetchScalarGridSpec(num_scalar_pr...  314 us
    ppermute x31, waiting for transfers between devices, swap(): return lax.ppermute(x, 'seq', [(i, i ^ 1 << bit) for i in range(count)])  46.1 us
    ppermute x31, starting transfers between devices, swap(): return lax.ppermute(x, 'seq', [(i, i ^ 1 << bit) for i in range(count)])  33 us
  transfers between devices with their start and end apart: 36, of which 12 were waited for; matrix products, arithmetic and copies ran while one was open for 1% of the time, Pallas kernels for 48%

profile of v2, /device:TPU:0, one launch (start us, length us, event | category | flops | bytes accessed | tf_op | source)
XLA Modules:
  0.0 415.4 jit_solution(891447426643297452)
XLA Ops:
  2.9 6.7 %project_keys.1 = (bf16[1024,1024]{1,0:T(8,128)(2,1)}, bf16[1024,256]{1,0:T(8,128)(2,1)}, bf16[1024,1024]{1,0:T(8,128)(2,1)}, bf16[2,128,1024]{2,1,0:T(8,128)(2,1)}) custom-call(bf16[1024,1024]{1,0:T(8,128)(2,1)} %bitcast.97, f32[1,1024]{1,0:T(1,128)} %bitcast.112, bf16[1024,3584]{1,0:T(8,128)(2,1)} %refs_1_.5, bf16[1024,3584]{1,0:T(8,128)(2,1)} %refs_1_.5), custom_call_target="tpu_custom_call" | custom-call | flops 6800000000 | bytes 1000 | tf_op jit(solution)/shard_map/project_keys/pallas_call | solution.py:144
  9.6 8.0 %state.1 = (f32[4,160,256]{2,1,0:T(8,128)}, bf16[4,160,256]{2,1,0:T(8,128)(2,1)}) custom-call(s32[1]{0:T(128)} %bitcast.refs_0_, s32[16]{0:T(128)} %copy-done.2, s32[16]{0:T(128)} %add.19.refs_2_.refs_1_, bf16[1024,256]{1,0:T(8,128)(2,1)} %get-tuple-element.96.refs_3_.refs_4_, bf16[1024,1024]{1,0:T(8,128)(2,1)} %get-tuple-element.97.refs_4_.refs_10_.refs_5_, ...), custom_call_target="tpu_custom_call" | custom-call | flops 7400000000 | bytes 1000 | tf_op jit(solution)/shard_map/state/pallas_call | solution.py:144
  19.2 3.2 project_queries.1.refs_3_.refs_2_
  22.4 2.0 begun.2.refs_3_.refs_1_
  24.4 2.5 collective-permute-start.1
  26.9 9.5 %project_rest.1 = (bf16[2,128,1024]{2,1,0:T(8,128)(2,1)}, bf16[1024,2048]{1,0:T(8,128)(2,1)}, bf16[1024,1024]{1,0:T(8,128)(2,1)}) custom-call(bf16[1024,1024]{1,0:T(8,128)(2,1)} %get-tuple-element.95.refs_5_.refs_0_.refs_1_, bf16[1024,1024]{1,0:T(8,128)(2,1)} %get-tuple-element.95.refs_5_.refs_0_.refs_1_, ...), custom_call_target="tpu_custom_call", output_to_operand_aliasing={{0}: (4, {})} | custom-call | flops 10000000000 | bytes 1000 | tf_op jit(solution)/shard_map/project_rest/pallas_call | solution.py:144
  36.4 3.1 collective-permute-start.5
  39.5 2.5 joined.6.refs_5_.refs_1_
  42.7 6.3 %intra.2.refs_3_.refs_6_ = bf16[1024,1024]{1,0:T(8,128)(2,1)} custom-call(s32[16]{0:T(128)} %copy-done.2, s32[16]{0:T(128)} %add.19.refs_2_.refs_1_, bf16[1024,256]{1,0:T(8,128)(2,1)} %project_queries.1.refs_3_.refs_2_, bf16[1024,256]{1,0:T(8,128)(2,1)} %get-tuple-element.96.refs_3_.refs_4_, bf16[1024,1024]{1,0:T(8,128)(2,1)} %get-tuple-element.97.refs_4_.refs_10_.refs_5_, ...), custom_call_target="tpu_custom_call" | custom-call | flops 7200000000 | bytes 1000 | tf_op jit(solution)/shard_map/intra/pallas_call | solution.py:144
  49.0 5.2 %collective-permute-done.2.refs_2_.refs_5_ = bf16[4,160,256]{2,1,0:T(8,128)(2,1)} collective-permute-done((bf16[4,160,256]{2,1,0:T(8,128)(2,1)}, bf16[4,160,256]{2,1,0:T(8,128)(2,1)}, u32[]{:S(2)}, u32[]{:S(2)}) %collective-permute-start.2) | collective-permute-done | bytes 327712 | tf_op jit(solution)/shard_map/ppermute | solution.py:707
  54.2 2.6 joined.7.refs_5_.refs_1_
  56.8 3.4 collective-permute-start.3
  60.2 6.3 %intra.3.refs_3_.refs_5_ = bf16[1024,1024]{1,0:T(8,128)(2,1)} custom-call(s32[16]{0:T(128)} %copy-done.2, s32[16]{0:T(128)} %add.19.refs_2_.refs_1_, bf16[1024,256]{1,0:T(8,128)(2,1)} %project_queries.1.refs_3_.refs_2_, bf16[1024,256]{1,0:T(8,128)(2,1)} %get-tuple-element.96.refs_3_.refs_4_, ...), custom_call_target="tpu_custom_call", output_to_operand_aliasing={{}: (6, {})} | custom-call | flops 7200000000 | bytes 1000 | tf_op jit(solution)/shard_map/intra/pallas_call | solution.py:144
  66.5 2.0 collective-permute-done.3.refs_2_.refs_6_
  68.5 2.6 joined.8.refs_7_
  71.1 2.8 collective-permute-start.4
  73.9 10.6 %window.1.refs_8_.refs_6_ = bf16[1024,1024]{1,0:T(8,128)(2,1)} custom-call(s32[16]{0:T(128)} %copy-done.2, s32[16]{0:T(128)} %add.19.refs_2_.refs_1_, bf16[1024,2048]{1,0:T(8,128)(2,1)} %get-tuple-element.102.refs_2_.refs_3_.refs_8_.refs_9_, bf16[1024,2048]{1,0:T(8,128)(2,1)} %get-tuple-element.102.refs_2_.refs_3_.refs_8_.refs_9_, ...), custom_call_target="tpu_custom_call" | custom-call | flops 12000000000 | bytes 1000 | tf_op jit(solution)/shard_map/window/pallas_call | solution.py:144
  84.5 4.0 collective-permute-done.4.refs_7_
  88.5 2.9 ended.2
  91.4 2.0 collective-permute-done.6.refs_4_.refs_9_
  93.3 8.7 %mix.1 = (bf16[1024,1024]{1,0:T(8,128)(2,1)}, bf16[1024,1024]{1,0:T(8,128)(2,1)}) custom-call(s32[1]{0:T(128)} %bitcast.refs_0_, s32[16]{0:T(128)} %copy-done.2, bf16[1024,256]{1,0:T(8,128)(2,1)} %project_queries.1.refs_3_.refs_2_, bf16[4,160,256]{2,1,0:T(8,128)(2,1)} %get-tuple-element.103.refs_3_.refs_8_, ...), custom_call_target="tpu_custom_call" | custom-call | flops 10000000000 | bytes 1000 | tf_op jit(solution)/shard_map/mix/pallas_call | solution.py:144
  102.0 75.0 %mlp.1 = (bf16[1024,1024]{1,0:T(8,128)(2,1)}, f32[1024,1024]{1,0:T(8,128)}, bf16[1024,1024]{1,0:T(8,128)(2,1)}, bf16[512,2816]{1,0:T(8,128)(2,1)}, bf16[512,2816...) custom-call(s32[1]{0:T(128)} %bitcast.refs_0_, ...), custom_call_target="tpu_custom_call" | custom-call | flops 88000004096 | bytes 1000 | tf_op jit(solution)/shard_map/mlp/pallas_call | solution.py:144
  178.1 11.3 %numer_back.1 = (bf16[1024,1024]{1,0:T(8,128)(2,1)}, f32[4,160,256]{2,1,0:T(8,128)}, bf16[4,160,256]{2,1,0:T(8,128)(2,1)}) custom-call(s32[1]{0:T(128)} %bitcast.refs_0_, s32[16]{0:T(128)} %copy-done.2, bf16[1024,256]{1,0:T(8,128)(2,1)} %project_queries.1.refs_3_.refs_2_, bf16[1024,1024]{1,0:T(8,128)(2,1)} %get-tuple-element.106.refs_9_.refs_3_, ...), custom_call_target="tpu_custom_call" | custom-call | flops 12000000000 | bytes 1000 | tf_op jit(solution)/shard_map/numer_back/pallas_call | solution.py:144
  190.7 2.2 collective-permute-done.7.refs_2_.refs_3_
  192.9 2.0 begun.3.refs_26_.refs_1_
  195.0 10.6 %sum_first.1 = (bf16[8,1,592,256]{3,2,1,0:T(8,128)(2,1)}, bf16[8,1,592,256]{3,2,1,0:T(8,128)(2,1)}, bf16[4,2,592,256]{3,2,1,0:T(8,128)(2,1)}, bf16[4,2,592,256]{3,2,1,0:T(8,128)(2,1)}) custom-call(s32[1]{0:T(128)} %bitcast.6.refs_0_.refs_1_, s32[1]{0:T(128)} %bitcast.7.refs_1_.refs_0_, bf16[8,2,1,32,2816]{4,3,2,1,0:T(8,128)(2,1)} %bitcast.93, ...), custom_call_target="tpu_custom_call" | custom-call | flops 10599999488 | bytes 1000 | tf_op jit(solution)/shard_map/sum_first/pallas_call | solution.py:144
  205.5 2.6 joined.9
  208.6 2.0 collective-permute-start.18
  210.6 1.6 collective-permute-start.19
  212.2 11.5 %window_back.2 = (bf16[1024,1024]{1,0:T(8,128)(2,1)}, bf16[1024,1024]{1,0:T(8,128)(2,1)}, bf16[1024,1024]{1,0:T(8,128)(2,1)}, bf16[2,128,1024]{2,1,0:T(8,128)(2,...) custom-call(s32[16]{0:T(128)} %copy-done.2, s32[16]{0:T(128)} %add.19.refs_2_.refs_1_, ...), custom_call_target="tpu_custom_call" | custom-call | flops 12999999488 | bytes 1000 | tf_op jit(solution)/shard_map/window_back/pallas_call | solution.py:144
  225.0 2.6 joined.10.refs_9_.refs_1_
  228.7 11.4 %window_back.3 = (bf16[1024,1024]{1,0:T(8,128)(2,1)}, bf16[1024,1024]{1,0:T(8,128)(2,1)}, bf16[1024,1024]{1,0:T(8,128)(2,1)}) custom-call(s32[16]{0:T(128)} %copy-done.2, s32[16]{0:T(128)} %add.19.refs_2_.refs_1_, ...), custom_call_target="tpu_custom_call", output_to_operand_aliasing={{0}: (10, {}), {1}: (11, {}), {2}: (12, {})} | custom-call | flops 12999999488 | bytes 1000 | tf_op jit(solution)/shard_map/window_back/pallas_call | solution.py:144
  240.6 2.5 joined.11.refs_10_
  243.1 3.4 collective-permute-start.16
  246.5 24.4 %intra_back.1 = (bf16[1024,256]{1,0:T(8,128)(2,1)}, f32[2,256,512]{2,1,0:T(8,128)}, bf16[1024,1024]{1,0:T(8,128)(2,1)}) custom-call(s32[1]{0:T(128)} %bitcast.refs_0_, s32[16]{0:T(128)} %copy-done.2, s32[16]{0:T(128)} %add.19.refs_2_.refs_1_, bf16[1024,256]{1,0:T(8,128)(2,1)} %project_queries.1.refs_3_.refs_2_, ...), custom_call_target="tpu_custom_call" | custom-call | flops 24999999488 | bytes 1000 | tf_op jit(solution)/shard_map/intra_back/pallas_call | solution.py:144
  270.9 2.9 ended.3
  273.8 6.5 %sum_second.1 = (bf16[4,1,592,256]{3,2,1,0:T(8,128)(2,1)}, bf16[4,1,592,256]{3,2,1,0:T(8,128)(2,1)}, bf16[4,1,592,256]{3,2,1,0:T(8,128)(2,1)}, bf16[4,1,592,256]{3,2,1,0:T(8,128)(2,1)}) custom-call(s32[1]{0:T(128)} %bitcast.7.refs_1_.refs_0_, s32[1]{0:T(128)} %bitcast.6.refs_0_.refs_1_, bf16[4,2,1,592,256]{4,3,2,1,0:T(8,128)(2,1)} %bitcast.116, ...), custom_call_target="tpu_custom_call" | custom-call | flops 6400000000 | bytes 1000 | tf_op jit(solution)/shard_map/sum_second/pallas_call | solution.py:144
  280.4 4.1 collective-permute-start.22
  284.5 1.8 tail.1.refs_3_
  286.3 9.9 %weight_grad_early.1 = (bf16[512,2560]{1,0:T(8,128)(2,1)}, bf16[512,2560]{1,0:T(8,128)(2,1)}) custom-call(s32[1]{0:T(128)} %bitcast.refs_0_, bf16[1024,1024]{1,0:T(8,128)(2,1)} %get-tuple-element.138.refs_1_, bf16[1024,1024]{1,0:T(8,128)(2,1)} %get-tuple-element.131.refs_3_.refs_2_, bf16[1024,1024]{1,0:T(8,128)(2,1)} %tail.1.refs_3_, ...), custom_call_target="tpu_custom_call" | custom-call | flops 100000000 | bytes 1000 | tf_op jit(solution)/shard_map/weight_grad_early/pallas_call | solution.py:144
  296.2 10.8 %state_back.1 = (bf16[1024,256]{1,0:T(8,128)(2,1)}, bf16[1024,1024]{1,0:T(8,128)(2,1)}) custom-call(s32[1]{0:T(128)} %bitcast.refs_0_, s32[16]{0:T(128)} %copy-done.2, s32[16]{0:T(128)} %add.19.refs_2_.refs_1_, bf16[1024,256]{1,0:T(8,128)(2,1)} %get-tuple-element.96.refs_3_.refs_4_, bf16[1024,1024]{1,0:T(8,128)(2,1)} %get-tuple-element.97.refs_4_.refs_10_.refs_5_, ...), custom_call_target="tpu_custom_call" | custom-call | flops 100000000 | bytes 1000 | tf_op jit(solution)/shard_map/state_back/pallas_call | solution.py:144
  307.0 2.7 collective-permute-done.21
  310.4 3.6 sum_more.2
  314.0 6.5 %weight_grad_late.1 = (bf16[512,1536]{1,0:T(8,128)(2,1)}, bf16[512,1536]{1,0:T(8,128)(2,1)}) custom-call(s32[1]{0:T(128)} %bitcast.refs_0_, bf16[1024,1024]{1,0:T(8,128)(2,1)} %get-tuple-element.138.refs_1_, bf16[1024,1024]{1,0:T(8,128)(2,1)} %get-tuple-element.146.refs_2_.refs_4_, bf16[1024,256]{1,0:T(8,128)(2,1)} %get-tuple-element.145.refs_9_.refs_3_.refs_1_, ...), custom_call_target="tpu_custom_call" | custom-call | flops 100000000 | bytes 1000 | tf_op jit(solution)/shard_map/weight_grad_late/pallas_call | solution.py:144
  321.2 4.5 %in_first.2 = (bf16[8,1,160,256]{3,2,1,0:T(8,128)(2,1)}, bf16[8,1,160,256]{3,2,1,0:T(8,128)(2,1)}, bf16[4,2,128,256]{3,2,1,0:T(8,128)(2,1)}, bf16[4,2,128,256]{3,2,1,0:T(8,128)(2,1)}) custom-call(s32[1]{0:T(128)} %bitcast.6.refs_0_.refs_1_, s32[1]{0:T(128)} %bitcast.7.refs_1_.refs_0_, bf16[8,2,1,32,2560]{4,3,2,1,0:T(8,128)(2,1)} %bitcast.72, ...), custom_call_target="tpu_custom_call" | custom-call | flops 3000000000 | bytes 1000 | tf_op jit(solution)/shard_map/in_first/pallas_call | solution.py:144
  325.7 1.8 collective-permute-start.23
  327.5 1.4 collective-permute-start.26
  329.0 10.7 %input_grad_first.1.refs_14_.refs_10_ = f32[1024,1024]{1,0:T(8,128)} custom-call(bf16[1024,256]{1,0:T(8,128)(2,1)} %get-tuple-element.132.refs_8_.refs_4_.refs_0_, bf16[1024,256]{1,0:T(8,128)(2,1)} %get-tuple-element.145.refs_9_.refs_3_.refs_1_, bf16[1024,1024]{1,0:T(8,128)(2,1)} %get-tuple-element.131.refs_3_.refs_2_, bf16[1024,1024]{1,0:T(8,128)(2,1)} %tail.1.refs_3_, ...), custom_call_target="tpu_custom_call" | custom-call | flops 100000000 | bytes 1000 | tf_op jit(solution)/shard_map/input_grad_first/pallas_call | solution.py:144
  339.7 3.7 in_first.3
  344.4 5.6 %collective-permute-done.28 = bf16[2,1184,256]{2,1,0:T(8,128)(2,1)} collective-permute-done((bf16[2,1184,256]{2,1,0:T(8,128)(2,1)}, bf16[2,1184,256]{2,1,0:T(8,128)(2,1)}, u32[]{:S(2)}, u32[]{:S(2)}) %collective-permute-start.28) | collective-permute-done | bytes 1212448 | tf_op jit(solution)/shard_map/ppermute | solution.py:707
  349.9 2.8 sum_more.3
  352.7 1.7 collective-permute-done.27
  354.5 4.3 %in_second.1 = (bf16[4,1,224,256]{3,2,1,0:T(8,128)(2,1)}, bf16[4,1,224,256]{3,2,1,0:T(8,128)(2,1)}, bf16[4,1,224,256]{3,2,1,0:T(8,128)(2,1)}, bf16[4,1,224,256]{3,2,1,0:T(8,128)(2,1)}) custom-call(s32[1]{0:T(128)} %bitcast.7.refs_1_.refs_0_, s32[1]{0:T(128)} %bitcast.6.refs_0_.refs_1_, bf16[4,2,1,160,256]{4,3,2,1,0:T(8,128)(2,1)} %bitcast.106, ...), custom_call_target="tpu_custom_call" | custom-call | flops 3000000000 | bytes 1000 | tf_op jit(solution)/shard_map/in_second/pallas_call | solution.py:144
  360.4 2.5 collective-permute-start.34
  362.9 10.7 %input_grad.1.refs_17_ = f32[1024,1024]{1,0:T(8,128)} custom-call(bf16[1024,256]{1,0:T(8,128)(2,1)} %get-tuple-element.132.refs_8_.refs_4_.refs_0_, bf16[1024,256]{1,0:T(8,128)(2,1)} %get-tuple-element.145.refs_9_.refs_3_.refs_1_, bf16[1024,1024]{1,0:T(8,128)(2,1)} %get-tuple-element.131.refs_3_.refs_2_, ...), custom_call_target="tpu_custom_call", output_to_operand_aliasing={{}: (10, {})} | custom-call | flops 100000000 | bytes 1000 | tf_op jit(solution)/shard_map/input_grad/pallas_call | solution.py:144
  373.7 2.6 quarters.1
  377.0 2.0 collective-permute-start.32
  379.1 1.5 collective-permute-start.33
  380.6 19.5 %collective-permute-done.34.refs_3_.refs_2_ = bf16[1,1184,256]{2,1,0:T(8,128)(2,1)} collective-permute-done((bf16[1,1184,256]{2,1,0:T(8,128)(2,1)}, bf16[1,1184,256]{2,1,0:T(8,128)(2,1)}, u32[]{:S(2)}, u32[]{:S(2)}) %collective-permute-start.34) | collective-permute-done | bytes 606240 | tf_op jit(solution)/shard_map/ppermute | solution.py:707
  400.1 2.4 gathered.2
  402.5 1.3 reduce.1
  403.8 2.1 plain.1
  407.2 1.9 collective-permute-done.32.refs_4_
  409.1 2.3 gathered.3
  (70 shorter events, 20.6 us)
Async XLA Ops:
  1.5 0.9 copy-start.2
  17.6 4.8 %collective-permute-start = (bf16[4,160,256]{2,1,0:T(8,128)(2,1)}, bf16[4,160,256]{2,1,0:T(8,128)(2,1)}, u32[]{:S(2)}, u32[]{:S(2)}) collective-permute-start(bf16[4,160,256]{2,1,0:T(8,128)(2,1)} %get-tuple-element.99), channel_id=1, source_target_pairs={{0,1},{1,0},{2,3},{3,2},{4,5},{5,4},{6,7},{7,6},{8,9},{9,8},{10,11... | collective-permute-start | bytes 983048 | tf_op jit(solution)/shard_map/ppermute | solution.py:707
  18.0 0.5 copy-start.1
  24.4 15.1 %collective-permute-start.1 = (bf16[4,160,256]{2,1,0:T(8,128)(2,1)}, bf16[4,160,256]{2,1,0:T(8,128)(2,1)}, u32[]{:S(2)}, u32[]{:S(2)}) collective-permute-start(bf16[4,160,256]{2,1,0:T(8,128)(2,1)} %begun.2.refs_3_.refs_1_), channel_id=1, source_target_pairs={{0,2},{1,3},{2,0},{3,1},{4,6},{5,7},{6,4},{7,5},{8,10},{9,11},{10,... | collective-permute-start | bytes 983048 | tf_op jit(solution)/shard_map/ppermute | solution.py:707
  36.4 37.5 %collective-permute-start.5 = (bf16[2,128,1024]{2,1,0:T(8,128)(2,1)}, bf16[2,128,1024]{2,1,0:T(8,128)(2,1)}, u32[]{:S(2)}, u32[]{:S(2)}) collective-permute-start(bf16[2,128,1024]{2,1,0:T(8,128)(2,1)} %get-tuple-element.101.refs_3_), channel_id=1, source_target_pairs={{0,1},{1,2},{2,3},{3,4},{4,5},{5,6},{6,7},{7,8},{8,9},{9,10},{10,1... | collective-permute-start | bytes 1572872 | tf_op jit(solution)/shard_map/ppermute | solution.py:939
  42.0 12.2 %collective-permute-start.2 = (bf16[4,160,256]{2,1,0:T(8,128)(2,1)}, bf16[4,160,256]{2,1,0:T(8,128)(2,1)}, u32[]{:S(2)}, u32[]{:S(2)}) collective-permute-start(bf16[4,160,256]{2,1,0:T(8,128)(2,1)} %joined.6.refs_5_.refs_1_), channel_id=1, source_target_pairs={{0,4},{1,5},{2,6},{3,7},{4,0},{5,1},{6,2},{7,3},{8,12},{9,13},{10,... | collective-permute-start | bytes 983048 | tf_op jit(solution)/shard_map/ppermute | solution.py:707
  56.8 11.7 %collective-permute-start.3 = (bf16[4,160,256]{2,1,0:T(8,128)(2,1)}, bf16[4,160,256]{2,1,0:T(8,128)(2,1)}, u32[]{:S(2)}, u32[]{:S(2)}) collective-permute-start(bf16[4,160,256]{2,1,0:T(8,128)(2,1)} %joined.7.refs_5_.refs_1_), channel_id=1, source_target_pairs={{0,8},{1,9},{2,10},{3,11},{4,12},{5,13},{6,14},{7,15},{8,0},{9,1},... | collective-permute-start | bytes 983048 | tf_op jit(solution)/shard_map/ppermute | solution.py:707
  71.1 17.4 %collective-permute-start.4 = (bf16[4,160,256]{2,1,0:T(8,128)(2,1)}, bf16[4,160,256]{2,1,0:T(8,128)(2,1)}, u32[]{:S(2)}, u32[]{:S(2)}) collective-permute-start(bf16[4,160,256]{2,1,0:T(8,128)(2,1)} %joined.8.refs_7_), channel_id=1, source_target_pairs={{0,16},{1,17},{2,18},{3,19},{4,20},{5,21},{6,22},{7,23},{8,24},{9,... | collective-permute-start | bytes 983048 | tf_op jit(solution)/shard_map/ppermute | solution.py:707
  91.4 2.0 collective-permute-start.6
  177.0 17.9 %collective-permute-start.10 = (bf16[2816,512]{1,0:T(8,128)(2,1)}, bf16[2816,512]{1,0:T(8,128)(2,1)}, u32[]{:S(2)}, u32[]{:S(2)}) collective-permute-start(bf16[2816,512]{1,0:T(8,128)(2,1)} %get-tuple-element.115), channel_id=1, source_target_pairs={{0,1},{1,0},{2,3},{3,2},{4,5},{5,4},{6,7},{7,6},{8,9},{9,8},{10,11... | collective-permute-start | bytes 8650760 | tf_op jit(solution)/shard_map/ppermute | solution.py:707
  177.2 17.7 %collective-permute-start.12 = (bf16[512,2816]{1,0:T(8,128)(2,1)}, bf16[512,2816]{1,0:T(8,128)(2,1)}, u32[]{:S(2)}, u32[]{:S(2)}) collective-permute-start(bf16[512,2816]{1,0:T(8,128)(2,1)} %get-tuple-element.119), channel_id=1, source_target_pairs={{0,1},{1,0},{2,3},{3,2},{4,5},{5,4},{6,7},{7,6},{8,9},{9,8},{10,11... | collective-permute-start | bytes 8650760 | tf_op jit(solution)/shard_map/ppermute | solution.py:707
  177.6 17.4 %collective-permute-start.9 = (bf16[512,2816]{1,0:T(8,128)(2,1)}, bf16[512,2816]{1,0:T(8,128)(2,1)}, u32[]{:S(2)}, u32[]{:S(2)}) collective-permute-start(bf16[512,2816]{1,0:T(8,128)(2,1)} %get-tuple-element.113), channel_id=1, source_target_pairs={{0,1},{1,0},{2,3},{3,2},{4,5},{5,4},{6,7},{7,6},{8,9},{9,8},{10,11... | collective-permute-start | bytes 8650760 | tf_op jit(solution)/shard_map/ppermute | solution.py:707
  177.7 17.2 %collective-permute-start.11 = (bf16[512,1024]{1,0:T(8,128)(2,1)}, bf16[512,1024]{1,0:T(8,128)(2,1)}, u32[]{:S(2)}, u32[]{:S(2)}) collective-permute-start(bf16[512,1024]{1,0:T(8,128)(2,1)} %get-tuple-element.117), channel_id=1, source_target_pairs={{0,1},{1,0},{2,3},{3,2},{4,5},{5,4},{6,7},{7,6},{8,9},{9,8},{10,11... | collective-permute-start | bytes 3145736 | tf_op jit(solution)/shard_map/ppermute | solution.py:707
  189.3 3.6 collective-permute-start.7
  189.5 0.5 copy-start
  194.9 10.6 %collective-permute-start.8 = (bf16[4,160,256]{2,1,0:T(8,128)(2,1)}, bf16[4,160,256]{2,1,0:T(8,128)(2,1)}, u32[]{:S(2)}, u32[]{:S(2)}) collective-permute-start(bf16[4,160,256]{2,1,0:T(8,128)(2,1)} %begun.3.refs_26_.refs_1_), channel_id=1, source_target_pairs={{0,2},{1,3},{2,0},{3,1},{4,6},{5,7},{6,4},{7,5},{8,10},{9,11},{10,... | collective-permute-start | bytes 983048 | tf_op jit(solution)/shard_map/ppermute | solution.py:707
  208.1 16.8 %collective-permute-start.13 = (bf16[4,160,256]{2,1,0:T(8,128)(2,1)}, bf16[4,160,256]{2,1,0:T(8,128)(2,1)}, u32[]{:S(2)}, u32[]{:S(2)}) collective-permute-start(bf16[4,160,256]{2,1,0:T(8,128)(2,1)} %get-tuple-element.123.refs_14_.refs_1_), channel_id=1, source_target_pairs={{0,4},{1,5},{2,6},{3,7},{4,0},{5,1},{6,2},{7,3},{8,12},{9,13},{10,... | collective-permute-start | bytes 983048 | tf_op jit(solution)/shard_map/ppermute | solution.py:707
  208.6 65.2 %collective-permute-start.18 = (bf16[8,592,256]{2,1,0:T(8,128)(2,1)}, bf16[8,592,256]{2,1,0:T(8,128)(2,1)}, u32[]{:S(2)}, u32[]{:S(2)}) collective-permute-start(bf16[8,592,256]{2,1,0:T(8,128)(2,1)} %get-tuple-element.140), channel_id=1, source_target_pairs={{0,2},{1,3},{2,0},{3,1},{4,6},{5,7},{6,4},{7,5},{8,10},{9,11},{10,... | collective-permute-start | bytes 7274504 | tf_op jit(solution)/shard_map/ppermute | solution.py:707
  210.6 63.2 %collective-permute-start.19 = (bf16[8,592,256]{2,1,0:T(8,128)(2,1)}, bf16[8,592,256]{2,1,0:T(8,128)(2,1)}, u32[]{:S(2)}, u32[]{:S(2)}) collective-permute-start(bf16[8,592,256]{2,1,0:T(8,128)(2,1)} %get-tuple-element.142), channel_id=1, source_target_pairs={{0,4},{1,5},{2,6},{3,7},{4,0},{5,1},{6,2},{7,3},{8,12},{9,13},{10,... | collective-permute-start | bytes 7274504 | tf_op jit(solution)/shard_map/ppermute | solution.py:707
  223.6 60.9 %collective-permute-start.15 = (bf16[2,128,1024]{2,1,0:T(8,128)(2,1)}, bf16[2,128,1024]{2,1,0:T(8,128)(2,1)}, u32[]{:S(2)}, u32[]{:S(2)}) collective-permute-start(bf16[2,128,1024]{2,1,0:T(8,128)(2,1)} %get-tuple-element.135), channel_id=1, source_target_pairs={{1,0},{2,1},{3,2},{4,3},{5,4},{6,5},{7,6},{8,7},{9,8},{10,9},{11,1... | collective-permute-start | bytes 1572872 | tf_op jit(solution)/shard_map/ppermute | solution.py:963
  227.6 13.1 %collective-permute-start.14 = (bf16[4,160,256]{2,1,0:T(8,128)(2,1)}, bf16[4,160,256]{2,1,0:T(8,128)(2,1)}, u32[]{:S(2)}, u32[]{:S(2)}) collective-permute-start(bf16[4,160,256]{2,1,0:T(8,128)(2,1)} %joined.10.refs_9_.refs_1_), channel_id=1, source_target_pairs={{0,8},{1,9},{2,10},{3,11},{4,12},{5,13},{6,14},{7,15},{8,0},{9,1},... | collective-permute-start | bytes 983048 | tf_op jit(solution)/shard_map/ppermute | solution.py:707
  243.1 27.8 %collective-permute-start.16 = (bf16[4,160,256]{2,1,0:T(8,128)(2,1)}, bf16[4,160,256]{2,1,0:T(8,128)(2,1)}, u32[]{:S(2)}, u32[]{:S(2)}) collective-permute-start(bf16[4,160,256]{2,1,0:T(8,128)(2,1)} %joined.11.refs_10_), channel_id=1, source_target_pairs={{0,16},{1,17},{2,18},{3,19},{4,20},{5,21},{6,22},{7,23},{8,24},{9,... | collective-permute-start | bytes 983048 | tf_op jit(solution)/shard_map/ppermute | solution.py:707
  273.8 10.7 %collective-permute-start.17 = (bf16[4,160,256]{2,1,0:T(8,128)(2,1)}, bf16[4,160,256]{2,1,0:T(8,128)(2,1)}, u32[]{:S(2)}, u32[]{:S(2)}) collective-permute-start(bf16[4,160,256]{2,1,0:T(8,128)(2,1)} %get-tuple-element.137), channel_id=1, source_target_pairs={{0,1},{1,0},{2,3},{3,2},{4,5},{5,4},{6,7},{7,6},{8,9},{9,8},{10,11... | collective-permute-start | bytes 983048 | tf_op jit(solution)/shard_map/ppermute | solution.py:707
  280.3 29.4 %collective-permute-start.21 = (bf16[4,592,256]{2,1,0:T(8,128)(2,1)}, bf16[4,592,256]{2,1,0:T(8,128)(2,1)}, u32[]{:S(2)}, u32[]{:S(2)}) collective-permute-start(bf16[4,592,256]{2,1,0:T(8,128)(2,1)} %bitcast.125), channel_id=1, source_target_pairs={{0,4},{1,5},{2,6},{3,7},{4,0},{5,1},{6,2},{7,3},{8,12},{9,13},{10,... | collective-permute-start | bytes 3637256 | tf_op jit(solution)/shard_map/ppermute | solution.py:707
  280.4 29.9 %collective-permute-start.22 = (bf16[4,592,256]{2,1,0:T(8,128)(2,1)}, bf16[4,592,256]{2,1,0:T(8,128)(2,1)}, u32[]{:S(2)}, u32[]{:S(2)}) collective-permute-start(bf16[4,592,256]{2,1,0:T(8,128)(2,1)} %bitcast.124), channel_id=1, source_target_pairs={{0,2},{1,3},{2,0},{3,1},{4,6},{5,7},{6,4},{7,5},{8,10},{9,11},{10,... | collective-permute-start | bytes 3637256 | tf_op jit(solution)/shard_map/ppermute | solution.py:707
  296.2 25.0 %collective-permute-start.20 = (bf16[512,2560]{1,0:T(8,128)(2,1)}, bf16[512,2560]{1,0:T(8,128)(2,1)}, u32[]{:S(2)}, u32[]{:S(2)}) collective-permute-start(bf16[512,2560]{1,0:T(8,128)(2,1)} %get-tuple-element.148), channel_id=1, source_target_pairs={{0,1},{1,0},{2,3},{3,2},{4,5},{5,4},{6,7},{7,6},{8,9},{9,8},{10,11... | collective-permute-start | bytes 7864328 | tf_op jit(solution)/shard_map/ppermute | solution.py:707
  320.5 19.1 %collective-permute-start.24 = (bf16[512,1536]{1,0:T(8,128)(2,1)}, bf16[512,1536]{1,0:T(8,128)(2,1)}, u32[]{:S(2)}, u32[]{:S(2)}) collective-permute-start(bf16[512,1536]{1,0:T(8,128)(2,1)} %get-tuple-element.156), channel_id=1, source_target_pairs={{0,1},{1,0},{2,3},{3,2},{4,5},{5,4},{6,7},{7,6},{8,9},{9,8},{10,11... | collective-permute-start | bytes 4718600 | tf_op jit(solution)/shard_map/ppermute | solution.py:707
  320.5 29.4 %collective-permute-start.28 = (bf16[2,1184,256]{2,1,0:T(8,128)(2,1)}, bf16[2,1184,256]{2,1,0:T(8,128)(2,1)}, u32[]{:S(2)}, u32[]{:S(2)}) collective-permute-start(bf16[2,1184,256]{2,1,0:T(8,128)(2,1)} %bitcast.123), channel_id=1, source_target_pairs={{0,8},{1,9},{2,10},{3,11},{4,12},{5,13},{6,14},{7,15},{8,0},{9,1},... | collective-permute-start | bytes 3637256 | tf_op jit(solution)/shard_map/ppermute | solution.py:707
  325.7 28.8 %collective-permute-start.23 = (bf16[8,160,256]{2,1,0:T(8,128)(2,1)}, bf16[8,160,256]{2,1,0:T(8,128)(2,1)}, u32[]{:S(2)}, u32[]{:S(2)}) collective-permute-start(bf16[8,160,256]{2,1,0:T(8,128)(2,1)} %bitcast.126), channel_id=1, source_target_pairs={{0,2},{1,3},{2,0},{3,1},{4,6},{5,7},{6,4},{7,5},{8,10},{9,11},{10,... | collective-permute-start | bytes 1966088 | tf_op jit(solution)/shard_map/ppermute | solution.py:707
  327.5 25.2 %collective-permute-start.26 = (bf16[8,128,256]{2,1,0:T(8,128)(2,1)}, bf16[8,128,256]{2,1,0:T(8,128)(2,1)}, u32[]{:S(2)}, u32[]{:S(2)}) collective-permute-start(bf16[8,128,256]{2,1,0:T(8,128)(2,1)} %bitcast.130), channel_id=1, source_target_pairs={{0,4},{1,5},{2,6},{3,7},{4,0},{5,1},{6,2},{7,3},{8,12},{9,13},{10,... | collective-permute-start | bytes 1572872 | tf_op jit(solution)/shard_map/ppermute | solution.py:707
  343.4 11.1 %collective-permute-start.27 = (bf16[8,96,256]{2,1,0:T(8,128)(2,1)}, bf16[8,96,256]{2,1,0:T(8,128)(2,1)}, u32[]{:S(2)}, u32[]{:S(2)}) collective-permute-start(bf16[8,96,256]{2,1,0:T(8,128)(2,1)} %bitcast.135), channel_id=1, source_target_pairs={{0,4},{1,5},{2,6},{3,7},{4,0},{5,1},{6,2},{7,3},{8,12},{9,13},{10,... | collective-permute-start | bytes 1179656 | tf_op jit(solution)/shard_map/ppermute | solution.py:707
  344.1 8.6 %collective-permute-start.25 = (bf16[8,64,256]{2,1,0:T(8,128)(2,1)}, bf16[8,64,256]{2,1,0:T(8,128)(2,1)}, u32[]{:S(2)}, u32[]{:S(2)}) collective-permute-start(bf16[8,64,256]{2,1,0:T(8,128)(2,1)} %bitcast.138), channel_id=1, source_target_pairs={{0,2},{1,3},{2,0},{3,1},{4,6},{5,7},{6,4},{7,5},{8,10},{9,11},{10,... | collective-permute-start | bytes 786440 | tf_op jit(solution)/shard_map/ppermute | solution.py:707
  358.7 14.9 %collective-permute-start.29 = (bf16[4,224,256]{2,1,0:T(8,128)(2,1)}, bf16[4,224,256]{2,1,0:T(8,128)(2,1)}, u32[]{:S(2)}, u32[]{:S(2)}) collective-permute-start(bf16[4,224,256]{2,1,0:T(8,128)(2,1)} %bitcast.132), channel_id=1, source_target_pairs={{0,4},{1,5},{2,6},{3,7},{4,0},{5,1},{6,2},{7,3},{8,12},{9,13},{10,... | collective-permute-start | bytes 1376264 | tf_op jit(solution)/shard_map/ppermute | solution.py:707
  359.4 14.2 %collective-permute-start.30 = (bf16[4,224,256]{2,1,0:T(8,128)(2,1)}, bf16[4,224,256]{2,1,0:T(8,128)(2,1)}, u32[]{:S(2)}, u32[]{:S(2)}) collective-permute-start(bf16[4,224,256]{2,1,0:T(8,128)(2,1)} %bitcast.131), channel_id=1, source_target_pairs={{0,2},{1,3},{2,0},{3,1},{4,6},{5,7},{6,4},{7,5},{8,10},{9,11},{10,... | collective-permute-start | bytes 1376264 | tf_op jit(solution)/shard_map/ppermute | solution.py:707
  360.4 39.7 %collective-permute-start.34 = (bf16[1,1184,256]{2,1,0:T(8,128)(2,1)}, bf16[1,1184,256]{2,1,0:T(8,128)(2,1)}, u32[]{:S(2)}, u32[]{:S(2)}) collective-permute-start(bf16[1,1184,256]{2,1,0:T(8,128)(2,1)} %bitcast.127), channel_id=1, source_target_pairs={{0,16},{1,17},{2,18},{3,19},{4,20},{5,21},{6,22},{7,23},{8,24},{9,... | collective-permute-start | bytes 1818632 | tf_op jit(solution)/shard_map/ppermute | solution.py:707
  376.2 31.0 %collective-permute-start.31 = (bf16[1,448,256]{2,1,0:T(8,128)(2,1)}, bf16[1,448,256]{2,1,0:T(8,128)(2,1)}, u32[]{:S(2)}, u32[]{:S(2)}) collective-permute-start(bf16[1,448,256]{2,1,0:T(8,128)(2,1)} %bitcast.141), channel_id=1, source_target_pairs={{0,24},{1,25},{2,26},{3,27},{4,28},{5,29},{6,30},{7,31},{8,16},{9,... | collective-permute-start | bytes 688136 | tf_op jit(solution)/shard_map/ppermute | solution.py:842
  377.0 32.0 %collective-permute-start.32 = (bf16[1,448,256]{2,1,0:T(8,128)(2,1)}, bf16[1,448,256]{2,1,0:T(8,128)(2,1)}, u32[]{:S(2)}, u32[]{:S(2)}) collective-permute-start(bf16[1,448,256]{2,1,0:T(8,128)(2,1)} %bitcast.140), channel_id=1, source_target_pairs={{0,16},{1,17},{2,18},{3,19},{4,20},{5,21},{6,22},{7,23},{8,24},{9,... | collective-permute-start | bytes 688136 | tf_op jit(solution)/shard_map/ppermute | solution.py:842
  379.1 30.0 %collective-permute-start.33 = (bf16[1,448,256]{2,1,0:T(8,128)(2,1)}, bf16[1,448,256]{2,1,0:T(8,128)(2,1)}, u32[]{:S(2)}, u32[]{:S(2)}) collective-permute-start(bf16[1,448,256]{2,1,0:T(8,128)(2,1)} %bitcast.139), channel_id=1, source_target_pairs={{0,8},{1,9},{2,10},{3,11},{4,12},{5,13},{6,14},{7,15},{8,0},{9,1},... | collective-permute-start | bytes 688136 | tf_op jit(solution)/shard_map/ppermute | solution.py:842
  411.3 2.1 collective-permute-start.35

commit v3 on v2

--- a/solution.py
+++ b/solution.py
@@ -695,13 +695,12 @@
     c = grad * gain[...]
     out[...] = resid[...] + scale * c - x * (scale * scale * scale * jnp.mean(c * x, axis=-1, keepdims=True))
 
-def input_grad(parts, w_in, tokens, gain, resid, part, ways, name, deps=(), into=None):
+def input_grad(parts, w_in, tokens, gain, resid, piece=512):
     toks, width = tokens.shape
-    piece = toks // ways
-    by_rows = lambda columns: pl.BlockSpec((piece, columns), lambda s: (part, 0), **ONE)
-    return call(input_kernel, name, (1,),
+    by_rows = lambda columns: pl.BlockSpec((piece, columns), lambda s: (s, 0))
+    return call(input_kernel, "input_grad", (toks // piece,),
         [(p, by_rows(p.shape[1])) for p in parts] + [(w_in, resident(w_in.shape)), (tokens, by_rows(width)), (gain.reshape(1, width), resident((1, width))), (resid, by_rows(width))],
-        [((toks, width), F32, by_rows(width))], flops=2 * piece * width * w_in.shape[1], deps=deps, into=into)
+        [((toks, width), F32, by_rows(width))])[0]
 
 def swap(x, bit, count):
     return lax.ppermute(x, "seq", [(i, i ^ (1 << bit)) for i in range(count)])
@@ -834,9 +833,13 @@
             (ka, sa), (kb, sb) = add_up([([Piece(self.a)], chips // 4, 1, (me >> 2) & 1), ([Piece(self.b)], chips // 4, 1, (me >> 1) & 1)], 2, "sum_second")
             self.a, self.b = [ka, swap(sa, 2, self.count)], [kb, swap(sb, 1, self.count)]
         else:
-            pieces = [Piece(self.a), Piece(self.b)] if self.bit == 3 else [Piece(self.all)]
-            (k, s), = add_up([(pieces, chips >> self.bit, 1, (me >> self.bit) & 1)], 2, "sum_more")
-            self.all = [k, swap(s, self.bit, self.count)]
+            got, = add_up([self.group()], 2, "sum_more")
+            self.send(got)
+    def group(self):
+        pieces = [Piece(self.a), Piece(self.b)] if self.bit == 3 else [Piece(self.all)]
+        return pieces, self.chips >> self.bit, 1, (self.me >> self.bit) & 1
+    def send(self, got):
+        self.all = [got[0], swap(got[1], self.bit, self.count)]
 
 def quarters(pieces, bit, me, count):
     flip = lambda x, k: lax.ppermute(x, "seq", [(i, i ^ (k << bit)) for i in range(count)])
@@ -855,10 +858,12 @@
         a, b = ([Piece(arrays, first, size) for first, size in c] for c in columns)
         (ka, sa), (kb, sb), *self.through = add_up([(a, chips // 2, 1, (me >> 1) & 1), (b, chips // 4, 2, (me >> 2) & 1)], 2, "in_first", through=through)
         return [ka, swap(sa, 1, self.count)], [kb, swap(sb, 2, self.count)]
-    def third(self, *parts):
+    def third(self, mlp_sum, *parts):
         me, chips = self.me, self.chips
         a, b = ([Piece(p[n]) for p in parts] for n in (0, 1))
-        (ka, sa), (kb, sb) = add_up([(a, chips // 4, 1, (me >> 2) & 1), (b, chips // 4, 1, (me >> 1) & 1)], 2, "in_second")
+        mlp_sum.bit += 1
+        (ka, sa), (kb, sb), got = add_up([(a, chips // 4, 1, (me >> 2) & 1), (b, chips // 4, 1, (me >> 1) & 1), mlp_sum.group()], 2, "in_second")
+        mlp_sum.send(got)
         self.arrays = [Piece([ka, swap(sa, 2, self.count)]), Piece([kb, swap(sb, 1, self.count)])]
         self.bit = 3
     def rest(self):
@@ -976,12 +981,11 @@
     late = in_sum.first(*weight_grad(core, p.normed_t, [dv, dk_lin], count, "weight_grad_late"), (((0, width // 2),), ((width // 2, width // 2), (width, lin))))
     parts = [dq_lin, dk_lin, dq_win, dk_win, dv]
     early = in_sum.second(*early)
-    grad_tokens = input_grad(parts, w_in, x, gain_in, grad_resid, 0, 2, "input_grad_first")
     late = in_sum.second(*late)
-    while mlp_sum.bit < bits - 1:
+    while mlp_sum.bit < bits - 2:
         mlp_sum.step()
-    in_sum.third(early, late)
-    grad_tokens, = input_grad(parts, w_in, x, gain_in, grad_resid, 1, 2, "input_grad", into=grad_tokens)
+    in_sum.third(mlp_sum, early, late)
+    grad_tokens = input_grad(parts, w_in, x, gain_in, grad_resid)
     in_got = in_sum.rest()
     ff, each, chip = w_down.shape[0], width // count, w_down.shape[0] // (count // 2)
     pad = padded(each)

time: 421 us -> 419 us (level)
  Pallas kernels: 314 us -> 305 us
  waiting for transfers between devices: 48 us -> 52.4 us
    pallas_call x40 -> x38, Pallas kernels: 314 us -> 305 us  [call(): pl.pallas_call(body, grid_spec=pltpu.PrefetchScalarGridSpec(num_scalar_pr...]
    ppermute x31, waiting for transfers between devices: 46.1 us -> 50.5 us  [swap(): return lax.ppermute(x, 'seq', [(i, i ^ 1 << bit) for i in range(count)])]
  transfers between devices with their start and end apart: 36 -> 36, of which waited for: 12 -> 12; matrix products, arithmetic and copies ran while one was open for 1% -> 1% of each run, Pallas kernels for 48% -> 47%
where the time goes in v3:
time: 419 us; the launch traced here: 413 us
  Pallas kernels  305 us (73%)
  waiting for transfers between devices  52.4 us (13%)
  starting transfers between devices  43 us (10%)
  other arithmetic  7.07 us (2%)
    pallas_call x38, Pallas kernels, call(): pl.pallas_call(body, grid_spec=pltpu.PrefetchScalarGridSpec(num_scalar_pr...  305 us
    ppermute x31, waiting for transfers between devices, swap(): return lax.ppermute(x, 'seq', [(i, i ^ 1 << bit) for i in range(count)])  50.5 us
    ppermute x31, starting transfers between devices, swap(): return lax.ppermute(x, 'seq', [(i, i ^ 1 << bit) for i in range(count)])  34.2 us
  transfers between devices with their start and end apart: 36, of which 12 were waited for; matrix products, arithmetic and copies ran while one was open for 1% of the time, Pallas kernels for 47%

profile of v3, /device:TPU:0, one launch (start us, length us, event | category | flops | bytes accessed | tf_op | source)
XLA Modules:
  0.0 412.8 jit_solution(4196248436269330779)
XLA Ops:
  3.0 6.7 %project_keys.1 = (bf16[1024,1024]{1,0:T(8,128)(2,1)}, bf16[1024,256]{1,0:T(8,128)(2,1)}, bf16[1024,1024]{1,0:T(8,128)(2,1)}, bf16[2,128,1024]{2,1,0:T(8,128)(2,1)}) custom-call(bf16[1024,1024]{1,0:T(8,128)(2,1)} %bitcast.107, f32[1,1024]{1,0:T(1,128)} %bitcast.117, bf16[1024,3584]{1,0:T(8,128)(2,1)} %refs_1_.5, bf16[1024,3584]{1,0:T(8,128)(2,1)} %refs_1_.5), custom_call_target="tpu_custom_call" | custom-call | flops 6800000000 | bytes 1000 | tf_op jit(solution)/shard_map/project_keys/pallas_call | solution.py:144
  9.7 8.0 %state.1 = (f32[4,160,256]{2,1,0:T(8,128)}, bf16[4,160,256]{2,1,0:T(8,128)(2,1)}) custom-call(s32[1]{0:T(128)} %bitcast.refs_0_, s32[16]{0:T(128)} %copy-done.2, s32[16]{0:T(128)} %add.19.refs_2_.refs_1_, bf16[1024,256]{1,0:T(8,128)(2,1)} %get-tuple-element.96.refs_3_.refs_4_, bf16[1024,1024]{1,0:T(8,128)(2,1)} %get-tuple-element.97.refs_4_.refs_10_.refs_5_, ...), custom_call_target="tpu_custom_call" | custom-call | flops 7400000000 | bytes 1000 | tf_op jit(solution)/shard_map/state/pallas_call | solution.py:144
  19.2 3.2 project_queries.1.refs_3_.refs_2_
  22.4 2.0 begun.2.refs_3_.refs_1_
  24.5 2.5 collective-permute-start.1
  27.0 9.5 %project_rest.1 = (bf16[2,128,1024]{2,1,0:T(8,128)(2,1)}, bf16[1024,2048]{1,0:T(8,128)(2,1)}, bf16[1024,1024]{1,0:T(8,128)(2,1)}) custom-call(bf16[1024,1024]{1,0:T(8,128)(2,1)} %get-tuple-element.95.refs_5_.refs_0_.refs_1_, bf16[1024,1024]{1,0:T(8,128)(2,1)} %get-tuple-element.95.refs_5_.refs_0_.refs_1_, ...), custom_call_target="tpu_custom_call", output_to_operand_aliasing={{0}: (4, {})} | custom-call | flops 10000000000 | bytes 1000 | tf_op jit(solution)/shard_map/project_rest/pallas_call | solution.py:144
  36.5 3.0 collective-permute-start.5
  39.5 2.6 joined.6.refs_5_.refs_1_
  42.9 6.3 %intra.2.refs_3_.refs_6_ = bf16[1024,1024]{1,0:T(8,128)(2,1)} custom-call(s32[16]{0:T(128)} %copy-done.2, s32[16]{0:T(128)} %add.19.refs_2_.refs_1_, bf16[1024,256]{1,0:T(8,128)(2,1)} %project_queries.1.refs_3_.refs_2_, bf16[1024,256]{1,0:T(8,128)(2,1)} %get-tuple-element.96.refs_3_.refs_4_, bf16[1024,1024]{1,0:T(8,128)(2,1)} %get-tuple-element.97.refs_4_.refs_10_.refs_5_, ...), custom_call_target="tpu_custom_call" | custom-call | flops 7200000000 | bytes 1000 | tf_op jit(solution)/shard_map/intra/pallas_call | solution.py:144
  49.2 5.0 %collective-permute-done.2.refs_2_.refs_5_ = bf16[4,160,256]{2,1,0:T(8,128)(2,1)} collective-permute-done((bf16[4,160,256]{2,1,0:T(8,128)(2,1)}, bf16[4,160,256]{2,1,0:T(8,128)(2,1)}, u32[]{:S(2)}, u32[]{:S(2)}) %collective-permute-start.2) | collective-permute-done | bytes 327712 | tf_op jit(solution)/shard_map/ppermute | solution.py:706
  54.2 2.6 joined.7.refs_5_.refs_1_
  56.8 3.4 collective-permute-start.3
  60.3 6.3 %intra.3.refs_3_.refs_5_ = bf16[1024,1024]{1,0:T(8,128)(2,1)} custom-call(s32[16]{0:T(128)} %copy-done.2, s32[16]{0:T(128)} %add.19.refs_2_.refs_1_, bf16[1024,256]{1,0:T(8,128)(2,1)} %project_queries.1.refs_3_.refs_2_, bf16[1024,256]{1,0:T(8,128)(2,1)} %get-tuple-element.96.refs_3_.refs_4_, ...), custom_call_target="tpu_custom_call", output_to_operand_aliasing={{}: (6, {})} | custom-call | flops 7200000000 | bytes 1000 | tf_op jit(solution)/shard_map/intra/pallas_call | solution.py:144
  66.6 2.0 collective-permute-done.3.refs_2_.refs_6_
  68.5 2.6 joined.8.refs_7_
  71.1 2.8 collective-permute-start.4
  73.9 10.6 %window.1.refs_8_.refs_6_ = bf16[1024,1024]{1,0:T(8,128)(2,1)} custom-call(s32[16]{0:T(128)} %copy-done.2, s32[16]{0:T(128)} %add.19.refs_2_.refs_1_, bf16[1024,2048]{1,0:T(8,128)(2,1)} %get-tuple-element.102.refs_2_.refs_3_.refs_8_.refs_9_, bf16[1024,2048]{1,0:T(8,128)(2,1)} %get-tuple-element.102.refs_2_.refs_3_.refs_8_.refs_9_, ...), custom_call_target="tpu_custom_call" | custom-call | flops 12000000000 | bytes 1000 | tf_op jit(solution)/shard_map/window/pallas_call | solution.py:144
  84.5 4.1 collective-permute-done.4.refs_7_
  88.5 2.9 ended.2
  91.4 2.0 collective-permute-done.6.refs_4_.refs_9_
  93.3 8.7 %mix.1 = (bf16[1024,1024]{1,0:T(8,128)(2,1)}, bf16[1024,1024]{1,0:T(8,128)(2,1)}) custom-call(s32[1]{0:T(128)} %bitcast.refs_0_, s32[16]{0:T(128)} %copy-done.2, bf16[1024,256]{1,0:T(8,128)(2,1)} %project_queries.1.refs_3_.refs_2_, bf16[4,160,256]{2,1,0:T(8,128)(2,1)} %get-tuple-element.103.refs_3_.refs_8_, ...), custom_call_target="tpu_custom_call" | custom-call | flops 10000000000 | bytes 1000 | tf_op jit(solution)/shard_map/mix/pallas_call | solution.py:144
  102.0 74.9 %mlp.1 = (bf16[1024,1024]{1,0:T(8,128)(2,1)}, f32[1024,1024]{1,0:T(8,128)}, bf16[1024,1024]{1,0:T(8,128)(2,1)}, bf16[512,2816]{1,0:T(8,128)(2,1)}, bf16[512,2816...) custom-call(s32[1]{0:T(128)} %bitcast.refs_0_, ...), custom_call_target="tpu_custom_call" | custom-call | flops 88000004096 | bytes 1000 | tf_op jit(solution)/shard_map/mlp/pallas_call | solution.py:144
  178.1 11.3 %numer_back.1 = (bf16[1024,1024]{1,0:T(8,128)(2,1)}, f32[4,160,256]{2,1,0:T(8,128)}, bf16[4,160,256]{2,1,0:T(8,128)(2,1)}) custom-call(s32[1]{0:T(128)} %bitcast.refs_0_, s32[16]{0:T(128)} %copy-done.2, bf16[1024,256]{1,0:T(8,128)(2,1)} %project_queries.1.refs_3_.refs_2_, bf16[1024,1024]{1,0:T(8,128)(2,1)} %get-tuple-element.106.refs_9_.refs_3_, ...), custom_call_target="tpu_custom_call" | custom-call | flops 12000000000 | bytes 1000 | tf_op jit(solution)/shard_map/numer_back/pallas_call | solution.py:144
  190.6 2.3 collective-permute-done.7.refs_2_.refs_3_
  192.9 2.0 begun.3.refs_26_.refs_1_
  194.9 10.6 %sum_first.1 = (bf16[8,1,592,256]{3,2,1,0:T(8,128)(2,1)}, bf16[8,1,592,256]{3,2,1,0:T(8,128)(2,1)}, bf16[4,2,592,256]{3,2,1,0:T(8,128)(2,1)}, bf16[4,2,592,256]{3,2,1,0:T(8,128)(2,1)}) custom-call(s32[1]{0:T(128)} %bitcast.6.refs_0_.refs_1_, s32[1]{0:T(128)} %bitcast.7.refs_1_.refs_0_, bf16[8,2,1,32,2816]{4,3,2,1,0:T(8,128)(2,1)} %bitcast.92, ...), custom_call_target="tpu_custom_call" | custom-call | flops 10599999488 | bytes 1000 | tf_op jit(solution)/shard_map/sum_first/pallas_call | solution.py:144
  205.6 2.6 joined.9
  208.6 2.0 collective-permute-start.18
  210.6 1.6 collective-permute-start.19
  212.2 11.5 %window_back.2 = (bf16[1024,1024]{1,0:T(8,128)(2,1)}, bf16[1024,1024]{1,0:T(8,128)(2,1)}, bf16[1024,1024]{1,0:T(8,128)(2,1)}, bf16[2,128,1024]{2,1,0:T(8,128)(2,...) custom-call(s32[16]{0:T(128)} %copy-done.2, s32[16]{0:T(128)} %add.19.refs_2_.refs_1_, ...), custom_call_target="tpu_custom_call" | custom-call | flops 12999999488 | bytes 1000 | tf_op jit(solution)/shard_map/window_back/pallas_call | solution.py:144
  223.7 1.3 collective-permute-start.15
  225.0 2.5 joined.10.refs_9_.refs_1_
  228.6 11.4 %window_back.3 = (bf16[1024,1024]{1,0:T(8,128)(2,1)}, bf16[1024,1024]{1,0:T(8,128)(2,1)}, bf16[1024,1024]{1,0:T(8,128)(2,1)}) custom-call(s32[16]{0:T(128)} %copy-done.2, s32[16]{0:T(128)} %add.19.refs_2_.refs_1_, ...), custom_call_target="tpu_custom_call", output_to_operand_aliasing={{0}: (10, {}), {1}: (11, {}), {2}: (12, {})} | custom-call | flops 12999999488 | bytes 1000 | tf_op jit(solution)/shard_map/window_back/pallas_call | solution.py:144
  240.6 2.5 joined.11.refs_10_
  243.2 3.4 collective-permute-start.16
  246.6 24.4 %intra_back.1 = (bf16[1024,256]{1,0:T(8,128)(2,1)}, f32[2,256,512]{2,1,0:T(8,128)}, bf16[1024,1024]{1,0:T(8,128)(2,1)}) custom-call(s32[1]{0:T(128)} %bitcast.refs_0_, s32[16]{0:T(128)} %copy-done.2, s32[16]{0:T(128)} %add.19.refs_2_.refs_1_, bf16[1024,256]{1,0:T(8,128)(2,1)} %project_queries.1.refs_3_.refs_2_, ...), custom_call_target="tpu_custom_call" | custom-call | flops 24999999488 | bytes 1000 | tf_op jit(solution)/shard_map/intra_back/pallas_call | solution.py:144
  270.9 2.9 ended.3
  273.8 6.5 %sum_second.1 = (bf16[4,1,592,256]{3,2,1,0:T(8,128)(2,1)}, bf16[4,1,592,256]{3,2,1,0:T(8,128)(2,1)}, bf16[4,1,592,256]{3,2,1,0:T(8,128)(2,1)}, bf16[4,1,592,256]{3,2,1,0:T(8,128)(2,1)}) custom-call(s32[1]{0:T(128)} %bitcast.7.refs_1_.refs_0_, s32[1]{0:T(128)} %bitcast.6.refs_0_.refs_1_, bf16[4,2,1,592,256]{4,3,2,1,0:T(8,128)(2,1)} %bitcast.120, ...), custom_call_target="tpu_custom_call" | custom-call | flops 6400000000 | bytes 1000 | tf_op jit(solution)/shard_map/sum_second/pallas_call | solution.py:144
  280.4 4.1 %collective-permute-start.22 = (bf16[4,592,256]{2,1,0:T(8,128)(2,1)}, bf16[4,592,256]{2,1,0:T(8,128)(2,1)}, u32[]{:S(2)}, u32[]{:S(2)}) collective-permute-start(bf16[4,592,256]{2,1,0:T(8,128)(2,1)} %bitcast.128), channel_id=1, source_target_pairs={{0,2},{1,3},{2,0},{3,1},{4,6},{5,7},{6,4},{7,5},{8,10},{9,11},{10,... | collective-permute-start | bytes 3637256 | tf_op jit(solution)/shard_map/ppermute | solution.py:706
  284.5 1.8 tail.1.refs_3_
  286.3 9.9 %weight_grad_early.1 = (bf16[512,2560]{1,0:T(8,128)(2,1)}, bf16[512,2560]{1,0:T(8,128)(2,1)}) custom-call(s32[1]{0:T(128)} %bitcast.refs_0_, bf16[1024,1024]{1,0:T(8,128)(2,1)} %get-tuple-element.138.refs_1_, bf16[1024,1024]{1,0:T(8,128)(2,1)} %get-tuple-element.131.refs_3_.refs_2_, bf16[1024,1024]{1,0:T(8,128)(2,1)} %tail.1.refs_3_, ...), custom_call_target="tpu_custom_call" | custom-call | flops 100000000 | bytes 1000 | tf_op jit(solution)/shard_map/weight_grad_early/pallas_call | solution.py:144
  296.2 10.8 %state_back.1 = (bf16[1024,256]{1,0:T(8,128)(2,1)}, bf16[1024,1024]{1,0:T(8,128)(2,1)}) custom-call(s32[1]{0:T(128)} %bitcast.refs_0_, s32[16]{0:T(128)} %copy-done.2, s32[16]{0:T(128)} %add.19.refs_2_.refs_1_, bf16[1024,256]{1,0:T(8,128)(2,1)} %get-tuple-element.96.refs_3_.refs_4_, bf16[1024,1024]{1,0:T(8,128)(2,1)} %get-tuple-element.97.refs_4_.refs_10_.refs_5_, ...), custom_call_target="tpu_custom_call" | custom-call | flops 100000000 | bytes 1000 | tf_op jit(solution)/shard_map/state_back/pallas_call | solution.py:144
  307.0 2.7 collective-permute-done.21
  310.4 3.7 sum_more.1
  314.1 6.5 %weight_grad_late.1 = (bf16[512,1536]{1,0:T(8,128)(2,1)}, bf16[512,1536]{1,0:T(8,128)(2,1)}) custom-call(s32[1]{0:T(128)} %bitcast.refs_0_, bf16[1024,1024]{1,0:T(8,128)(2,1)} %get-tuple-element.138.refs_1_, bf16[1024,1024]{1,0:T(8,128)(2,1)} %get-tuple-element.146.refs_2_.refs_4_, bf16[1024,256]{1,0:T(8,128)(2,1)} %get-tuple-element.145.refs_9_.refs_3_.refs_1_, ...), custom_call_target="tpu_custom_call" | custom-call | flops 100000000 | bytes 1000 | tf_op jit(solution)/shard_map/weight_grad_late/pallas_call | solution.py:144
  321.2 4.5 %in_first.2 = (bf16[8,1,160,256]{3,2,1,0:T(8,128)(2,1)}, bf16[8,1,160,256]{3,2,1,0:T(8,128)(2,1)}, bf16[4,2,128,256]{3,2,1,0:T(8,128)(2,1)}, bf16[4,2,128,256]{3,2,1,0:T(8,128)(2,1)}) custom-call(s32[1]{0:T(128)} %bitcast.6.refs_0_.refs_1_, s32[1]{0:T(128)} %bitcast.7.refs_1_.refs_0_, bf16[8,2,1,32,2560]{4,3,2,1,0:T(8,128)(2,1)} %bitcast.72, ...), custom_call_target="tpu_custom_call" | custom-call | flops 3000000000 | bytes 1000 | tf_op jit(solution)/shard_map/in_first/pallas_call | solution.py:144
  325.7 1.8 collective-permute-start.23
  327.5 1.4 collective-permute-start.26
  329.0 3.7 in_first.3
  333.7 16.3 %collective-permute-done.28 = bf16[2,1184,256]{2,1,0:T(8,128)(2,1)} collective-permute-done((bf16[2,1184,256]{2,1,0:T(8,128)(2,1)}, bf16[2,1184,256]{2,1,0:T(8,128)(2,1)}, u32[]{:S(2)}, u32[]{:S(2)}) %collective-permute-start.28) | collective-permute-done | bytes 1212448 | tf_op jit(solution)/shard_map/ppermute | solution.py:706
  350.1 4.5 %in_second.1 = (bf16[4,1,224,256]{3,2,1,0:T(8,128)(2,1)}, bf16[4,1,224,256]{3,2,1,0:T(8,128)(2,1)}, bf16[4,1,224,256]{3,2,1,0:T(8,128)(2,1)}, bf16[4,1,224,256]{...) custom-call(s32[1]{0:T(128)} %bitcast.7.refs_1_.refs_0_, ...), custom_call_target="tpu_custom_call" | custom-call | flops 3000000000 | bytes 1000 | tf_op jit(solution)/shard_map/in_second/pallas_call | solution.py:144
  354.6 1.5 collective-permute-start.29
  356.1 1.7 collective-permute-start.30
  357.9 2.2 collective-permute-start.34
  360.0 15.8 %input_grad.1.refs_17_ = f32[1024,1024]{1,0:T(8,128)} custom-call(bf16[1024,256]{1,0:T(8,128)(2,1)} %get-tuple-element.132.refs_8_.refs_4_.refs_0_, bf16[1024,256]{1,0:T(8,128)(2,1)} %get-tuple-element.145.refs_9_.refs_3_.refs_1_, bf16[1024,1024]{1,0:T(8,128)(2,1)} %get-tuple-element.131.refs_3_.refs_2_, bf16[1024,1024]{1,0:T(8,128)(2,1)} %tail.1.refs_3_, ...), custom_call_target="tpu_custom_call" | custom-call | flops 100000000 | bytes 1000 | tf_op jit(solution)/shard_map/input_grad/pallas_call | solution.py:144
  375.8 2.5 quarters.1
  379.6 2.0 collective-permute-start.32
  382.8 14.8 %collective-permute-done.34.refs_3_.refs_2_ = bf16[1,1184,256]{2,1,0:T(8,128)(2,1)} collective-permute-done((bf16[1,1184,256]{2,1,0:T(8,128)(2,1)}, bf16[1,1184,256]{2,1,0:T(8,128)(2,1)}, u32[]{:S(2)}, u32[]{:S(2)}) %collective-permute-start.34) | collective-permute-done | bytes 606240 | tf_op jit(solution)/shard_map/ppermute | solution.py:706
  397.6 2.4 gathered.2
  399.9 1.3 reduce.1
  401.3 2.1 plain.1
  403.3 1.3 dynamic-slice_divide_fusion
  404.6 1.9 collective-permute-done.32.refs_4_
  406.5 2.3 gathered.3
  (68 shorter events, 18.1 us)
Async XLA Ops:
  1.5 0.9 copy-start.2
  17.6 4.8 %collective-permute-start = (bf16[4,160,256]{2,1,0:T(8,128)(2,1)}, bf16[4,160,256]{2,1,0:T(8,128)(2,1)}, u32[]{:S(2)}, u32[]{:S(2)}) collective-permute-start(bf16[4,160,256]{2,1,0:T(8,128)(2,1)} %get-tuple-element.99), channel_id=1, source_target_pairs={{0,1},{1,0},{2,3},{3,2},{4,5},{5,4},{6,7},{7,6},{8,9},{9,8},{10,11... | collective-permute-start | bytes 983048 | tf_op jit(solution)/shard_map/ppermute | solution.py:706
  18.1 0.5 copy-start.1
  24.5 15.1 %collective-permute-start.1 = (bf16[4,160,256]{2,1,0:T(8,128)(2,1)}, bf16[4,160,256]{2,1,0:T(8,128)(2,1)}, u32[]{:S(2)}, u32[]{:S(2)}) collective-permute-start(bf16[4,160,256]{2,1,0:T(8,128)(2,1)} %begun.2.refs_3_.refs_1_), channel_id=1, source_target_pairs={{0,2},{1,3},{2,0},{3,1},{4,6},{5,7},{6,4},{7,5},{8,10},{9,11},{10,... | collective-permute-start | bytes 983048 | tf_op jit(solution)/shard_map/ppermute | solution.py:706
  36.5 37.4 %collective-permute-start.5 = (bf16[2,128,1024]{2,1,0:T(8,128)(2,1)}, bf16[2,128,1024]{2,1,0:T(8,128)(2,1)}, u32[]{:S(2)}, u32[]{:S(2)}) collective-permute-start(bf16[2,128,1024]{2,1,0:T(8,128)(2,1)} %get-tuple-element.101.refs_3_), channel_id=1, source_target_pairs={{0,1},{1,2},{2,3},{3,4},{4,5},{5,6},{6,7},{7,8},{8,9},{9,10},{10,1... | collective-permute-start | bytes 1572872 | tf_op jit(solution)/shard_map/ppermute | solution.py:944
  42.1 12.1 %collective-permute-start.2 = (bf16[4,160,256]{2,1,0:T(8,128)(2,1)}, bf16[4,160,256]{2,1,0:T(8,128)(2,1)}, u32[]{:S(2)}, u32[]{:S(2)}) collective-permute-start(bf16[4,160,256]{2,1,0:T(8,128)(2,1)} %joined.6.refs_5_.refs_1_), channel_id=1, source_target_pairs={{0,4},{1,5},{2,6},{3,7},{4,0},{5,1},{6,2},{7,3},{8,12},{9,13},{10,... | collective-permute-start | bytes 983048 | tf_op jit(solution)/shard_map/ppermute | solution.py:706
  56.8 11.7 %collective-permute-start.3 = (bf16[4,160,256]{2,1,0:T(8,128)(2,1)}, bf16[4,160,256]{2,1,0:T(8,128)(2,1)}, u32[]{:S(2)}, u32[]{:S(2)}) collective-permute-start(bf16[4,160,256]{2,1,0:T(8,128)(2,1)} %joined.7.refs_5_.refs_1_), channel_id=1, source_target_pairs={{0,8},{1,9},{2,10},{3,11},{4,12},{5,13},{6,14},{7,15},{8,0},{9,1},... | collective-permute-start | bytes 983048 | tf_op jit(solution)/shard_map/ppermute | solution.py:706
  71.1 17.4 %collective-permute-start.4 = (bf16[4,160,256]{2,1,0:T(8,128)(2,1)}, bf16[4,160,256]{2,1,0:T(8,128)(2,1)}, u32[]{:S(2)}, u32[]{:S(2)}) collective-permute-start(bf16[4,160,256]{2,1,0:T(8,128)(2,1)} %joined.8.refs_7_), channel_id=1, source_target_pairs={{0,16},{1,17},{2,18},{3,19},{4,20},{5,21},{6,22},{7,23},{8,24},{9,... | collective-permute-start | bytes 983048 | tf_op jit(solution)/shard_map/ppermute | solution.py:706
  91.4 2.0 collective-permute-start.6
  177.0 17.9 %collective-permute-start.10 = (bf16[2816,512]{1,0:T(8,128)(2,1)}, bf16[2816,512]{1,0:T(8,128)(2,1)}, u32[]{:S(2)}, u32[]{:S(2)}) collective-permute-start(bf16[2816,512]{1,0:T(8,128)(2,1)} %get-tuple-element.115), channel_id=1, source_target_pairs={{0,1},{1,0},{2,3},{3,2},{4,5},{5,4},{6,7},{7,6},{8,9},{9,8},{10,11... | collective-permute-start | bytes 8650760 | tf_op jit(solution)/shard_map/ppermute | solution.py:706
  177.2 17.7 %collective-permute-start.12 = (bf16[512,2816]{1,0:T(8,128)(2,1)}, bf16[512,2816]{1,0:T(8,128)(2,1)}, u32[]{:S(2)}, u32[]{:S(2)}) collective-permute-start(bf16[512,2816]{1,0:T(8,128)(2,1)} %get-tuple-element.119), channel_id=1, source_target_pairs={{0,1},{1,0},{2,3},{3,2},{4,5},{5,4},{6,7},{7,6},{8,9},{9,8},{10,11... | collective-permute-start | bytes 8650760 | tf_op jit(solution)/shard_map/ppermute | solution.py:706
  177.6 17.4 %collective-permute-start.9 = (bf16[512,2816]{1,0:T(8,128)(2,1)}, bf16[512,2816]{1,0:T(8,128)(2,1)}, u32[]{:S(2)}, u32[]{:S(2)}) collective-permute-start(bf16[512,2816]{1,0:T(8,128)(2,1)} %get-tuple-element.113), channel_id=1, source_target_pairs={{0,1},{1,0},{2,3},{3,2},{4,5},{5,4},{6,7},{7,6},{8,9},{9,8},{10,11... | collective-permute-start | bytes 8650760 | tf_op jit(solution)/shard_map/ppermute | solution.py:706
  177.7 17.2 %collective-permute-start.11 = (bf16[512,1024]{1,0:T(8,128)(2,1)}, bf16[512,1024]{1,0:T(8,128)(2,1)}, u32[]{:S(2)}, u32[]{:S(2)}) collective-permute-start(bf16[512,1024]{1,0:T(8,128)(2,1)} %get-tuple-element.117), channel_id=1, source_target_pairs={{0,1},{1,0},{2,3},{3,2},{4,5},{5,4},{6,7},{7,6},{8,9},{9,8},{10,11... | collective-permute-start | bytes 3145736 | tf_op jit(solution)/shard_map/ppermute | solution.py:706
  189.3 3.6 collective-permute-start.7
  189.5 0.5 copy-start
  194.9 10.7 %collective-permute-start.8 = (bf16[4,160,256]{2,1,0:T(8,128)(2,1)}, bf16[4,160,256]{2,1,0:T(8,128)(2,1)}, u32[]{:S(2)}, u32[]{:S(2)}) collective-permute-start(bf16[4,160,256]{2,1,0:T(8,128)(2,1)} %begun.3.refs_26_.refs_1_), channel_id=1, source_target_pairs={{0,2},{1,3},{2,0},{3,1},{4,6},{5,7},{6,4},{7,5},{8,10},{9,11},{10,... | collective-permute-start | bytes 983048 | tf_op jit(solution)/shard_map/ppermute | solution.py:706
  208.2 16.8 %collective-permute-start.13 = (bf16[4,160,256]{2,1,0:T(8,128)(2,1)}, bf16[4,160,256]{2,1,0:T(8,128)(2,1)}, u32[]{:S(2)}, u32[]{:S(2)}) collective-permute-start(bf16[4,160,256]{2,1,0:T(8,128)(2,1)} %get-tuple-element.123.refs_14_.refs_1_), channel_id=1, source_target_pairs={{0,4},{1,5},{2,6},{3,7},{4,0},{5,1},{6,2},{7,3},{8,12},{9,13},{10,... | collective-permute-start | bytes 983048 | tf_op jit(solution)/shard_map/ppermute | solution.py:706
  208.6 65.2 %collective-permute-start.18 = (bf16[8,592,256]{2,1,0:T(8,128)(2,1)}, bf16[8,592,256]{2,1,0:T(8,128)(2,1)}, u32[]{:S(2)}, u32[]{:S(2)}) collective-permute-start(bf16[8,592,256]{2,1,0:T(8,128)(2,1)} %get-tuple-element.140), channel_id=1, source_target_pairs={{0,2},{1,3},{2,0},{3,1},{4,6},{5,7},{6,4},{7,5},{8,10},{9,11},{10,... | collective-permute-start | bytes 7274504 | tf_op jit(solution)/shard_map/ppermute | solution.py:706
  210.6 63.2 %collective-permute-start.19 = (bf16[8,592,256]{2,1,0:T(8,128)(2,1)}, bf16[8,592,256]{2,1,0:T(8,128)(2,1)}, u32[]{:S(2)}, u32[]{:S(2)}) collective-permute-start(bf16[8,592,256]{2,1,0:T(8,128)(2,1)} %get-tuple-element.142), channel_id=1, source_target_pairs={{0,4},{1,5},{2,6},{3,7},{4,0},{5,1},{6,2},{7,3},{8,12},{9,13},{10,... | collective-permute-start | bytes 7274504 | tf_op jit(solution)/shard_map/ppermute | solution.py:706
  223.7 60.8 %collective-permute-start.15 = (bf16[2,128,1024]{2,1,0:T(8,128)(2,1)}, bf16[2,128,1024]{2,1,0:T(8,128)(2,1)}, u32[]{:S(2)}, u32[]{:S(2)}) collective-permute-start(bf16[2,128,1024]{2,1,0:T(8,128)(2,1)} %get-tuple-element.135), channel_id=1, source_target_pairs={{1,0},{2,1},{3,2},{4,3},{5,4},{6,5},{7,6},{8,7},{9,8},{10,9},{11,1... | collective-permute-start | bytes 1572872 | tf_op jit(solution)/shard_map/ppermute | solution.py:968
  227.5 13.2 %collective-permute-start.14 = (bf16[4,160,256]{2,1,0:T(8,128)(2,1)}, bf16[4,160,256]{2,1,0:T(8,128)(2,1)}, u32[]{:S(2)}, u32[]{:S(2)}) collective-permute-start(bf16[4,160,256]{2,1,0:T(8,128)(2,1)} %joined.10.refs_9_.refs_1_), channel_id=1, source_target_pairs={{0,8},{1,9},{2,10},{3,11},{4,12},{5,13},{6,14},{7,15},{8,0},{9,1},... | collective-permute-start | bytes 983048 | tf_op jit(solution)/shard_map/ppermute | solution.py:706
  243.2 27.7 %collective-permute-start.16 = (bf16[4,160,256]{2,1,0:T(8,128)(2,1)}, bf16[4,160,256]{2,1,0:T(8,128)(2,1)}, u32[]{:S(2)}, u32[]{:S(2)}) collective-permute-start(bf16[4,160,256]{2,1,0:T(8,128)(2,1)} %joined.11.refs_10_), channel_id=1, source_target_pairs={{0,16},{1,17},{2,18},{3,19},{4,20},{5,21},{6,22},{7,23},{8,24},{9,... | collective-permute-start | bytes 983048 | tf_op jit(solution)/shard_map/ppermute | solution.py:706
  273.8 10.7 %collective-permute-start.17 = (bf16[4,160,256]{2,1,0:T(8,128)(2,1)}, bf16[4,160,256]{2,1,0:T(8,128)(2,1)}, u32[]{:S(2)}, u32[]{:S(2)}) collective-permute-start(bf16[4,160,256]{2,1,0:T(8,128)(2,1)} %get-tuple-element.137), channel_id=1, source_target_pairs={{0,1},{1,0},{2,3},{3,2},{4,5},{5,4},{6,7},{7,6},{8,9},{9,8},{10,11... | collective-permute-start | bytes 983048 | tf_op jit(solution)/shard_map/ppermute | solution.py:706
  280.3 29.4 %collective-permute-start.21 = (bf16[4,592,256]{2,1,0:T(8,128)(2,1)}, bf16[4,592,256]{2,1,0:T(8,128)(2,1)}, u32[]{:S(2)}, u32[]{:S(2)}) collective-permute-start(bf16[4,592,256]{2,1,0:T(8,128)(2,1)} %bitcast.129), channel_id=1, source_target_pairs={{0,4},{1,5},{2,6},{3,7},{4,0},{5,1},{6,2},{7,3},{8,12},{9,13},{10,... | collective-permute-start | bytes 3637256 | tf_op jit(solution)/shard_map/ppermute | solution.py:706
  280.4 30.0 %collective-permute-start.22 = (bf16[4,592,256]{2,1,0:T(8,128)(2,1)}, bf16[4,592,256]{2,1,0:T(8,128)(2,1)}, u32[]{:S(2)}, u32[]{:S(2)}) collective-permute-start(bf16[4,592,256]{2,1,0:T(8,128)(2,1)} %bitcast.128), channel_id=1, source_target_pairs={{0,2},{1,3},{2,0},{3,1},{4,6},{5,7},{6,4},{7,5},{8,10},{9,11},{10,... | collective-permute-start | bytes 3637256 | tf_op jit(solution)/shard_map/ppermute | solution.py:706
  296.2 25.0 %collective-permute-start.20 = (bf16[512,2560]{1,0:T(8,128)(2,1)}, bf16[512,2560]{1,0:T(8,128)(2,1)}, u32[]{:S(2)}, u32[]{:S(2)}) collective-permute-start(bf16[512,2560]{1,0:T(8,128)(2,1)} %get-tuple-element.148), channel_id=1, source_target_pairs={{0,1},{1,0},{2,3},{3,2},{4,5},{5,4},{6,7},{7,6},{8,9},{9,8},{10,11... | collective-permute-start | bytes 7864328 | tf_op jit(solution)/shard_map/ppermute | solution.py:706
  320.5 8.4 %collective-permute-start.24 = (bf16[512,1536]{1,0:T(8,128)(2,1)}, bf16[512,1536]{1,0:T(8,128)(2,1)}, u32[]{:S(2)}, u32[]{:S(2)}) collective-permute-start(bf16[512,1536]{1,0:T(8,128)(2,1)} %get-tuple-element.156), channel_id=1, source_target_pairs={{0,1},{1,0},{2,3},{3,2},{4,5},{5,4},{6,7},{7,6},{8,9},{9,8},{10,11... | collective-permute-start | bytes 4718600 | tf_op jit(solution)/shard_map/ppermute | solution.py:706
  320.5 29.4 %collective-permute-start.28 = (bf16[2,1184,256]{2,1,0:T(8,128)(2,1)}, bf16[2,1184,256]{2,1,0:T(8,128)(2,1)}, u32[]{:S(2)}, u32[]{:S(2)}) collective-permute-start(bf16[2,1184,256]{2,1,0:T(8,128)(2,1)} %bitcast.127), channel_id=1, source_target_pairs={{0,8},{1,9},{2,10},{3,11},{4,12},{5,13},{6,14},{7,15},{8,0},{9,1},... | collective-permute-start | bytes 3637256 | tf_op jit(solution)/shard_map/ppermute | solution.py:706
  325.7 24.3 %collective-permute-start.23 = (bf16[8,160,256]{2,1,0:T(8,128)(2,1)}, bf16[8,160,256]{2,1,0:T(8,128)(2,1)}, u32[]{:S(2)}, u32[]{:S(2)}) collective-permute-start(bf16[8,160,256]{2,1,0:T(8,128)(2,1)} %bitcast.130), channel_id=1, source_target_pairs={{0,2},{1,3},{2,0},{3,1},{4,6},{5,7},{6,4},{7,5},{8,10},{9,11},{10,... | collective-permute-start | bytes 1966088 | tf_op jit(solution)/shard_map/ppermute | solution.py:706
  327.5 22.4 %collective-permute-start.26 = (bf16[8,128,256]{2,1,0:T(8,128)(2,1)}, bf16[8,128,256]{2,1,0:T(8,128)(2,1)}, u32[]{:S(2)}, u32[]{:S(2)}) collective-permute-start(bf16[8,128,256]{2,1,0:T(8,128)(2,1)} %bitcast.132), channel_id=1, source_target_pairs={{0,4},{1,5},{2,6},{3,7},{4,0},{5,1},{6,2},{7,3},{8,12},{9,13},{10,... | collective-permute-start | bytes 1572872 | tf_op jit(solution)/shard_map/ppermute | solution.py:706
  332.7 17.3 %collective-permute-start.27 = (bf16[8,96,256]{2,1,0:T(8,128)(2,1)}, bf16[8,96,256]{2,1,0:T(8,128)(2,1)}, u32[]{:S(2)}, u32[]{:S(2)}) collective-permute-start(bf16[8,96,256]{2,1,0:T(8,128)(2,1)} %bitcast.139), channel_id=1, source_target_pairs={{0,4},{1,5},{2,6},{3,7},{4,0},{5,1},{6,2},{7,3},{8,12},{9,13},{10,... | collective-permute-start | bytes 1179656 | tf_op jit(solution)/shard_map/ppermute | solution.py:706
  333.4 16.6 %collective-permute-start.25 = (bf16[8,64,256]{2,1,0:T(8,128)(2,1)}, bf16[8,64,256]{2,1,0:T(8,128)(2,1)}, u32[]{:S(2)}, u32[]{:S(2)}) collective-permute-start(bf16[8,64,256]{2,1,0:T(8,128)(2,1)} %bitcast.140), channel_id=1, source_target_pairs={{0,2},{1,3},{2,0},{3,1},{4,6},{5,7},{6,4},{7,5},{8,10},{9,11},{10,... | collective-permute-start | bytes 786440 | tf_op jit(solution)/shard_map/ppermute | solution.py:706
  354.6 21.2 %collective-permute-start.29 = (bf16[4,224,256]{2,1,0:T(8,128)(2,1)}, bf16[4,224,256]{2,1,0:T(8,128)(2,1)}, u32[]{:S(2)}, u32[]{:S(2)}) collective-permute-start(bf16[4,224,256]{2,1,0:T(8,128)(2,1)} %bitcast.138), channel_id=1, source_target_pairs={{0,4},{1,5},{2,6},{3,7},{4,0},{5,1},{6,2},{7,3},{8,12},{9,13},{10,... | collective-permute-start | bytes 1376264 | tf_op jit(solution)/shard_map/ppermute | solution.py:706
  356.1 19.7 %collective-permute-start.30 = (bf16[4,224,256]{2,1,0:T(8,128)(2,1)}, bf16[4,224,256]{2,1,0:T(8,128)(2,1)}, u32[]{:S(2)}, u32[]{:S(2)}) collective-permute-start(bf16[4,224,256]{2,1,0:T(8,128)(2,1)} %bitcast.137), channel_id=1, source_target_pairs={{0,2},{1,3},{2,0},{3,1},{4,6},{5,7},{6,4},{7,5},{8,10},{9,11},{10,... | collective-permute-start | bytes 1376264 | tf_op jit(solution)/shard_map/ppermute | solution.py:706
  357.9 39.7 %collective-permute-start.34 = (bf16[1,1184,256]{2,1,0:T(8,128)(2,1)}, bf16[1,1184,256]{2,1,0:T(8,128)(2,1)}, u32[]{:S(2)}, u32[]{:S(2)}) collective-permute-start(bf16[1,1184,256]{2,1,0:T(8,128)(2,1)} %bitcast.131), channel_id=1, source_target_pairs={{0,16},{1,17},{2,18},{3,19},{4,20},{5,21},{6,22},{7,23},{8,24},{9,... | collective-permute-start | bytes 1818632 | tf_op jit(solution)/shard_map/ppermute | solution.py:706
  378.4 26.2 %collective-permute-start.31 = (bf16[1,448,256]{2,1,0:T(8,128)(2,1)}, bf16[1,448,256]{2,1,0:T(8,128)(2,1)}, u32[]{:S(2)}, u32[]{:S(2)}) collective-permute-start(bf16[1,448,256]{2,1,0:T(8,128)(2,1)} %bitcast.143), channel_id=1, source_target_pairs={{0,24},{1,25},{2,26},{3,27},{4,28},{5,29},{6,30},{7,31},{8,16},{9,... | collective-permute-start | bytes 688136 | tf_op jit(solution)/shard_map/ppermute | solution.py:845
  379.6 26.9 %collective-permute-start.32 = (bf16[1,448,256]{2,1,0:T(8,128)(2,1)}, bf16[1,448,256]{2,1,0:T(8,128)(2,1)}, u32[]{:S(2)}, u32[]{:S(2)}) collective-permute-start(bf16[1,448,256]{2,1,0:T(8,128)(2,1)} %bitcast.142), channel_id=1, source_target_pairs={{0,16},{1,17},{2,18},{3,19},{4,20},{5,21},{6,22},{7,23},{8,24},{9,... | collective-permute-start | bytes 688136 | tf_op jit(solution)/shard_map/ppermute | solution.py:845
  381.6 24.9 %collective-permute-start.33 = (bf16[1,448,256]{2,1,0:T(8,128)(2,1)}, bf16[1,448,256]{2,1,0:T(8,128)(2,1)}, u32[]{:S(2)}, u32[]{:S(2)}) collective-permute-start(bf16[1,448,256]{2,1,0:T(8,128)(2,1)} %bitcast.141), channel_id=1, source_target_pairs={{0,8},{1,9},{2,10},{3,11},{4,12},{5,13},{6,14},{7,15},{8,0},{9,1},... | collective-permute-start | bytes 688136 | tf_op jit(solution)/shard_map/ppermute | solution.py:845
  408.8 2.1 collective-permute-start.35

commit v4 on v3

--- a/solution.py
+++ b/solution.py
@@ -130,7 +130,7 @@
     count, ahead = len(arrays), len(scalars)
     into = list(into or ())
     deps = list(deps)
-    if Order.last is not None and not any(Order.last is a for a in into + deps + arrays):
+    if Order.last is not None and not any(Order.last is a for a in into + deps + arrays + list(through)):
         deps.append(Order.last)
     extra = deps + into + list(through)
     aliases = {ahead + count + len(deps) + n: n for n in range(len(into))}
@@ -941,8 +941,8 @@
     project_rest(p, w_in, rows)
     forward = [(i, i + 1) for i in range(count - 1)]
     backward = [(i + 1, i) for i in range(count - 1)]
-    halo = lax.ppermute(p.tails, "seq", forward)
-    scan.step()
+    scan.step(through=(p.tails,))
+    halo = lax.ppermute(scan.through[0], "seq", forward)
     local = intra(low, high, p, rows, length, 0)
     scan.step()
     local, = intra(low, high, p, rows, length, 1, into=local)

time: 419 us -> 414 us (0.988)
  transfers between devices with their start and end apart: 36 -> 36, of which waited for: 12 -> 11; matrix products, arithmetic and copies ran while one was open for 1% -> 1% of each run, Pallas kernels for 47% -> 47%
where the time goes in v4:
time: 414 us; the launch traced here: 407 us
  Pallas kernels  305 us (74%)
  waiting for transfers between devices  48.8 us (12%)
  starting transfers between devices  40.7 us (10%)
  other arithmetic  7 us (2%)
    pallas_call x38, Pallas kernels, call(): pl.pallas_call(body, grid_spec=pltpu.PrefetchScalarGridSpec(num_scalar_pr...  305 us
    ppermute x31, waiting for transfers between devices, swap(): return lax.ppermute(x, 'seq', [(i, i ^ 1 << bit) for i in range(count)])  47.1 us
    ppermute x31, starting transfers between devices, swap(): return lax.ppermute(x, 'seq', [(i, i ^ 1 << bit) for i in range(count)])  32.2 us
  transfers between devices with their start and end apart: 36, of which 11 were waited for; matrix products, arithmetic and copies ran while one was open for 1% of the time, Pallas kernels for 47%

profile of v4, /device:TPU:0, one launch (start us, length us, event | category | flops | bytes accessed | tf_op | source)
XLA Modules:
  0.0 407.0 jit_solution(6179642941400237847)
XLA Ops:
  2.9 6.7 %project_keys.1 = (bf16[1024,1024]{1,0:T(8,128)(2,1)}, bf16[1024,256]{1,0:T(8,128)(2,1)}, bf16[1024,1024]{1,0:T(8,128)(2,1)}, bf16[2,128,1024]{2,1,0:T(8,128)(2,1)}) custom-call(bf16[1024,1024]{1,0:T(8,128)(2,1)} %bitcast.107, f32[1,1024]{1,0:T(1,128)} %bitcast.117, bf16[1024,3584]{1,0:T(8,128)(2,1)} %refs_1_.5, bf16[1024,3584]{1,0:T(8,128)(2,1)} %refs_1_.5), custom_call_target="tpu_custom_call" | custom-call | flops 6800000000 | bytes 1000 | tf_op jit(solution)/shard_map/project_keys/pallas_call | solution.py:144
  9.6 8.0 %state.1 = (f32[4,160,256]{2,1,0:T(8,128)}, bf16[4,160,256]{2,1,0:T(8,128)(2,1)}) custom-call(s32[1]{0:T(128)} %bitcast.refs_0_, s32[16]{0:T(128)} %copy-done.2, s32[16]{0:T(128)} %add.19.refs_2_.refs_1_, bf16[1024,256]{1,0:T(8,128)(2,1)} %get-tuple-element.98.refs_3_.refs_4_, bf16[1024,1024]{1,0:T(8,128)(2,1)} %get-tuple-element.99.refs_4_.refs_10_.refs_5_, ...), custom_call_target="tpu_custom_call" | custom-call | flops 7400000000 | bytes 1000 | tf_op jit(solution)/shard_map/state/pallas_call | solution.py:144
  19.2 3.2 project_queries.1.refs_3_.refs_2_
  22.4 2.0 begun.2.refs_3_.refs_1_
  24.4 2.5 collective-permute-start.1
  26.9 9.5 %project_rest.1 = (bf16[2,128,1024]{2,1,0:T(8,128)(2,1)}, bf16[1024,2048]{1,0:T(8,128)(2,1)}, bf16[1024,1024]{1,0:T(8,128)(2,1)}) custom-call(bf16[1024,1024]{1,0:T(8,128)(2,1)} %get-tuple-element.97.refs_5_.refs_0_.refs_1_, bf16[1024,1024]{1,0:T(8,128)(2,1)} %get-tuple-element.97.refs_5_.refs_0_.refs_1_, ...), custom_call_target="tpu_custom_call", output_to_operand_aliasing={{0}: (4, {})} | custom-call | flops 10000000000 | bytes 1000 | tf_op jit(solution)/shard_map/project_rest/pallas_call | solution.py:144
  36.4 2.5 joined.6
  38.9 1.5 collective-permute-start.2
  40.4 6.3 %intra.2.refs_3_.refs_6_ = bf16[1024,1024]{1,0:T(8,128)(2,1)} custom-call(s32[16]{0:T(128)} %copy-done.2, s32[16]{0:T(128)} %add.19.refs_2_.refs_1_, bf16[1024,256]{1,0:T(8,128)(2,1)} %project_queries.1.refs_3_.refs_2_, bf16[1024,256]{1,0:T(8,128)(2,1)} %get-tuple-element.98.refs_3_.refs_4_, bf16[1024,1024]{1,0:T(8,128)(2,1)} %get-tuple-element.99.refs_4_.refs_10_.refs_5_, ...), custom_call_target="tpu_custom_call" | custom-call | flops 7200000000 | bytes 1000 | tf_op jit(solution)/shard_map/intra/pallas_call | solution.py:144
  46.7 2.8 collective-permute-start.5
  49.5 2.6 joined.7.refs_5_.refs_1_
  53.3 6.3 %intra.3.refs_3_.refs_5_ = bf16[1024,1024]{1,0:T(8,128)(2,1)} custom-call(s32[16]{0:T(128)} %copy-done.2, s32[16]{0:T(128)} %add.19.refs_2_.refs_1_, bf16[1024,256]{1,0:T(8,128)(2,1)} %project_queries.1.refs_3_.refs_2_, bf16[1024,256]{1,0:T(8,128)(2,1)} %get-tuple-element.98.refs_3_.refs_4_, ...), custom_call_target="tpu_custom_call", output_to_operand_aliasing={{}: (6, {})} | custom-call | flops 7200000000 | bytes 1000 | tf_op jit(solution)/shard_map/intra/pallas_call | solution.py:144
  59.6 2.8 collective-permute-done.3.refs_2_.refs_6_
  62.4 2.6 joined.8.refs_7_
  65.0 2.6 collective-permute-start.4
  67.6 10.6 %window.1.refs_8_.refs_6_ = bf16[1024,1024]{1,0:T(8,128)(2,1)} custom-call(s32[16]{0:T(128)} %copy-done.2, s32[16]{0:T(128)} %add.19.refs_2_.refs_1_, bf16[1024,2048]{1,0:T(8,128)(2,1)} %get-tuple-element.105.refs_2_.refs_3_.refs_8_.refs_9_, bf16[1024,2048]{1,0:T(8,128)(2,1)} %get-tuple-element.105.refs_2_.refs_3_.refs_8_.refs_9_, ...), custom_call_target="tpu_custom_call" | custom-call | flops 12000000000 | bytes 1000 | tf_op jit(solution)/shard_map/window/pallas_call | solution.py:144
  78.2 4.5 %collective-permute-done.4.refs_7_ = bf16[4,160,256]{2,1,0:T(8,128)(2,1)} collective-permute-done((bf16[4,160,256]{2,1,0:T(8,128)(2,1)}, bf16[4,160,256]{2,1,0:T(8,128)(2,1)}, u32[]{:S(2)}, u32[]{:S(2)}) %collective-permute-start.4) | collective-permute-done | bytes 327712 | tf_op jit(solution)/shard_map/ppermute | solution.py:706
  82.8 2.9 ended.2
  85.6 2.0 collective-permute-done.6.refs_4_.refs_9_
  87.6 8.7 %mix.1 = (bf16[1024,1024]{1,0:T(8,128)(2,1)}, bf16[1024,1024]{1,0:T(8,128)(2,1)}) custom-call(s32[1]{0:T(128)} %bitcast.refs_0_, s32[16]{0:T(128)} %copy-done.2, bf16[1024,256]{1,0:T(8,128)(2,1)} %project_queries.1.refs_3_.refs_2_, bf16[4,160,256]{2,1,0:T(8,128)(2,1)} %get-tuple-element.107.refs_3_.refs_8_, ...), custom_call_target="tpu_custom_call" | custom-call | flops 10000000000 | bytes 1000 | tf_op jit(solution)/shard_map/mix/pallas_call | solution.py:144
  96.3 75.0 %mlp.1 = (bf16[1024,1024]{1,0:T(8,128)(2,1)}, f32[1024,1024]{1,0:T(8,128)}, bf16[1024,1024]{1,0:T(8,128)(2,1)}, bf16[512,2816]{1,0:T(8,128)(2,1)}, bf16[512,2816...) custom-call(s32[1]{0:T(128)} %bitcast.refs_0_, ...), custom_call_target="tpu_custom_call" | custom-call | flops 88000004096 | bytes 1000 | tf_op jit(solution)/shard_map/mlp/pallas_call | solution.py:144
  172.3 11.3 %numer_back.1 = (bf16[1024,1024]{1,0:T(8,128)(2,1)}, f32[4,160,256]{2,1,0:T(8,128)}, bf16[4,160,256]{2,1,0:T(8,128)(2,1)}) custom-call(s32[1]{0:T(128)} %bitcast.refs_0_, s32[16]{0:T(128)} %copy-done.2, bf16[1024,256]{1,0:T(8,128)(2,1)} %project_queries.1.refs_3_.refs_2_, bf16[1024,1024]{1,0:T(8,128)(2,1)} %get-tuple-element.110.refs_9_.refs_3_, ...), custom_call_target="tpu_custom_call" | custom-call | flops 12000000000 | bytes 1000 | tf_op jit(solution)/shard_map/numer_back/pallas_call | solution.py:144
  184.9 2.2 collective-permute-done.7.refs_2_.refs_3_
  187.2 2.0 begun.3.refs_26_.refs_1_
  190.1 10.6 %sum_first.1 = (bf16[8,1,592,256]{3,2,1,0:T(8,128)(2,1)}, bf16[8,1,592,256]{3,2,1,0:T(8,128)(2,1)}, bf16[4,2,592,256]{3,2,1,0:T(8,128)(2,1)}, bf16[4,2,592,256]{3,2,1,0:T(8,128)(2,1)}) custom-call(s32[1]{0:T(128)} %bitcast.6.refs_0_.refs_1_, s32[1]{0:T(128)} %bitcast.7.refs_1_.refs_0_, bf16[8,2,1,32,2816]{4,3,2,1,0:T(8,128)(2,1)} %bitcast.92, ...), custom_call_target="tpu_custom_call" | custom-call | flops 10599999488 | bytes 1000 | tf_op jit(solution)/shard_map/sum_first/pallas_call | solution.py:144
  200.7 2.6 joined.9
  204.4 2.0 collective-permute-start.19
  206.4 11.5 %window_back.2 = (bf16[1024,1024]{1,0:T(8,128)(2,1)}, bf16[1024,1024]{1,0:T(8,128)(2,1)}, bf16[1024,1024]{1,0:T(8,128)(2,1)}, bf16[2,128,1024]{2,1,0:T(8,128)(2,...) custom-call(s32[16]{0:T(128)} %copy-done.2, s32[16]{0:T(128)} %add.19.refs_2_.refs_1_, ...), custom_call_target="tpu_custom_call" | custom-call | flops 12999999488 | bytes 1000 | tf_op jit(solution)/shard_map/window_back/pallas_call | solution.py:144
  217.9 1.3 collective-permute-start.15
  219.2 2.6 joined.10.refs_9_.refs_1_
  221.8 2.3 collective-permute-start.14
  224.1 11.4 %window_back.3 = (bf16[1024,1024]{1,0:T(8,128)(2,1)}, bf16[1024,1024]{1,0:T(8,128)(2,1)}, bf16[1024,1024]{1,0:T(8,128)(2,1)}) custom-call(s32[16]{0:T(128)} %copy-done.2, s32[16]{0:T(128)} %add.19.refs_2_.refs_1_, ...), custom_call_target="tpu_custom_call", output_to_operand_aliasing={{0}: (10, {}), {1}: (11, {}), {2}: (12, {})} | custom-call | flops 12999999488 | bytes 1000 | tf_op jit(solution)/shard_map/window_back/pallas_call | solution.py:144
  236.0 2.5 joined.11.refs_10_
  238.5 2.4 collective-permute-start.16
  240.9 24.4 %intra_back.1 = (bf16[1024,256]{1,0:T(8,128)(2,1)}, f32[2,256,512]{2,1,0:T(8,128)}, bf16[1024,1024]{1,0:T(8,128)(2,1)}) custom-call(s32[1]{0:T(128)} %bitcast.refs_0_, s32[16]{0:T(128)} %copy-done.2, s32[16]{0:T(128)} %add.19.refs_2_.refs_1_, bf16[1024,256]{1,0:T(8,128)(2,1)} %project_queries.1.refs_3_.refs_2_, ...), custom_call_target="tpu_custom_call" | custom-call | flops 24999999488 | bytes 1000 | tf_op jit(solution)/shard_map/intra_back/pallas_call | solution.py:144
  265.3 2.9 ended.3
  268.2 6.5 %sum_second.1 = (bf16[4,1,592,256]{3,2,1,0:T(8,128)(2,1)}, bf16[4,1,592,256]{3,2,1,0:T(8,128)(2,1)}, bf16[4,1,592,256]{3,2,1,0:T(8,128)(2,1)}, bf16[4,1,592,256]{3,2,1,0:T(8,128)(2,1)}) custom-call(s32[1]{0:T(128)} %bitcast.7.refs_1_.refs_0_, s32[1]{0:T(128)} %bitcast.6.refs_0_.refs_1_, bf16[4,2,1,592,256]{4,3,2,1,0:T(8,128)(2,1)} %bitcast.120, ...), custom_call_target="tpu_custom_call" | custom-call | flops 6400000000 | bytes 1000 | tf_op jit(solution)/shard_map/sum_second/pallas_call | solution.py:144
  275.2 3.5 collective-permute-start.22
  278.7 1.8 tail.1.refs_3_
  280.6 9.9 %weight_grad_early.1 = (bf16[512,2560]{1,0:T(8,128)(2,1)}, bf16[512,2560]{1,0:T(8,128)(2,1)}) custom-call(s32[1]{0:T(128)} %bitcast.refs_0_, bf16[1024,1024]{1,0:T(8,128)(2,1)} %get-tuple-element.142.refs_1_, bf16[1024,1024]{1,0:T(8,128)(2,1)} %get-tuple-element.135.refs_3_.refs_2_, bf16[1024,1024]{1,0:T(8,128)(2,1)} %tail.1.refs_3_, ...), custom_call_target="tpu_custom_call" | custom-call | flops 100000000 | bytes 1000 | tf_op jit(solution)/shard_map/weight_grad_early/pallas_call | solution.py:144
  290.4 10.8 %state_back.1 = (bf16[1024,256]{1,0:T(8,128)(2,1)}, bf16[1024,1024]{1,0:T(8,128)(2,1)}) custom-call(s32[1]{0:T(128)} %bitcast.refs_0_, s32[16]{0:T(128)} %copy-done.2, s32[16]{0:T(128)} %add.19.refs_2_.refs_1_, bf16[1024,256]{1,0:T(8,128)(2,1)} %get-tuple-element.98.refs_3_.refs_4_, bf16[1024,1024]{1,0:T(8,128)(2,1)} %get-tuple-element.99.refs_4_.refs_10_.refs_5_, ...), custom_call_target="tpu_custom_call" | custom-call | flops 100000000 | bytes 1000 | tf_op jit(solution)/shard_map/state_back/pallas_call | solution.py:144
  301.2 2.9 collective-permute-done.21
  305.1 3.7 sum_more.1
  308.8 6.4 %weight_grad_late.1 = (bf16[512,1536]{1,0:T(8,128)(2,1)}, bf16[512,1536]{1,0:T(8,128)(2,1)}) custom-call(s32[1]{0:T(128)} %bitcast.refs_0_, bf16[1024,1024]{1,0:T(8,128)(2,1)} %get-tuple-element.142.refs_1_, bf16[1024,1024]{1,0:T(8,128)(2,1)} %get-tuple-element.150.refs_2_.refs_4_, bf16[1024,256]{1,0:T(8,128)(2,1)} %get-tuple-element.149.refs_9_.refs_3_.refs_1_, ...), custom_call_target="tpu_custom_call" | custom-call | flops 100000000 | bytes 1000 | tf_op jit(solution)/shard_map/weight_grad_late/pallas_call | solution.py:144
  316.2 4.5 %in_first.2 = (bf16[8,1,160,256]{3,2,1,0:T(8,128)(2,1)}, bf16[8,1,160,256]{3,2,1,0:T(8,128)(2,1)}, bf16[4,2,128,256]{3,2,1,0:T(8,128)(2,1)}, bf16[4,2,128,256]{3,2,1,0:T(8,128)(2,1)}) custom-call(s32[1]{0:T(128)} %bitcast.6.refs_0_.refs_1_, s32[1]{0:T(128)} %bitcast.7.refs_1_.refs_0_, bf16[8,2,1,32,2560]{4,3,2,1,0:T(8,128)(2,1)} %bitcast.72, ...), custom_call_target="tpu_custom_call" | custom-call | flops 3000000000 | bytes 1000 | tf_op jit(solution)/shard_map/in_first/pallas_call | solution.py:144
  320.7 1.8 collective-permute-start.23
  323.4 3.7 in_first.3
  327.2 1.2 collective-permute-start.27
  328.6 16.0 %collective-permute-done.28 = bf16[2,1184,256]{2,1,0:T(8,128)(2,1)} collective-permute-done((bf16[2,1184,256]{2,1,0:T(8,128)(2,1)}, bf16[2,1184,256]{2,1,0:T(8,128)(2,1)}, u32[]{:S(2)}, u32[]{:S(2)}) %collective-permute-start.28) | collective-permute-done | bytes 1212448 | tf_op jit(solution)/shard_map/ppermute | solution.py:706
  345.0 4.5 %in_second.1 = (bf16[4,1,224,256]{3,2,1,0:T(8,128)(2,1)}, bf16[4,1,224,256]{3,2,1,0:T(8,128)(2,1)}, bf16[4,1,224,256]{3,2,1,0:T(8,128)(2,1)}, bf16[4,1,224,256]{...) custom-call(s32[1]{0:T(128)} %bitcast.7.refs_1_.refs_0_, ...), custom_call_target="tpu_custom_call" | custom-call | flops 3000000000 | bytes 1000 | tf_op jit(solution)/shard_map/in_second/pallas_call | solution.py:144
  350.4 1.6 collective-permute-start.30
  352.1 2.4 collective-permute-start.34
  354.4 15.8 %input_grad.1.refs_17_ = f32[1024,1024]{1,0:T(8,128)} custom-call(bf16[1024,256]{1,0:T(8,128)(2,1)} %get-tuple-element.136.refs_8_.refs_4_.refs_0_, bf16[1024,256]{1,0:T(8,128)(2,1)} %get-tuple-element.149.refs_9_.refs_3_.refs_1_, bf16[1024,1024]{1,0:T(8,128)(2,1)} %get-tuple-element.135.refs_3_.refs_2_, bf16[1024,1024]{1,0:T(8,128)(2,1)} %tail.1.refs_3_, ...), custom_call_target="tpu_custom_call" | custom-call | flops 100000000 | bytes 1000 | tf_op jit(solution)/shard_map/input_grad/pallas_call | solution.py:144
  370.3 2.6 quarters.1
  372.8 1.2 collective-permute-start.31
  374.0 2.0 collective-permute-start.32
  377.2 14.7 %collective-permute-done.34.refs_3_.refs_2_ = bf16[1,1184,256]{2,1,0:T(8,128)(2,1)} collective-permute-done((bf16[1,1184,256]{2,1,0:T(8,128)(2,1)}, bf16[1,1184,256]{2,1,0:T(8,128)(2,1)}, u32[]{:S(2)}, u32[]{:S(2)}) %collective-permute-start.34) | collective-permute-done | bytes 606240 | tf_op jit(solution)/shard_map/ppermute | solution.py:706
  391.9 2.4 gathered.2
  394.3 1.3 reduce.1
  395.6 2.1 plain.1
  397.7 1.3 dynamic-slice_divide_fusion
  399.0 1.7 collective-permute-done.32.refs_4_
  400.7 2.3 gathered.3
  403.8 1.3 dynamic-slice_divide_fusion.1
  (68 shorter events, 18.6 us)
Async XLA Ops:
  1.5 0.9 copy-start.2
  17.6 4.8 %collective-permute-start = (bf16[4,160,256]{2,1,0:T(8,128)(2,1)}, bf16[4,160,256]{2,1,0:T(8,128)(2,1)}, u32[]{:S(2)}, u32[]{:S(2)}) collective-permute-start(bf16[4,160,256]{2,1,0:T(8,128)(2,1)} %get-tuple-element.101), channel_id=1, source_target_pairs={{0,1},{1,0},{2,3},{3,2},{4,5},{5,4},{6,7},{7,6},{8,9},{9,8},{10,11... | collective-permute-start | bytes 983048 | tf_op jit(solution)/shard_map/ppermute | solution.py:706
  18.0 0.5 copy-start.1
  24.4 12.0 %collective-permute-start.1 = (bf16[4,160,256]{2,1,0:T(8,128)(2,1)}, bf16[4,160,256]{2,1,0:T(8,128)(2,1)}, u32[]{:S(2)}, u32[]{:S(2)}) collective-permute-start(bf16[4,160,256]{2,1,0:T(8,128)(2,1)} %begun.2.refs_3_.refs_1_), channel_id=1, source_target_pairs={{0,2},{1,3},{2,0},{3,1},{4,6},{5,7},{6,4},{7,5},{8,10},{9,11},{10,... | collective-permute-start | bytes 983048 | tf_op jit(solution)/shard_map/ppermute | solution.py:706
  38.9 10.6 %collective-permute-start.2 = (bf16[4,160,256]{2,1,0:T(8,128)(2,1)}, bf16[4,160,256]{2,1,0:T(8,128)(2,1)}, u32[]{:S(2)}, u32[]{:S(2)}) collective-permute-start(bf16[4,160,256]{2,1,0:T(8,128)(2,1)} %get-tuple-element.104.refs_5_.refs_1_), channel_id=1, source_target_pairs={{0,4},{1,5},{2,6},{3,7},{4,0},{5,1},{6,2},{7,3},{8,12},{9,13},{10,... | collective-permute-start | bytes 983048 | tf_op jit(solution)/shard_map/ppermute | solution.py:706
  46.7 20.9 %collective-permute-start.5 = (bf16[2,128,1024]{2,1,0:T(8,128)(2,1)}, bf16[2,128,1024]{2,1,0:T(8,128)(2,1)}, u32[]{:S(2)}, u32[]{:S(2)}) collective-permute-start(bf16[2,128,1024]{2,1,0:T(8,128)(2,1)} %get-tuple-element.106), channel_id=1, source_target_pairs={{0,1},{1,2},{2,3},{3,4},{4,5},{5,6},{6,7},{7,8},{8,9},{9,10},{10,1... | collective-permute-start | bytes 1572872 | tf_op jit(solution)/shard_map/ppermute | solution.py:945
  52.1 10.3 %collective-permute-start.3 = (bf16[4,160,256]{2,1,0:T(8,128)(2,1)}, bf16[4,160,256]{2,1,0:T(8,128)(2,1)}, u32[]{:S(2)}, u32[]{:S(2)}) collective-permute-start(bf16[4,160,256]{2,1,0:T(8,128)(2,1)} %joined.7.refs_5_.refs_1_), channel_id=1, source_target_pairs={{0,8},{1,9},{2,10},{3,11},{4,12},{5,13},{6,14},{7,15},{8,0},{9,1},... | collective-permute-start | bytes 983048 | tf_op jit(solution)/shard_map/ppermute | solution.py:706
  65.0 17.7 %collective-permute-start.4 = (bf16[4,160,256]{2,1,0:T(8,128)(2,1)}, bf16[4,160,256]{2,1,0:T(8,128)(2,1)}, u32[]{:S(2)}, u32[]{:S(2)}) collective-permute-start(bf16[4,160,256]{2,1,0:T(8,128)(2,1)} %joined.8.refs_7_), channel_id=1, source_target_pairs={{0,16},{1,17},{2,18},{3,19},{4,20},{5,21},{6,22},{7,23},{8,24},{9,... | collective-permute-start | bytes 983048 | tf_op jit(solution)/shard_map/ppermute | solution.py:706
  85.6 2.0 collective-permute-start.6
  171.2 18.9 %collective-permute-start.10 = (bf16[2816,512]{1,0:T(8,128)(2,1)}, bf16[2816,512]{1,0:T(8,128)(2,1)}, u32[]{:S(2)}, u32[]{:S(2)}) collective-permute-start(bf16[2816,512]{1,0:T(8,128)(2,1)} %get-tuple-element.119), channel_id=1, source_target_pairs={{0,1},{1,0},{2,3},{3,2},{4,5},{5,4},{6,7},{7,6},{8,9},{9,8},{10,11... | collective-permute-start | bytes 8650760 | tf_op jit(solution)/shard_map/ppermute | solution.py:706
  171.4 18.7 %collective-permute-start.12 = (bf16[512,2816]{1,0:T(8,128)(2,1)}, bf16[512,2816]{1,0:T(8,128)(2,1)}, u32[]{:S(2)}, u32[]{:S(2)}) collective-permute-start(bf16[512,2816]{1,0:T(8,128)(2,1)} %get-tuple-element.123), channel_id=1, source_target_pairs={{0,1},{1,0},{2,3},{3,2},{4,5},{5,4},{6,7},{7,6},{8,9},{9,8},{10,11... | collective-permute-start | bytes 8650760 | tf_op jit(solution)/shard_map/ppermute | solution.py:706
  171.8 18.3 %collective-permute-start.9 = (bf16[512,2816]{1,0:T(8,128)(2,1)}, bf16[512,2816]{1,0:T(8,128)(2,1)}, u32[]{:S(2)}, u32[]{:S(2)}) collective-permute-start(bf16[512,2816]{1,0:T(8,128)(2,1)} %get-tuple-element.117), channel_id=1, source_target_pairs={{0,1},{1,0},{2,3},{3,2},{4,5},{5,4},{6,7},{7,6},{8,9},{9,8},{10,11... | collective-permute-start | bytes 8650760 | tf_op jit(solution)/shard_map/ppermute | solution.py:706
  171.9 18.2 %collective-permute-start.11 = (bf16[512,1024]{1,0:T(8,128)(2,1)}, bf16[512,1024]{1,0:T(8,128)(2,1)}, u32[]{:S(2)}, u32[]{:S(2)}) collective-permute-start(bf16[512,1024]{1,0:T(8,128)(2,1)} %get-tuple-element.121), channel_id=1, source_target_pairs={{0,1},{1,0},{2,3},{3,2},{4,5},{5,4},{6,7},{7,6},{8,9},{9,8},{10,11... | collective-permute-start | bytes 3145736 | tf_op jit(solution)/shard_map/ppermute | solution.py:706
  183.6 3.6 collective-permute-start.7
  183.7 0.5 copy-start
  189.2 11.5 %collective-permute-start.8 = (bf16[4,160,256]{2,1,0:T(8,128)(2,1)}, bf16[4,160,256]{2,1,0:T(8,128)(2,1)}, u32[]{:S(2)}, u32[]{:S(2)}) collective-permute-start(bf16[4,160,256]{2,1,0:T(8,128)(2,1)} %begun.3.refs_26_.refs_1_), channel_id=1, source_target_pairs={{0,2},{1,3},{2,0},{3,1},{4,6},{5,7},{6,4},{7,5},{8,10},{9,11},{10,... | collective-permute-start | bytes 983048 | tf_op jit(solution)/shard_map/ppermute | solution.py:706
  203.3 15.9 %collective-permute-start.13 = (bf16[4,160,256]{2,1,0:T(8,128)(2,1)}, bf16[4,160,256]{2,1,0:T(8,128)(2,1)}, u32[]{:S(2)}, u32[]{:S(2)}) collective-permute-start(bf16[4,160,256]{2,1,0:T(8,128)(2,1)} %get-tuple-element.127.refs_14_.refs_1_), channel_id=1, source_target_pairs={{0,4},{1,5},{2,6},{3,7},{4,0},{5,1},{6,2},{7,3},{8,12},{9,13},{10,... | collective-permute-start | bytes 983048 | tf_op jit(solution)/shard_map/ppermute | solution.py:706
  204.3 63.9 %collective-permute-start.18 = (bf16[8,592,256]{2,1,0:T(8,128)(2,1)}, bf16[8,592,256]{2,1,0:T(8,128)(2,1)}, u32[]{:S(2)}, u32[]{:S(2)}) collective-permute-start(bf16[8,592,256]{2,1,0:T(8,128)(2,1)} %get-tuple-element.144), channel_id=1, source_target_pairs={{0,2},{1,3},{2,0},{3,1},{4,6},{5,7},{6,4},{7,5},{8,10},{9,11},{10,... | collective-permute-start | bytes 7274504 | tf_op jit(solution)/shard_map/ppermute | solution.py:706
  204.4 63.8 %collective-permute-start.19 = (bf16[8,592,256]{2,1,0:T(8,128)(2,1)}, bf16[8,592,256]{2,1,0:T(8,128)(2,1)}, u32[]{:S(2)}, u32[]{:S(2)}) collective-permute-start(bf16[8,592,256]{2,1,0:T(8,128)(2,1)} %get-tuple-element.146), channel_id=1, source_target_pairs={{0,4},{1,5},{2,6},{3,7},{4,0},{5,1},{6,2},{7,3},{8,12},{9,13},{10,... | collective-permute-start | bytes 7274504 | tf_op jit(solution)/shard_map/ppermute | solution.py:706
  217.9 60.8 %collective-permute-start.15 = (bf16[2,128,1024]{2,1,0:T(8,128)(2,1)}, bf16[2,128,1024]{2,1,0:T(8,128)(2,1)}, u32[]{:S(2)}, u32[]{:S(2)}) collective-permute-start(bf16[2,128,1024]{2,1,0:T(8,128)(2,1)} %get-tuple-element.139), channel_id=1, source_target_pairs={{1,0},{2,1},{3,2},{4,3},{5,4},{6,5},{7,6},{8,7},{9,8},{10,9},{11,1... | collective-permute-start | bytes 1572872 | tf_op jit(solution)/shard_map/ppermute | solution.py:968
  221.8 14.2 %collective-permute-start.14 = (bf16[4,160,256]{2,1,0:T(8,128)(2,1)}, bf16[4,160,256]{2,1,0:T(8,128)(2,1)}, u32[]{:S(2)}, u32[]{:S(2)}) collective-permute-start(bf16[4,160,256]{2,1,0:T(8,128)(2,1)} %joined.10.refs_9_.refs_1_), channel_id=1, source_target_pairs={{0,8},{1,9},{2,10},{3,11},{4,12},{5,13},{6,14},{7,15},{8,0},{9,1},... | collective-permute-start | bytes 983048 | tf_op jit(solution)/shard_map/ppermute | solution.py:706
  238.5 26.8 %collective-permute-start.16 = (bf16[4,160,256]{2,1,0:T(8,128)(2,1)}, bf16[4,160,256]{2,1,0:T(8,128)(2,1)}, u32[]{:S(2)}, u32[]{:S(2)}) collective-permute-start(bf16[4,160,256]{2,1,0:T(8,128)(2,1)} %joined.11.refs_10_), channel_id=1, source_target_pairs={{0,16},{1,17},{2,18},{3,19},{4,20},{5,21},{6,22},{7,23},{8,24},{9,... | collective-permute-start | bytes 983048 | tf_op jit(solution)/shard_map/ppermute | solution.py:706
  268.2 10.5 %collective-permute-start.17 = (bf16[4,160,256]{2,1,0:T(8,128)(2,1)}, bf16[4,160,256]{2,1,0:T(8,128)(2,1)}, u32[]{:S(2)}, u32[]{:S(2)}) collective-permute-start(bf16[4,160,256]{2,1,0:T(8,128)(2,1)} %get-tuple-element.141), channel_id=1, source_target_pairs={{0,1},{1,0},{2,3},{3,2},{4,5},{5,4},{6,7},{7,6},{8,9},{9,8},{10,11... | collective-permute-start | bytes 983048 | tf_op jit(solution)/shard_map/ppermute | solution.py:706
  274.7 29.4 %collective-permute-start.21 = (bf16[4,592,256]{2,1,0:T(8,128)(2,1)}, bf16[4,592,256]{2,1,0:T(8,128)(2,1)}, u32[]{:S(2)}, u32[]{:S(2)}) collective-permute-start(bf16[4,592,256]{2,1,0:T(8,128)(2,1)} %bitcast.129), channel_id=1, source_target_pairs={{0,4},{1,5},{2,6},{3,7},{4,0},{5,1},{6,2},{7,3},{8,12},{9,13},{10,... | collective-permute-start | bytes 3637256 | tf_op jit(solution)/shard_map/ppermute | solution.py:706
  275.2 29.9 %collective-permute-start.22 = (bf16[4,592,256]{2,1,0:T(8,128)(2,1)}, bf16[4,592,256]{2,1,0:T(8,128)(2,1)}, u32[]{:S(2)}, u32[]{:S(2)}) collective-permute-start(bf16[4,592,256]{2,1,0:T(8,128)(2,1)} %bitcast.128), channel_id=1, source_target_pairs={{0,2},{1,3},{2,0},{3,1},{4,6},{5,7},{6,4},{7,5},{8,10},{9,11},{10,... | collective-permute-start | bytes 3637256 | tf_op jit(solution)/shard_map/ppermute | solution.py:706
  290.4 25.8 %collective-permute-start.20 = (bf16[512,2560]{1,0:T(8,128)(2,1)}, bf16[512,2560]{1,0:T(8,128)(2,1)}, u32[]{:S(2)}, u32[]{:S(2)}) collective-permute-start(bf16[512,2560]{1,0:T(8,128)(2,1)} %get-tuple-element.152), channel_id=1, source_target_pairs={{0,1},{1,0},{2,3},{3,2},{4,5},{5,4},{6,7},{7,6},{8,9},{9,8},{10,11... | collective-permute-start | bytes 7864328 | tf_op jit(solution)/shard_map/ppermute | solution.py:706
  315.3 8.2 %collective-permute-start.24 = (bf16[512,1536]{1,0:T(8,128)(2,1)}, bf16[512,1536]{1,0:T(8,128)(2,1)}, u32[]{:S(2)}, u32[]{:S(2)}) collective-permute-start(bf16[512,1536]{1,0:T(8,128)(2,1)} %get-tuple-element.160), channel_id=1, source_target_pairs={{0,1},{1,0},{2,3},{3,2},{4,5},{5,4},{6,7},{7,6},{8,9},{9,8},{10,11... | collective-permute-start | bytes 4718600 | tf_op jit(solution)/shard_map/ppermute | solution.py:706
  315.3 29.4 %collective-permute-start.28 = (bf16[2,1184,256]{2,1,0:T(8,128)(2,1)}, bf16[2,1184,256]{2,1,0:T(8,128)(2,1)}, u32[]{:S(2)}, u32[]{:S(2)}) collective-permute-start(bf16[2,1184,256]{2,1,0:T(8,128)(2,1)} %bitcast.127), channel_id=1, source_target_pairs={{0,8},{1,9},{2,10},{3,11},{4,12},{5,13},{6,14},{7,15},{8,0},{9,1},... | collective-permute-start | bytes 3637256 | tf_op jit(solution)/shard_map/ppermute | solution.py:706
  320.7 24.3 %collective-permute-start.23 = (bf16[8,160,256]{2,1,0:T(8,128)(2,1)}, bf16[8,160,256]{2,1,0:T(8,128)(2,1)}, u32[]{:S(2)}, u32[]{:S(2)}) collective-permute-start(bf16[8,160,256]{2,1,0:T(8,128)(2,1)} %bitcast.130), channel_id=1, source_target_pairs={{0,2},{1,3},{2,0},{3,1},{4,6},{5,7},{6,4},{7,5},{8,10},{9,11},{10,... | collective-permute-start | bytes 1966088 | tf_op jit(solution)/shard_map/ppermute | solution.py:706
  322.5 22.1 %collective-permute-start.26 = (bf16[8,128,256]{2,1,0:T(8,128)(2,1)}, bf16[8,128,256]{2,1,0:T(8,128)(2,1)}, u32[]{:S(2)}, u32[]{:S(2)}) collective-permute-start(bf16[8,128,256]{2,1,0:T(8,128)(2,1)} %bitcast.132), channel_id=1, source_target_pairs={{0,4},{1,5},{2,6},{3,7},{4,0},{5,1},{6,2},{7,3},{8,12},{9,13},{10,... | collective-permute-start | bytes 1572872 | tf_op jit(solution)/shard_map/ppermute | solution.py:706
  327.2 17.8 %collective-permute-start.27 = (bf16[8,96,256]{2,1,0:T(8,128)(2,1)}, bf16[8,96,256]{2,1,0:T(8,128)(2,1)}, u32[]{:S(2)}, u32[]{:S(2)}) collective-permute-start(bf16[8,96,256]{2,1,0:T(8,128)(2,1)} %bitcast.139), channel_id=1, source_target_pairs={{0,4},{1,5},{2,6},{3,7},{4,0},{5,1},{6,2},{7,3},{8,12},{9,13},{10,... | collective-permute-start | bytes 1179656 | tf_op jit(solution)/shard_map/ppermute | solution.py:706
  328.4 16.3 %collective-permute-start.25 = (bf16[8,64,256]{2,1,0:T(8,128)(2,1)}, bf16[8,64,256]{2,1,0:T(8,128)(2,1)}, u32[]{:S(2)}, u32[]{:S(2)}) collective-permute-start(bf16[8,64,256]{2,1,0:T(8,128)(2,1)} %bitcast.140), channel_id=1, source_target_pairs={{0,2},{1,3},{2,0},{3,1},{4,6},{5,7},{6,4},{7,5},{8,10},{9,11},{10,... | collective-permute-start | bytes 786440 | tf_op jit(solution)/shard_map/ppermute | solution.py:706
  349.5 20.7 %collective-permute-start.29 = (bf16[4,224,256]{2,1,0:T(8,128)(2,1)}, bf16[4,224,256]{2,1,0:T(8,128)(2,1)}, u32[]{:S(2)}, u32[]{:S(2)}) collective-permute-start(bf16[4,224,256]{2,1,0:T(8,128)(2,1)} %bitcast.138), channel_id=1, source_target_pairs={{0,4},{1,5},{2,6},{3,7},{4,0},{5,1},{6,2},{7,3},{8,12},{9,13},{10,... | collective-permute-start | bytes 1376264 | tf_op jit(solution)/shard_map/ppermute | solution.py:706
  350.4 19.8 %collective-permute-start.30 = (bf16[4,224,256]{2,1,0:T(8,128)(2,1)}, bf16[4,224,256]{2,1,0:T(8,128)(2,1)}, u32[]{:S(2)}, u32[]{:S(2)}) collective-permute-start(bf16[4,224,256]{2,1,0:T(8,128)(2,1)} %bitcast.137), channel_id=1, source_target_pairs={{0,2},{1,3},{2,0},{3,1},{4,6},{5,7},{6,4},{7,5},{8,10},{9,11},{10,... | collective-permute-start | bytes 1376264 | tf_op jit(solution)/shard_map/ppermute | solution.py:706
  352.1 39.9 %collective-permute-start.34 = (bf16[1,1184,256]{2,1,0:T(8,128)(2,1)}, bf16[1,1184,256]{2,1,0:T(8,128)(2,1)}, u32[]{:S(2)}, u32[]{:S(2)}) collective-permute-start(bf16[1,1184,256]{2,1,0:T(8,128)(2,1)} %bitcast.131), channel_id=1, source_target_pairs={{0,16},{1,17},{2,18},{3,19},{4,20},{5,21},{6,22},{7,23},{8,24},{9,... | collective-permute-start | bytes 1818632 | tf_op jit(solution)/shard_map/ppermute | solution.py:706
  372.8 26.2 %collective-permute-start.31 = (bf16[1,448,256]{2,1,0:T(8,128)(2,1)}, bf16[1,448,256]{2,1,0:T(8,128)(2,1)}, u32[]{:S(2)}, u32[]{:S(2)}) collective-permute-start(bf16[1,448,256]{2,1,0:T(8,128)(2,1)} %bitcast.143), channel_id=1, source_target_pairs={{0,24},{1,25},{2,26},{3,27},{4,28},{5,29},{6,30},{7,31},{8,16},{9,... | collective-permute-start | bytes 688136 | tf_op jit(solution)/shard_map/ppermute | solution.py:845
  374.0 26.7 %collective-permute-start.32 = (bf16[1,448,256]{2,1,0:T(8,128)(2,1)}, bf16[1,448,256]{2,1,0:T(8,128)(2,1)}, u32[]{:S(2)}, u32[]{:S(2)}) collective-permute-start(bf16[1,448,256]{2,1,0:T(8,128)(2,1)} %bitcast.142), channel_id=1, source_target_pairs={{0,16},{1,17},{2,18},{3,19},{4,20},{5,21},{6,22},{7,23},{8,24},{9,... | collective-permute-start | bytes 688136 | tf_op jit(solution)/shard_map/ppermute | solution.py:845
  376.0 24.7 %collective-permute-start.33 = (bf16[1,448,256]{2,1,0:T(8,128)(2,1)}, bf16[1,448,256]{2,1,0:T(8,128)(2,1)}, u32[]{:S(2)}, u32[]{:S(2)}) collective-permute-start(bf16[1,448,256]{2,1,0:T(8,128)(2,1)} %bitcast.141), channel_id=1, source_target_pairs={{0,8},{1,9},{2,10},{3,11},{4,12},{5,13},{6,14},{7,15},{8,0},{9,1},... | collective-permute-start | bytes 688136 | tf_op jit(solution)/shard_map/ppermute | solution.py:845
  403.0 2.1 collective-permute-start.35
